TPU v7x, 32 devices: a whole 2x2x4 slice. The times are simulated.
32 devices in a mesh: dp: 8 (over z, y), mp: 4 (over x, core).
Axes of the slice: x: 2, y: 2, z: 4, core: 2. Of those that a mesh axis runs over, the one named last changes fastest.
Arguments:
- tokens: bfloat16 [16384, 1024], P('dp'), may hold values from -96 to 96
- doc_ids: int32 [16384], P('dp'), may hold values from 0 to 255, as said below
- ln_gain: float32 [1024], replicated, may hold values from 0.1 to 1.9
- w_query: bfloat16 [1024, 1024], P(None, 'mp'), may hold values from -16 to 16
- w_key: bfloat16 [1024, 1024], P(None, 'mp'), may hold values from -0.5 to 0.5
- w_value: bfloat16 [1024, 1024], P(None, 'mp'), may hold values from -0.1875 to 0.1875
- w_out: bfloat16 [1024, 1024], P('mp'), may hold values from -0.1875 to 0.1875
- centroids: float32 [8192, 1024], P('dp', 'mp'), may hold values from -6 to 6
- cluster_mass: float32 [8192], P('dp'), may hold values from 0.5 to 4
- assigned: int32 [256], P('dp'), may hold values from 0 to 8191, as said below
Outputs:
- doc_vectors: float32 [256, 1024], P('dp', 'mp')
- new_centroids: float32 [8192, 1024], P('dp', 'mp')
Inputs may be any that keep to these rules, and one draw needn't show every extreme that they name: `doc_ids`: never falls along the positions. The documents that begin in row r (positions r * 2048 onward) have the ids r * 32 upward without gaps, from 24 to 32 of them, and some row has 32; ids of slots that no document takes never occur. A row begins with its own first document or with the rest of the last document begun in the row before, and row 0 begins with document 0; every document lies within the row where it begins and the next one. `assigned`: centroid c belongs to dp index c // 1024. Among the 32 slots of one row at most 5 name centroids of one dp index; in every row exactly 5 slots that hold documents name centroids of one dp index common to all rows.
All inputs are finite; a program needn't handle non-finite values.
Results may differ from a plain program's by a relative error of at most 0.0024.
Values sent between devices are 32-bit elements; how exact they have to be, the bound alone decides.
No kernel may reach another device: no remote copies, remote signals or barrier semaphores. Data moves between devices by JAX's collectives and lax.ppermute only.
A program may use at most 128 MiB of HBM per device.

v0:
```python
import math

import jax
import jax.numpy as jnp
from jax import lax
from jax.sharding import PartitionSpec as P

D = 1024
HEAD_DIM = 64


def shifted(x, axis, by):
    devices = lax.axis_size(axis)
    pairs = [(i, i + by) for i in range(devices) if 0 <= i + by < devices]
    return lax.ppermute(x, axis, pairs)


def layer_norm(tokens, ln_gain):
    widened = tokens.astype(jnp.float32)
    average = jnp.mean(widened, axis=-1, keepdims=True)
    centered = widened - average
    variance = jnp.mean(centered * centered, axis=-1, keepdims=True)
    return (centered * lax.rsqrt(variance + 1e-05) * ln_gain).astype(jnp.bfloat16)


def attend_block(queries, keys_all, values_all, query_ids, row_ids):
    scores = jnp.einsum("qhd,khd->hqk", queries, keys_all, preferred_element_type=jnp.float32) * (
        1.0 / math.sqrt(HEAD_DIM)
    )
    same_doc = query_ids[:, None] == row_ids[None, :]
    scores = jnp.where(same_doc[None], scores, -1e30)
    top_score = jnp.max(scores, axis=-1, keepdims=True)
    raised = jnp.exp(scores - top_score)
    weights = (raised / jnp.sum(raised, axis=-1, keepdims=True)).astype(jnp.bfloat16)
    return jnp.einsum(
        "hqk,khd->qhd", weights, values_all, preferred_element_type=jnp.float32
    ).astype(jnp.bfloat16)


def self_attention(normed, w_query, w_key, w_value, row_ids):
    length = normed.shape[0]
    width = w_query.shape[1]
    head_count = width // HEAD_DIM

    def project(weight):
        return (
            jnp.dot(normed, weight, preferred_element_type=jnp.float32)
            .astype(jnp.bfloat16)
            .reshape(length, head_count, HEAD_DIM)
        )

    queries = project(w_query)
    keys_all = project(w_key)
    values_all = project(w_value)
    block_rows = min(512, length)
    query_blocks = queries.reshape(length // block_rows, block_rows, head_count, HEAD_DIM)
    id_blocks = row_ids.reshape(length // block_rows, block_rows)
    context = lax.map(
        lambda pair: attend_block(pair[0], keys_all, values_all, pair[1], row_ids),
        (query_blocks, id_blocks),
    )
    return context.reshape(length, width)


def shards(
    tokens, doc_ids, ln_gain, w_query, w_key, w_value, w_out, centroids, cluster_mass, assigned
):
    length = tokens.shape[0]
    slot_count = assigned.shape[0]
    local_width = w_out.shape[0]
    cent_count = centroids.shape[0]
    row_index = lax.axis_index("dp")
    column_start = lax.axis_index("mp") * local_width
    highest = lax.Precision.HIGHEST
    dp_count = lax.axis_size("dp")
    capacity = max(2, (slot_count + dp_count - 2) // (dp_count - 1))
    normed = layer_norm(tokens, ln_gain)
    context = self_attention(normed, w_query, w_key, w_value, doc_ids)
    local_slot = doc_ids - row_index * slot_count
    targets = jnp.where(local_slot < 0, slot_count, local_slot)
    member = jnp.arange(slot_count + 1, dtype=jnp.int32)[:, None] == targets[None, :]
    counts = jnp.sum(member.astype(jnp.float32), axis=1)
    own_columns = lax.dynamic_slice_in_dim(tokens, column_start, local_width, 1)
    partial_out = jnp.dot(context, w_out, preferred_element_type=jnp.float32)
    mixed = own_columns.astype(jnp.float32) + lax.psum_scatter(
        partial_out, "mp", scatter_dimension=1, tiled=True
    )
    pooled = jnp.dot(member.astype(jnp.float32), mixed, precision=highest)
    received_sum, received_count = shifted((pooled[slot_count:], counts[slot_count:]), "dp", -1)
    last_pick = (jnp.arange(slot_count, dtype=jnp.int32) == local_slot[length - 1]).astype(
        jnp.float32
    )
    doc_sums = pooled[:slot_count] + last_pick[:, None] * received_sum
    doc_counts = counts[:slot_count] + last_pick * received_count[0]
    averages = doc_sums / jnp.maximum(doc_counts, 1.0)[:, None]
    squares = lax.psum(jnp.sum(averages * averages, axis=1), "mp")
    doc_vectors = averages * lax.rsqrt(squares / D + 1e-06)[:, None]
    is_used = doc_counts > 0
    gathered, all_assigned, all_used = (
        lax.all_gather(doc_vectors, "dp", axis=0, tiled=True),
        lax.all_gather(assigned.astype(jnp.float32), "dp", axis=0, tiled=True),
        lax.all_gather(is_used.astype(jnp.float32), "dp", axis=0, tiled=True),
    )
    offset = all_assigned - (row_index * cent_count).astype(jnp.float32)
    is_mine = (all_used > 0) & (offset >= 0) & (offset < cent_count)
    kept_total = dp_count * capacity
    picked = jnp.nonzero(is_mine, size=kept_total, fill_value=0)[0].astype(jnp.int32)
    kept_count = jnp.sum(is_mine.astype(jnp.int32))
    valid_slot = jnp.arange(kept_total, dtype=jnp.int32) < kept_count
    arriving = jnp.take(gathered, picked, axis=0)
    target = jnp.where(valid_slot, jnp.take(offset, picked, axis=0), -1.0)
    hits_table = (
        jnp.arange(cent_count, dtype=jnp.int32).astype(jnp.float32)[:, None] == target[None, :]
    ).astype(jnp.float32)
    gained = jnp.dot(hits_table, arriving, precision=highest)
    members = jnp.sum(hits_table, axis=1)
    blended = cluster_mass[:, None] * centroids + gained
    norm_terms = lax.psum(jnp.sum(blended * blended, axis=1), "mp")
    scaled = blended * lax.rsqrt(norm_terms / D + 1e-06)[:, None]
    updated = jnp.where((members > 0)[:, None], scaled, centroids)
    return (doc_vectors, updated)


def solution(mesh):
    placed = (
        P("dp", None),
        P("dp"),
        P(),
        P(None, "mp"),
        P(None, "mp"),
        P(None, "mp"),
        P("mp", None),
        P("dp", "mp"),
        P("dp"),
        P("dp"),
    )
    return jax.shard_map(
        shards,
        mesh=mesh,
        in_specs=placed,
        out_specs=(P("dp", "mp"), P("dp", "mp")),
        check_vma=False,
    )
```

profile of v0, /device:TPU:0, one launch (start us, length us, event | category | flops | bytes accessed | tf_op | source)
XLA Modules:
  0.0 254.7 jit_solution(594694632054875408)
XLA Ops:
  7.3 3.0 %convert_reduce_fusion = f32[2048]{0:T(1024)S(1)} fusion(bf16[2048,1024]{1,0:T(8,128)(2,1)} %param.12), kind=kLoop, calls=%fused_computation.28 | loop fusion | flops 4192256 | bytes 4202496 | tf_op jit(solution)/shard_map/reduce_sum | solution.py:20
  10.2 3.0 %fusion.30 = f32[2048]{0:T(1024)S(1)} fusion(bf16[2048,1024]{1,0:T(8,128)(2,1)} %param.12, f32[2048]{0:T(1024)S(1)} %broadcast_multiply_fusion.1), kind=kLoop, calls=%fused_computation.31 | loop fusion | flops 8386560 | bytes 4210688 | tf_op jit(solution)/shard_map/reduce_sum | solution.py:22
  13.3 1.4 fusion.32
  14.7 1.9 copy-done.2
  16.6 2.3 convolution_convert_fusion.2
  18.9 3.3 %reshape.271 = bf16[4,512,4,64]{3,2,1,0:T(4,128)(2,1)S(1)} reshape(bf16[2048,256]{1,0:T(8,128)(2,1)} %convolution_convert_fusion.2) | data formatting | bytes 2097152 | tf_op jit(solution)/shard_map/reshape;reshape | solution.py:56
  22.2 2.3 copy.25
  24.5 4.7 %convolution_convert_fusion.1 = bf16[2048,256]{0,1:T(8,128)(2,1)} fusion(bf16[2048,1024]{1,0:T(8,128)(2,1)} %copy-done.2, bf16[1024,256]{1,0:T(8,128)(2,1)S(1)} %copy-done.11), kind=kOutput, calls=%fused_computation.35 | convolution fusion | flops 1074266112 | bytes 5767168 | tf_op jit(solution)/shard_map/dot_general | solution.py:47
  29.2 2.3 convolution_convert_fusion
  31.5 79.7 %while.10 = (s32[]{:T(128)}, bf16[4,512,4,64]{1,3,2,0:T(8,128)(2,1)S(1)}, s32[4,512]{1,0:T(4,128)S(1)}, s32[2048]{0:T(1024)S(1)}, bf16[4,512,4,64]{1,3,2,0:T(8,1...) while((s32[]{:T(128)}, bf16[4,512,4,64]{1,3,2,0:T(8,128)(2,1)S(1)}, ...), condition=%wide.region_5.6_spmd, body=%wide.region_2.5_spmd.sunk | while | flops 1100089344 | bytes 38304348 | solution.py:58
  31.7 0.7 broadcast_compare_fusion.3
  32.4 10.5 %fusion.84 = (f32[4,512]{1,0:T(4,128)S(1)}, f32[4,512,2048]{2,1,0:T(8,128)}) fusion(pred[512,2048]{1,0:T(8,128)(4,1)S(1)} %broadcast_compare_fusion.3, bf16[2048,4,64]{0,2,1:T(8,128)(2,1)} %get-tuple-element.165, bf16[4,512,4,64]{1,3,2,0:T(8,128)(2,1)} %get-tuple-element.164, s32[]{:T(128)} %get-tuple-element.152), kind=kOutput, calls=%fused_computation.102.clone.1 | convolution fusion | flops 553650176 | bytes 19145216 | tf_op jit(solution)/shard_map/while/body/eval_jaxpr/sub | solution.py:33
  42.8 8.7 %fusion.85 = bf16[4,512,4,64]{1,3,2,0:T(8,128)(2,1)S(1)} fusion(bf16[4,512,4,64]{1,3,2,0:T(8,128)(2,1)S(1)} %get-tuple-element.153, s32[]{:T(128)} %get-tuple-element.152, bf16[2048,4,64]{0,2,1:T(8,128)(2,1)} %get-tuple-element.166, f32[4,512,2048]{2,1,0:T(8,128)} %get-tuple-element.142, f32[4,512]{1,0:T(4,128)S(1)} %get-tuple-element.143), kind=kOutput, calls=%fused_computation.16.clone.1 | convolution fusion | flops 545390592 | bytes 18096132 | tf_op jit(solution)/shard_map/while/body/eval_jaxpr/hqk,khd->qhd/dot_general | solution.py:35
  51.6 0.7 broadcast_compare_fusion.3
  52.2 10.5 %fusion.84 = (f32[4,512]{1,0:T(4,128)S(1)}, f32[4,512,2048]{2,1,0:T(8,128)}) fusion(pred[512,2048]{1,0:T(8,128)(4,1)S(1)} %broadcast_compare_fusion.3, bf16[2048,4,64]{0,2,1:T(8,128)(2,1)} %get-tuple-element.165, bf16[4,512,4,64]{1,3,2,0:T(8,128)(2,1)} %get-tuple-element.164, s32[]{:T(128)} %get-tuple-element.152), kind=kOutput, calls=%fused_computation.102.clone.1 | convolution fusion | flops 553650176 | bytes 19145216 | tf_op jit(solution)/shard_map/while/body/eval_jaxpr/sub | solution.py:33
  62.7 8.7 %fusion.85 = bf16[4,512,4,64]{1,3,2,0:T(8,128)(2,1)S(1)} fusion(bf16[4,512,4,64]{1,3,2,0:T(8,128)(2,1)S(1)} %get-tuple-element.153, s32[]{:T(128)} %get-tuple-element.152, bf16[2048,4,64]{0,2,1:T(8,128)(2,1)} %get-tuple-element.166, f32[4,512,2048]{2,1,0:T(8,128)} %get-tuple-element.142, f32[4,512]{1,0:T(4,128)S(1)} %get-tuple-element.143), kind=kOutput, calls=%fused_computation.16.clone.1 | convolution fusion | flops 545390592 | bytes 18096132 | tf_op jit(solution)/shard_map/while/body/eval_jaxpr/hqk,khd->qhd/dot_general | solution.py:35
  71.5 0.7 broadcast_compare_fusion.3
  72.1 10.5 %fusion.84 = (f32[4,512]{1,0:T(4,128)S(1)}, f32[4,512,2048]{2,1,0:T(8,128)}) fusion(pred[512,2048]{1,0:T(8,128)(4,1)S(1)} %broadcast_compare_fusion.3, bf16[2048,4,64]{0,2,1:T(8,128)(2,1)} %get-tuple-element.165, bf16[4,512,4,64]{1,3,2,0:T(8,128)(2,1)} %get-tuple-element.164, s32[]{:T(128)} %get-tuple-element.152), kind=kOutput, calls=%fused_computation.102.clone.1 | convolution fusion | flops 553650176 | bytes 19145216 | tf_op jit(solution)/shard_map/while/body/eval_jaxpr/sub | solution.py:33
  82.6 8.7 %fusion.85 = bf16[4,512,4,64]{1,3,2,0:T(8,128)(2,1)S(1)} fusion(bf16[4,512,4,64]{1,3,2,0:T(8,128)(2,1)S(1)} %get-tuple-element.153, s32[]{:T(128)} %get-tuple-element.152, bf16[2048,4,64]{0,2,1:T(8,128)(2,1)} %get-tuple-element.166, f32[4,512,2048]{2,1,0:T(8,128)} %get-tuple-element.142, f32[4,512]{1,0:T(4,128)S(1)} %get-tuple-element.143), kind=kOutput, calls=%fused_computation.16.clone.1 | convolution fusion | flops 545390592 | bytes 18096132 | tf_op jit(solution)/shard_map/while/body/eval_jaxpr/hqk,khd->qhd/dot_general | solution.py:35
  91.3 0.7 broadcast_compare_fusion.3
  92.0 10.5 %fusion.84 = (f32[4,512]{1,0:T(4,128)S(1)}, f32[4,512,2048]{2,1,0:T(8,128)}) fusion(pred[512,2048]{1,0:T(8,128)(4,1)S(1)} %broadcast_compare_fusion.3, bf16[2048,4,64]{0,2,1:T(8,128)(2,1)} %get-tuple-element.165, bf16[4,512,4,64]{1,3,2,0:T(8,128)(2,1)} %get-tuple-element.164, s32[]{:T(128)} %get-tuple-element.152), kind=kOutput, calls=%fused_computation.102.clone.1 | convolution fusion | flops 553650176 | bytes 19145216 | tf_op jit(solution)/shard_map/while/body/eval_jaxpr/sub | solution.py:33
  102.5 8.7 %fusion.85 = bf16[4,512,4,64]{1,3,2,0:T(8,128)(2,1)S(1)} fusion(bf16[4,512,4,64]{1,3,2,0:T(8,128)(2,1)S(1)} %get-tuple-element.153, s32[]{:T(128)} %get-tuple-element.152, bf16[2048,4,64]{0,2,1:T(8,128)(2,1)} %get-tuple-element.166, f32[4,512,2048]{2,1,0:T(8,128)} %get-tuple-element.142, f32[4,512]{1,0:T(4,128)S(1)} %get-tuple-element.143), kind=kOutput, calls=%fused_computation.16.clone.1 | convolution fusion | flops 545390592 | bytes 18096132 | tf_op jit(solution)/shard_map/while/body/eval_jaxpr/hqk,khd->qhd/dot_general | solution.py:35
  111.2 0.8 copy.26
  112.4 4.5 %fusion.64 = f32[2048,1024]{1,0:T(8,128)} fusion(bf16[2048,256]{0,1:T(8,128)(2,1)S(1)} %bitcast.57, bf16[256,1024]{1,0:T(8,128)(2,1)S(1)} %copy-done), kind=kOutput, calls=%fused_computation.103 | convolution fusion | flops 1073741824 | bytes 9961472 | tf_op jit(solution)/shard_map/dot_general | solution.py:84
  117.1 0.6 slice.26
  117.6 1.3 collective-permute-start.1
  118.9 0.6 slice.34
  119.8 0.6 dynamic-slice
  121.1 0.6 compare_convert_fusion.2
  121.8 2.3 collective-permute-done.1
  124.1 1.3 fusion.50
  125.4 22.4 %all-reduce.2 = (f32[256]{0:T(256)S(1)}, f32[256]{0:T(256)S(1)}) all-reduce(f32[256]{0:T(256)S(1)} %convert_dynamic-update-slice_fusion, f32[256]{0:T(256)S(1)} %get-tuple-element.89), channel_id=1, replica_groups=mesh['dp'=8,'mp'=4] {'dp'}, use_global_device_ids=true, to_apply=%add.1 | all-reduce | flops 512 | bytes 4096
  147.9 0.6 fusion.57
  149.2 2.3 scatter_custom_fusion
  151.6 0.8 fusion.46
  152.4 0.8 gather_fusion
  153.2 0.7 compare_select_fusion.7
  154.0 37.5 %reduce-scatter.2.cloned.1.call-done = f32[2048,256]{1,0:T(8,128)} async-done(((f32[2048,1024]{1,0:T(8,128)}), f32[2048,256]{1,0:T(8,128)}) %reduce-scatter.2.cloned.1.call-update) | async-done | bytes 2097168 | tf_op jit(solution)/shard_map/reduce_scatter | solution.py:85
  191.5 2.9 %fusion.33 = f32[33,256]{1,0:T(8,128)S(1)} fusion(f32[2048,256]{1,0:T(8,128)} %reduce-scatter.2.cloned.1.call-done, bf16[2048,1024]{1,0:T(8,128)(2,1)} %param.12, s32[]{:T(128)S(6)} %select_n.121, s32[2048]{0:T(1024)S(1)} %get-tuple-element.91), kind=kOutput, calls=%fused_computation.37 | convolution fusion | flops 208734208 | bytes 3187716 | tf_op jit(solution)/shard_map/dot_general | solution.py:88
  194.4 1.3 collective-permute-start
  195.7 4.2 %collective-permute-done = f32[1,256]{1,0:T(1,128)S(1)} collective-permute-done((f32[1,256]{1,0:T(1,128)S(1)}, f32[1,256]{1,0:T(1,128)S(1)}, u32[]{:S(2)}, u32[]{:S(2)}) %collective-permute-start) | collective-permute-done | bytes 1056 | tf_op jit(solution)/shard_map/ppermute | solution.py:15
  200.0 5.8 %psum.14 = f32[32]{0:T(128)S(1)} all-reduce(f32[32]{0:T(128)S(1)} %multiply_reduce_fusion.1), channel_id=1, replica_groups=mesh['dp'=8,'mp'=4] {'mp'}, use_global_device_ids=true, to_apply=%region_9.10 | all-reduce | flops 32 | bytes 256 | tf_op jit(solution)/shard_map/psum | solution.py:96
  205.9 31.1 %all_gather.11 = f32[256,256]{1,0:T(8,128)S(1)} all-gather(f32[32,256]{1,0:T(8,128)S(1)} %broadcast_multiply_fusion), channel_id=1, replica_groups=mesh['dp'=8,'mp'=4] {'dp'}, dimensions={0}, use_global_device_ids=true | all-gather | bytes 294912 | tf_op jit(solution)/shard_map/all_gather | solution.py:100
  237.0 0.6 gather_fusion.1
  237.6 1.8 multiply_reduce_fusion
  239.4 5.7 %psum.15 = f32[1024]{0:T(1024)S(1)} all-reduce(f32[1024]{0:T(1024)S(1)} %get-tuple-element.95), channel_id=1, replica_groups=mesh['dp'=8,'mp'=4] {'mp'}, use_global_device_ids=true, to_apply=%region_17.18 | all-reduce | flops 1024 | bytes 8192 | tf_op jit(solution)/shard_map/psum | solution.py:118
  245.1 1.4 multiply_select_fusion.4
  246.5 1.3 copy.30
  (66 shorter events, 2.2 us)
Async XLA Ops:
  7.2 105.1 %copy-start = (bf16[256,1024]{1,0:T(8,128)(2,1)S(1)}, bf16[256,1024]{1,0:T(8,128)(2,1)}, u32[]{:S(2)}) copy-start(bf16[256,1024]{1,0:T(8,128)(2,1)} %param.18) | copy-start | bytes 1572868
  7.2 6.1 %copy-start.8 = (f32[1024]{0:T(1024)S(1)}, f32[1024]{0:T(1024)}, u32[]{:S(2)}) copy-start(f32[1024]{0:T(1024)} %param.14) | copy-start | bytes 12292
  7.2 184.3 %reduce-scatter.2.cloned.1.call-start = ((), (), s32[]{:S(2)}) async-start(), calls=%async_computation.1 | async-start | bytes 10485760 | tf_op jit(solution)/shard_map/reduce_scatter | solution.py:85
  7.2 6.0 %copy-start.1 = (bf16[2048,1024]{1,0:T(8,128)(2,1)S(1)}, bf16[2048,1024]{1,0:T(8,128)(2,1)}, u32[]{:S(2)}) copy-start(bf16[2048,1024]{1,0:T(8,128)(2,1)} %param.12) | copy-start | bytes 12582916
  7.3 9.3 %copy-start.10 = (bf16[1024,256]{1,0:T(8,128)(2,1)S(1)}, bf16[1024,256]{1,0:T(8,128)(2,1)}, u32[]{:S(2)}) copy-start(bf16[1024,256]{1,0:T(8,128)(2,1)} %param.15) | copy-start | bytes 1572868
  14.7 1.9 copy-start.2
  16.6 7.9 %copy-start.11 = (bf16[1024,256]{1,0:T(8,128)(2,1)S(1)}, bf16[1024,256]{1,0:T(8,128)(2,1)}, u32[]{:S(2)}) copy-start(bf16[1024,256]{1,0:T(8,128)(2,1)} %param.16) | copy-start | bytes 1572868
  24.5 4.7 %copy-start.3 = (bf16[2048,1024]{1,0:T(8,128)(2,1)S(1)}, bf16[2048,1024]{1,0:T(8,128)(2,1)}, u32[]{:S(2)}) copy-start(bf16[2048,1024]{1,0:T(8,128)(2,1)} %copy-done.2) | copy-start | bytes 12582916
  24.5 4.7 %copy-start.12 = (bf16[1024,256]{1,0:T(8,128)(2,1)S(1)}, bf16[1024,256]{1,0:T(8,128)(2,1)}, u32[]{:S(2)}) copy-start(bf16[1024,256]{1,0:T(8,128)(2,1)} %param.17) | copy-start | bytes 1572868
  29.2 2.3 copy-start.6
  29.2 2.3 copy-start.5
  112.3 7.2 %copy-start.4 = (f32[1024,256]{1,0:T(8,128)S(1)}, f32[1024,256]{1,0:T(8,128)}, u32[]{:S(2)}) copy-start(f32[1024,256]{1,0:T(8,128)} %param.19) | copy-start | bytes 3145732
  112.3 7.5 %copy-start.14 = (u32[32]{0:T(128)S(1)}, u32[32]{0:T(128)}, u32[]{:S(2)}) copy-start(u32[32]{0:T(128)} %constant.136) | copy-start | bytes 388
  112.3 9.3 %copy-start.13 = (s32[32]{0:T(128)S(1)}, s32[32]{0:T(128)}, u32[]{:S(2)}) copy-start(s32[32]{0:T(128)} %param.21) | copy-start | bytes 388
  116.9 120.7 %copy-start.9 = (f32[1024]{0:T(1024)S(1)}, f32[1024]{0:T(1024)}, u32[]{:S(2)}) copy-start(f32[1024]{0:T(1024)} %param.20) | copy-start | bytes 12292
  117.6 6.5 %collective-permute-start.1 = (f32[1]{0:T(128)}, f32[1]{0:T(128)}, u32[]{:S(2)}, u32[]{:S(2)}) collective-permute-start(f32[1]{0:T(128)} %slice.26), channel_id=1, source_target_pairs={{4,0},{8,4},{12,8},{16,12},{20,16},{24,20},{28,24},{5,1},{9,5},{13... | collective-permute-start | bytes 20 | tf_op jit(solution)/shard_map/ppermute | solution.py:15
  194.4 5.5 %collective-permute-start = (f32[1,256]{1,0:T(1,128)S(1)}, f32[1,256]{1,0:T(1,128)S(1)}, u32[]{:S(2)}, u32[]{:S(2)}) collective-permute-start(f32[1,256]{1,0:T(1,128)S(1)} %slice.35), channel_id=1, source_target_pairs={{4,0},{8,4},{12,8},{16,12},{20,16},{24,20},{28,24},{5,1},{9,5},{13... | collective-permute-start | bytes 3080 | tf_op jit(solution)/shard_map/ppermute | solution.py:15
  205.9 42.0 %copy-start.7 = (f32[32,256]{1,0:T(8,128)}, f32[32,256]{1,0:T(8,128)S(1)}, u32[]{:S(2)}) copy-start(f32[32,256]{1,0:T(8,128)S(1)} %broadcast_multiply_fusion) | copy-start | bytes 98308
Sparse Core Ops, SparseCore 0:
  117.0 74.3 reduce-scatter.1
where the time goes:
time: 255 us
  matrix products  95.1 us (37%)
  blocking collectives  65.1 us (26%)
  waiting for transfers between devices  44 us (17%)
  other arithmetic  18.8 us (7%)
  between operations  15 us (6%)
  local copies, waits for them, and re-layouts  13.8 us (5%)
  starting transfers between devices  2.61 us (1%)
    sub x4, matrix products, attend_block(): raised = jnp.exp(scores - top_score)  41.9 us
    reduce_scatter x1, waiting for transfers between devices, shards(): lax.psum_scatter(partial_out, 'mp', scatter_dimension=1, tiled=True)  37.5 us
    dot_general x4, matrix products, attend_block(): jnp.einsum('hqk,khd->qhd', weights, values_all, preferred_element_type=jn...  34.9 us
    all_gather x1, blocking collectives, shards(): lax.all_gather(doc_vectors, 'dp', axis=0, tiled=True)  31.1 us
    unnamed x1, blocking collectives  22.4 us
    dot_general x3, matrix products, project(): jnp.dot(normed, weight, preferred_element_type=jnp.float32)  9.21 us
    ppermute x2, waiting for transfers between devices, shifted(): return lax.ppermute(x, axis, pairs)  6.48 us
    psum x1, blocking collectives, shards(): squares = lax.psum(jnp.sum(averages * averages, axis=1), 'mp')  5.76 us
  transfers between devices with their start and end apart: 3, of which 3 were waited for; matrix products, arithmetic and copies ran while one was open for 4% of the time, Pallas kernels for 0%

commit v1 on v0

v1 whole, which is shorter than its diff:
```python
import functools
import math

import jax
import jax.numpy as jnp
from jax import lax
from jax.experimental import pallas as pl
from jax.experimental.pallas import tpu as pltpu
from jax.sharding import PartitionSpec as P

D = 1024
HEAD_DIM = 64
QB = 128
GROUP = 4
SLOTS = 48
LANES = 128
BF = jnp.bfloat16
F32 = jnp.float32

NN = (((1,), (0,)), ((), ()))
NT = (((1,), (1,)), ((), ()))
TN = (((0,), (0,)), ((), ()))


def dot(a, b, dims=NN, precision=None):
    return lax.dot_general(a, b, dims, preferred_element_type=F32, precision=precision)


def iota(shape, dim):
    return lax.broadcasted_iota(jnp.int32, shape, dim)


def thirds(x):
    first = x.astype(BF)
    rest = x - first.astype(F32)
    second = rest.astype(BF)
    third = (rest - second.astype(F32)).astype(BF)
    return first, second, third


def pick_rows(one_hot, x, dims=NN):
    first, second, third = thirds(x)
    return dot(one_hot, first, dims) + (dot(one_hot, second, dims) + dot(one_hot, third, dims))


def round_up(n, by):
    return (n + by - 1) // by * by


def row_kernel(
    sizes, ids_hbm, assigned_hbm, gain_hbm, x_hbm, wq_hbm, wk_hbm, wv_hbm, wo_hbm, out_ref,
    ids_ref, ids_sm, assigned_sm, gain_ref, x_ref, w_ref, wo_ref, normed_ref, q_ref, k_ref, v_ref,
    slot_ref, slot_rows_ref, windows_sm, place_ref, meta_ref, acc_ref, part_ref, small_sems, x_sems, w_sems,
):
    length, tile, slots, capacity, block_rows, dp, mp, width, cents = sizes
    tiles = length // tile
    blocks_all = length // QB
    rows = dp * block_rows
    row = lax.axis_index("dp")
    column = lax.axis_index("mp")
    pairs = width // LANES

    small_copies = [
        pltpu.make_async_copy(ids_hbm, ids_ref, small_sems.at[0]),
        pltpu.make_async_copy(ids_hbm, ids_sm, small_sems.at[1]),
        pltpu.make_async_copy(assigned_hbm, assigned_sm, small_sems.at[2]),
        pltpu.make_async_copy(gain_hbm, gain_ref, small_sems.at[3]),
    ]
    x_copies = [
        pltpu.make_async_copy(x_hbm.at[pl.ds(i * tile, tile), :], x_ref.at[pl.ds(i * tile, tile), :], x_sems.at[i])
        for i in range(tiles)
    ]
    w_copies = [
        pltpu.make_async_copy(w_hbm, w_ref.at[:, pl.ds(i * width, width)], w_sems.at[i])
        for i, w_hbm in enumerate((wq_hbm, wk_hbm, wv_hbm))
    ] + [pltpu.make_async_copy(wo_hbm, wo_ref, w_sems.at[3])]
    for copy in small_copies + x_copies[:1] + w_copies[:3] + x_copies[1:] + w_copies[3:]:
        copy.start()
    for copy in small_copies:
        copy.wait()

    ids = ids_ref[...]
    local = ids - row * slots
    slot_rows = jnp.where(local < 0, slots, local).astype(F32)
    slot_rows_ref[...] = slot_rows
    on_diagonal = iota((LANES, LANES), 0) == iota((LANES, LANES), 1)
    ones = jnp.ones((LANES, LANES), BF)
    counts = jnp.zeros((8, LANES), F32)
    for block in range(blocks_all):
        slot = slot_rows[block:block + 1, :]
        diagonal = jnp.where(on_diagonal, slot, 0.0).astype(BF)
        slot_ref[block * LANES:(block + 1) * LANES, :] = dot(diagonal, ones)
        member = (iota((LANES, LANES), 0).astype(F32) == slot).astype(F32).astype(BF)
        counts += dot(ones[:8], member, NT)

    for block in range(blocks_all):
        first = ids_sm[block, 0]
        last = ids_sm[block, QB - 1]
        begin = jnp.sum((ids < first).astype(F32)).astype(jnp.int32)
        end = jnp.sum((ids <= last).astype(F32)).astype(jnp.int32)
        windows_sm[0, block] = (begin // 16) * 16
        windows_sm[1, block] = end

    lane = iota((1, LANES), 1)
    named = jnp.full((1, LANES), -1, jnp.int32)
    owner = jnp.full((1, LANES), -1, jnp.int32)
    for j in range(slots):
        name = assigned_sm[0, j]
        named = jnp.where(lane == j, name, named)
        owner = jnp.where(lane == j, name // cents, owner)
    wide = jnp.broadcast_to(owner.astype(F32), (LANES, LANES))
    earlier = (wide.T == wide) & (iota((LANES, LANES), 0) < iota((LANES, LANES), 1))
    rank = jnp.sum(earlier.astype(F32), axis=0, keepdims=True)
    goes_to = jnp.where(lane < slots, owner.astype(F32) * block_rows + rank, -1.0)
    row_of = iota((rows, LANES), 0)
    place = (row_of.astype(F32) == goes_to) | (
        (row_of % block_rows == capacity) & (iota((rows, LANES), 1) == slots)
    )
    place_ref[...] = place.astype(F32).astype(BF)
    last_slot = ids_sm[blocks_all - 1, QB - 1] - row * slots
    speaks = (column == 0).astype(F32)
    meta_ref[0:1, :LANES] = goes_to * speaks
    meta_ref[0:1, LANES:] = counts[:1] * speaks
    meta_ref[1:2, :LANES] = named.astype(F32) * speaks
    meta_ref[1:2, LANES:] = (lane == last_slot).astype(F32) * speaks
    part_ref[...] = jnp.zeros_like(part_ref)
    acc_ref[...] = jnp.zeros_like(acc_ref)

    own = pl.ds(pl.multiple_of(column * width, width), width)
    gain = gain_ref[...]
    piece_rows = 32

    def normalise(i):
        x_copies[i].wait()
        for piece in range(tile // piece_rows):
            at = i * tile + piece * piece_rows
            widened = x_ref[at:at + piece_rows, :].astype(F32)
            centered = widened - jnp.mean(widened, axis=1, keepdims=True)
            variance = jnp.mean(centered * centered, axis=1, keepdims=True)
            scaled = (centered * lax.rsqrt(variance + 1e-05) * gain).astype(BF)
            normed_ref[i % 2, piece * piece_rows:(piece + 1) * piece_rows, :] = scaled

    def project(i):
        here = slice(i * tile, (i + 1) * tile)
        both = dot(normed_ref[i % 2], w_ref[...])
        q_ref[here, :] = (both[:, :width] * (1.0 / math.sqrt(HEAD_DIM))).astype(BF)
        k_ref[here, :] = both[:, width:2 * width].astype(BF)
        v_ref[here, :] = both[:, 2 * width:].astype(BF)
        slot = jnp.concatenate(
            [slot_rows_ref[b:b + 1, :] for b in range(i * tile // LANES, (i + 1) * tile // LANES)], axis=1
        )
        member = (iota((SLOTS, tile), 0).astype(F32) == slot).astype(F32).astype(BF)
        return dot(member, x_ref[here, own])

    tokens_sum = jnp.zeros((SLOTS, width), F32)
    normalise(0)
    for copy in w_copies[:3]:
        copy.wait()
    for i in range(1, tiles):
        normalise(i)
        tokens_sum += project(i - 1)
    tokens_sum += project(tiles - 1)
    part_ref[:SLOTS, own] = tokens_sum

    low_head = iota((QB, LANES), 1) < HEAD_DIM

    def two_heads(block, pair):
        both = q_ref[pl.ds(pl.multiple_of(block * QB, QB), QB), pair * LANES:(pair + 1) * LANES]
        zero = jnp.zeros_like(both)
        return jnp.concatenate(
            [jnp.where(low_head, both, zero), jnp.where(low_head, zero, both)], axis=0
        )

    def query_slots(block):
        return slot_rows_ref[pl.ds(block, 1), :]

    def masked_scores(block, pair, at, extent):
        keys = k_ref[pl.ds(at, extent), pair * LANES:(pair + 1) * LANES]
        scores = dot(keys, two_heads(block, pair), NT)
        same = slot_ref[pl.ds(at, extent), :] == query_slots(block)
        same = jnp.concatenate([same, same], axis=1)
        return jnp.where(same, scores, -1e30)

    def pooled_shares(block, raised, inverse):
        member = iota((SLOTS, QB), 0).astype(F32) == query_slots(block)
        zero = jnp.zeros((SLOTS, QB), F32)
        left = jnp.concatenate([jnp.where(member, inverse[:, :QB], 0.0), zero], axis=1)
        right = jnp.concatenate([zero, jnp.where(member, inverse[:, QB:], 0.0)], axis=1)
        shares = jnp.concatenate([left, right], axis=0).astype(BF)
        return dot(shares, raised.astype(BF), NT).astype(BF)

    def values_at(pair, at, extent):
        return v_ref[pl.ds(at, extent), pair * LANES:(pair + 1) * LANES]

    def straight(blocks, begins, extent):
        ats = [pl.multiple_of(jnp.minimum(begin, length - extent), 16) for begin in begins]
        for pair in range(pairs):
            chains = list(zip(blocks, ats))
            scores = [masked_scores(block, pair, at, extent) for block, at in chains]
            raised = [jnp.exp(s - jnp.max(s, axis=0, keepdims=True)) for s in scores]
            inverse = [1.0 / jnp.sum(r, axis=0, keepdims=True) for r in raised]
            shares = [pooled_shares(block, r, v) for block, r, v in zip(blocks, raised, inverse)]
            total = [dot(share, values_at(pair, at, extent)) for share, at in zip(shares, ats)]
            acc_ref[pair] += functools.reduce(jnp.add, total)

    def any_length(block):
        chunk = 256
        first_chunk = windows_sm[0, block] // chunk
        end_chunk = (windows_sm[1, block] + chunk - 1) // chunk
        for pair in range(pairs):

            def scores_at(index):
                at = pl.multiple_of(index * chunk, chunk)
                return at, masked_scores(block, pair, at, chunk)

            def forward(index, carry):
                top, total = carry
                _, scores = scores_at(index)
                higher = jnp.maximum(top, jnp.max(scores, axis=0, keepdims=True))
                raised = jnp.sum(jnp.exp(scores - higher), axis=0, keepdims=True)
                return higher, total * jnp.exp(top - higher) + raised

            top, total = lax.fori_loop(
                first_chunk, end_chunk, forward,
                (jnp.full((1, 2 * QB), -1e30, F32), jnp.zeros((1, 2 * QB), F32)),
            )
            inverse = 1.0 / total

            def again(index, nothing):
                at, scores = scores_at(index)
                raised = jnp.exp(scores - top)
                acc_ref[pair] += dot(pooled_shares(block, raised, inverse), values_at(pair, at, chunk))
                return nothing

            lax.fori_loop(first_chunk, end_chunk, again, 0)

    def group_step(group, nothing):
        blocks = [group * GROUP + i for i in range(GROUP)]
        begins = [windows_sm[0, block] for block in blocks]
        widest = functools.reduce(
            jnp.maximum, [windows_sm[1, block] - begin for block, begin in zip(blocks, begins)]
        )
        done = jnp.int32(0)
        for extent in (256, 384, 640):
            if extent > length:
                break

            @pl.when((widest > done) & (widest <= extent))
            def run(extent=extent):
                straight(blocks, begins, extent)

            done = jnp.int32(extent)

        @pl.when(widest > done)
        def slow():
            def one(index, nothing):
                any_length(group * GROUP + index)
                return nothing

            lax.fori_loop(0, GROUP, one, 0)

        return nothing

    lax.fori_loop(0, blocks_all // GROUP, group_step, 0)

    low = iota((SLOTS, LANES), 1) < HEAD_DIM
    context = jnp.concatenate(
        [jnp.where(low, acc_ref[pair, :SLOTS], acc_ref[pair, SLOTS:]) for pair in range(pairs)], axis=1
    )
    upper = context.astype(BF)
    lower = (context - upper.astype(F32)).astype(BF)
    w_copies[3].wait()
    part_ref[:SLOTS, :] += dot(upper, wo_ref[...]) + dot(lower, wo_ref[...])
    sent = pick_rows(place_ref[...], part_ref[...])
    row_wide = iota((rows, 2 * LANES), 0) % block_rows
    for target in range(mp):
        piece = sent[:, target * width:(target + 1) * width]
        piece = jnp.where(row_wide == capacity + 1, meta_ref[0:1, :], piece)
        out_ref[target] = jnp.where(row_wide == capacity + 2, meta_ref[1:2, :], piece)


def row_sums(doc_ids, assigned, tokens, ln_gain, w_query, w_key, w_value, w_out, sizes):
    length, tile, slots, capacity, block_rows, dp, mp, width, cents = sizes
    rows = dp * block_rows
    return pl.pallas_call(
        functools.partial(row_kernel, sizes),
        in_specs=[pl.BlockSpec(memory_space=pltpu.HBM)] * 8,
        out_shape=jax.ShapeDtypeStruct((mp, rows, width), F32),
        scratch_shapes=[
            pltpu.VMEM((length // LANES, LANES), jnp.int32),
            pltpu.SMEM((length // LANES, LANES), jnp.int32),
            pltpu.SMEM((1, slots), jnp.int32),
            pltpu.VMEM((1, D), F32),
            pltpu.VMEM((length, D), BF),
            pltpu.VMEM((D, 3 * width), BF),
            pltpu.VMEM((width, D), BF),
            pltpu.VMEM((2, tile, D), BF),
            pltpu.VMEM((length, width), BF),
            pltpu.VMEM((length, width), BF),
            pltpu.VMEM((length, width), BF),
            pltpu.VMEM((length, LANES), F32),
            pltpu.VMEM((length // LANES, LANES), F32),
            pltpu.SMEM((2, length // QB), jnp.int32),
            pltpu.VMEM((rows, LANES), BF),
            pltpu.VMEM((8, 2 * LANES), F32),
            pltpu.VMEM((width // LANES, 2 * SLOTS, LANES), F32),
            pltpu.VMEM((LANES, D), F32),
            pltpu.SemaphoreType.DMA((4,)),
            pltpu.SemaphoreType.DMA((length // tile,)),
            pltpu.SemaphoreType.DMA((4,)),
        ],
        compiler_params=pltpu.CompilerParams(vmem_limit_bytes=48 * 1024 * 1024),
        name="row_sums",
    )(
        doc_ids.reshape(length // LANES, LANES), assigned.reshape(1, slots), ln_gain.reshape(1, D),
        tokens, w_query, w_key, w_value, w_out,
    )


def products_kernel(
    sizes, here_ref, own_ref, cent_ref, mass_ref, pay_ref, docs_ref, near_ref, info_ref, own_out_ref
):
    length, tile, slots, capacity, block_rows, dp, mp, width, cents = sizes
    me = lax.axis_index("dp")
    rows = dp * block_rows
    lane = iota((1, LANES), 1)

    def rows_of(meta, first_row, count):
        goes_to, counts = meta[0:1, :LANES], meta[0:1, LANES:]
        named, is_last = meta[1:2, :LANES], meta[1:2, LANES:]
        held = (goes_to == (iota((count, LANES), 0) + first_row).astype(F32)).astype(F32)

        def column(values):
            return jnp.sum(held * values, axis=1, keepdims=True)

        return column(named), column(counts), column(is_last), column(jnp.ones((1, LANES), F32))

    def carry_of(source):
        block = here_ref[pl.ds(pl.multiple_of(source * block_rows, 8), block_rows), :]
        counts = block[capacity + 1:capacity + 2, LANES:]
        count = jnp.sum(jnp.where(lane == slots, counts, 0.0), axis=1, keepdims=True)
        return block[capacity:capacity + 1, :], count

    columns = []
    for source in range(dp):
        base = source * block_rows
        block = here_ref[base:base + block_rows, :]
        meta = block[capacity + 1:capacity + 3, :]
        named, counts, is_last, held = rows_of(meta, me * block_rows, block_rows)
        sums = jnp.where(held > 0, block, 0.0)
        if source < dp - 1:
            carry, carry_count = carry_of(source + 1)
            sums = sums + is_last * carry
            counts = counts + is_last * carry_count
        docs_ref[base:base + block_rows, :] = sums
        columns.append((named - (me * cents).astype(F32), counts, held))
    local = jnp.concatenate([c[0] for c in columns], axis=0)
    counts = jnp.concatenate([c[1] for c in columns], axis=0)
    held = jnp.concatenate([c[2] for c in columns], axis=0)
    valid = ((held > 0) & (counts > 0)).astype(F32)

    docs = docs_ref[...]
    names = (iota((rows, cents), 1).astype(F32) == local) & (valid > 0)
    names = names.astype(F32)
    mass = jnp.sum(names * mass_ref[...], axis=1, keepdims=True)
    near = pick_rows(names.astype(BF), cent_ref[...])
    near_ref[...] = near

    own = own_ref[...]
    _, own_counts, own_last, _ = rows_of(own_ref[capacity + 1:capacity + 3, :], 0, rows)
    following = jnp.minimum(me + 1, dp - 1)
    more = (me < dp - 1).astype(F32)
    carry, carry_count = carry_of(following)
    own = own + own_last * (carry * more)
    own_counts = own_counts + own_last * (carry_count * more)
    own_out_ref[...] = own

    gram = dot(docs, docs, NT, precision=lax.Precision.HIGHEST)
    spot = iota((rows, LANES), 1)
    cross = jnp.sum(near * docs, axis=1, keepdims=True)
    square = jnp.sum(near * near, axis=1, keepdims=True)
    own_square = jnp.sum(own * own, axis=1, keepdims=True)
    doc_square = jnp.sum(docs * docs, axis=1, keepdims=True)
    for target in range(mp):
        pay_ref[target] = jnp.zeros(pay_ref.shape[1:], F32)
        pay_ref[target, :, :rows] = gram
        for i, sums in enumerate((cross, square, own_square, doc_square)):
            pay_ref[target, :, rows + i:rows + i + 1] = sums
    info_ref[...] = jnp.where(
        spot == 0, local, jnp.where(spot == 1, counts, jnp.where(spot == 2, valid, jnp.where(spot == 3, mass, own_counts)))
    )


def update_kernel(
    sizes, pay_ref, docs_ref, near_ref, info_ref, own_ref, meta_ref, cent_ref, vec_ref, new_ref
):
    length, tile, slots, capacity, block_rows, dp, mp, width, cents = sizes
    rows = dp * block_rows
    info = info_ref[...]
    local, counts, valid, mass, own_counts = (info[:, i:i + 1] for i in range(5))
    pay = functools.reduce(jnp.add, [pay_ref[i] for i in range(mp)])
    cross, square, own_square, doc_square = (pay[:, rows + i:rows + i + 1] for i in range(4))

    def scale(sums, count):
        inverse = 1.0 / jnp.maximum(count, 1.0)
        return inverse * lax.rsqrt(sums * inverse * inverse * (1.0 / D) + 1e-06)

    vectors = own_ref[...] * scale(own_square, own_counts)
    goes_to = meta_ref[capacity + 1:capacity + 2, :LANES]
    place = ((iota((rows, LANES), 0).astype(F32) == goes_to).astype(F32)).T
    vec_ref[...] = pick_rows(place[:slots].astype(BF), vectors)

    share = scale(doc_square, counts) * valid
    across = jnp.where(valid > 0, local, -1.0)
    flat = jnp.broadcast_to(across, (rows, LANES)).T[:1]
    share_flat = jnp.broadcast_to(share, (rows, LANES)).T[:1]
    cross_flat = jnp.broadcast_to(cross, (rows, LANES)).T[:1]
    same = (across == flat) & (valid > 0)
    mixed = jnp.where(same, share_flat, 0.0)
    gained = dot(mixed, docs_ref[...], precision=lax.Precision.HIGHEST)
    twice = dot(mixed, pay[:, :rows], precision=lax.Precision.HIGHEST)
    norm = (
        mass * mass * square
        + 2.0 * mass * jnp.sum(mixed * cross_flat, axis=1, keepdims=True)
        + jnp.sum(twice * mixed, axis=1, keepdims=True)
    )
    blended = mass * near_ref[...] + gained
    scaled = blended * lax.rsqrt(norm * (1.0 / D) + 1e-06)
    before = same & (iota((rows, rows), 0) < iota((rows, rows), 1))
    repeated = jnp.sum(before.astype(F32), axis=0, keepdims=True)
    target = jnp.where((flat >= 0) & (repeated < 0.5), flat, -1.0)
    hits = (iota((cents, rows), 0).astype(F32) == target).astype(F32)
    updated = pick_rows(hits.astype(BF), scaled)
    hit = jnp.sum(hits, axis=1, keepdims=True)
    new_ref[...] = jnp.where(hit > 0, updated, cent_ref[...])


def shards(
    tokens, doc_ids, ln_gain, w_query, w_key, w_value, w_out, centroids, cluster_mass, assigned
):
    length = tokens.shape[0]
    slots = assigned.shape[0]
    width = w_out.shape[0]
    cents = centroids.shape[0]
    dp = lax.axis_size("dp")
    mp = lax.axis_size("mp")
    capacity = max(2, (slots + dp - 2) // (dp - 1))
    block_rows = round_up(capacity + 3, 8)
    rows = dp * block_rows
    sizes = (length, min(256, length), slots, capacity, block_rows, dp, mp, width, cents)
    limit = pltpu.CompilerParams(vmem_limit_bytes=48 * 1024 * 1024)

    partial = row_sums(doc_ids, assigned, tokens, ln_gain, w_query, w_key, w_value, w_out, sizes)
    shared = lax.all_to_all(partial, "mp", split_axis=0, concat_axis=0, tiled=True)
    own = jnp.sum(shared, axis=0)
    here = lax.all_to_all(own, "dp", split_axis=0, concat_axis=0, tiled=True)

    pay, docs, near, info, own_sums = pl.pallas_call(
        functools.partial(products_kernel, sizes),
        out_shape=(
            jax.ShapeDtypeStruct((mp, rows, round_up(rows + 4, LANES)), F32),
            jax.ShapeDtypeStruct((rows, width), F32),
            jax.ShapeDtypeStruct((rows, width), F32),
            jax.ShapeDtypeStruct((rows, LANES), F32),
            jax.ShapeDtypeStruct((rows, width), F32),
        ),
        compiler_params=limit,
        name="products",
    )(here, own, centroids, cluster_mass.reshape(1, cents))
    pay = lax.all_to_all(pay, "mp", split_axis=0, concat_axis=0, tiled=True)
    return pl.pallas_call(
        functools.partial(update_kernel, sizes),
        out_shape=(
            jax.ShapeDtypeStruct((slots, width), F32),
            jax.ShapeDtypeStruct((cents, width), F32),
        ),
        compiler_params=limit,
        name="update",
    )(pay, docs, near, info, own_sums, own, centroids)


def solution(mesh):
    placed = (
        P("dp", None),
        P("dp"),
        P(),
        P(None, "mp"),
        P(None, "mp"),
        P(None, "mp"),
        P("mp", None),
        P("dp", "mp"),
        P("dp"),
        P("dp"),
    )
    return jax.shard_map(
        shards,
        mesh=mesh,
        in_specs=placed,
        out_specs=(P("dp", "mp"), P("dp", "mp")),
        check_vma=False,
    )
```

time: 255 us -> 55.6 us (0.22)
  matrix products: 95.1 us -> 0 us
  waiting for transfers between devices: 44 us -> 0 us
  blocking collectives: 65.1 us -> 30.5 us
  other arithmetic: 18.8 us -> 0.02 us
  Pallas kernels: 0 us -> 17.2 us
  between operations: 15 us -> 0.68 us
  local copies, waits for them, and re-layouts: 13.8 us -> 6.29 us
  starting transfers between devices: 2.61 us -> 0 us
    dot_general x10 -> x0, matrix products: 53.2 us -> none  [the longest x4 34.9 us: attend_block(): jnp.einsum('hqk,khd->qhd', weights, values_all, preferred_element_type=jn...]
    sub x4 -> x0, matrix products: 41.9 us -> none  [attend_block(): raised = jnp.exp(scores - top_score)]
    reduce_scatter x1 -> x0, waiting for transfers between devices: 37.5 us -> none  [shards(): lax.psum_scatter(partial_out, 'mp', scatter_dimension=1, tiled=True)]
    all_gather x1 -> x0, blocking collectives: 31.1 us -> none  [shards(): lax.all_gather(doc_vectors, 'dp', axis=0, tiled=True)]
    all_to_all x0 -> x3, blocking collectives: none -> 30.5 us  [the longest x1 13.4 us: shards(): here = lax.all_to_all(own, 'dp', split_axis=0, concat_axis=0, tiled=True)]
    unnamed x1 -> x0, blocking collectives: 22.4 us -> none
    pallas_call x0 -> x3, Pallas kernels: none -> 17.2 us  [the longest x1 14.2 us: row_sums(): pl.pallas_call(functools.partial(row_kernel, sizes), in_specs=[pl.BlockSp...]
    psum x2 -> x0, blocking collectives: 11.5 us -> none  [the longest x1 5.76 us: shards(): squares = lax.psum(jnp.sum(averages * averages, axis=1), 'mp')]
  transfers between devices with their start and end apart: 3 -> 0, of which waited for: 3 -> 0; matrix products, arithmetic and copies ran while one was open for 4% -> 0% of each run, Pallas kernels for 0% -> 0%
where the time goes in v1:
time: 55.6 us; the launch traced here: 54.6 us
  blocking collectives  30.5 us (55%)
  Pallas kernels  17.2 us (31%)
  local copies, waits for them, and re-layouts  6.29 us (11%)
  between operations  0.68 us (1%)
    pallas_call x1, Pallas kernels, row_sums(): pl.pallas_call(functools.partial(row_kernel, sizes), in_specs=[pl.BlockSp...  14.2 us
    all_to_all x1, blocking collectives, shards(): here = lax.all_to_all(own, 'dp', split_axis=0, concat_axis=0, tiled=True)  13.4 us
    all_to_all x1, blocking collectives, shards(): lax.all_to_all(partial, 'mp', split_axis=0, concat_axis=0, tiled=True)  10 us
    all_to_all x1, blocking collectives, shards(): pay = lax.all_to_all(pay, 'mp', split_axis=0, concat_axis=0, tiled=True)  7.02 us
    unnamed x18, local copies, waits for them, and re-layouts  6.29 us
    pallas_call x1, Pallas kernels, shards(): pl.pallas_call(functools.partial(update_kernel, sizes), out_shape=(jax.Sh...  2.22 us

profile of v1, /device:TPU:0, one launch (start us, length us, event | category | flops | bytes accessed | tf_op | source)
XLA Modules:
  0.0 54.6 jit_solution(1940934248092268603)
XLA Ops:
  0.6 0.0 copy-start
  0.6 0.0 copy-start.1
  0.7 1.1 %copy-done.1 = bf16[1024,256]{1,0:T(8,128)(2,1)S(1)} copy-done((bf16[1024,256]{1,0:T(8,128)(2,1)S(1)}, bf16[1024,256]{1,0:T(8,128)(2,1)}, u32[]{:S(2)}) %copy-start.1) | copy-done | bytes 524312
  1.8 0.0 copy-start.2
  1.8 1.0 %copy-done.2 = bf16[1024,256]{1,0:T(8,128)(2,1)S(1)} copy-done((bf16[1024,256]{1,0:T(8,128)(2,1)S(1)}, bf16[1024,256]{1,0:T(8,128)(2,1)}, u32[]{:S(2)}) %copy-start.2) | copy-done | bytes 524312
  2.8 0.0 copy-start.3
  2.8 1.0 %copy-done.3 = bf16[1024,256]{1,0:T(8,128)(2,1)S(1)} copy-done((bf16[1024,256]{1,0:T(8,128)(2,1)S(1)}, bf16[1024,256]{1,0:T(8,128)(2,1)}, u32[]{:S(2)}) %copy-start.3) | copy-done | bytes 524312
  3.9 0.0 copy-start.4
  3.9 1.0 %copy-done.4 = bf16[256,1024]{1,0:T(8,128)(2,1)S(1)} copy-done((bf16[256,1024]{1,0:T(8,128)(2,1)S(1)}, bf16[256,1024]{1,0:T(8,128)(2,1)}, u32[]{:S(2)}) %copy-start.4) | copy-done | bytes 524312
  4.9 0.0 copy-start.5
  4.9 0.7 %copy-done.5 = s32[2048]{0:T(1024)S(1)} copy-done((s32[2048]{0:T(1024)S(1)}, s32[2048]{0:T(1024)}, u32[]{:S(2)}) %copy-start.5) | copy-done | bytes 8216
  5.6 0.0 copy-start.6
  5.6 0.7 %copy-done.6 = f32[1024]{0:T(1024)S(1)} copy-done((f32[1024]{0:T(1024)S(1)}, f32[1024]{0:T(1024)}, u32[]{:S(2)}) %copy-start.6) | copy-done | bytes 4120
  6.3 0.0 copy-start.8
  6.3 0.7 %copy-done.8 = s32[32]{0:T(128)S(1)} copy-done((s32[32]{0:T(128)S(1)}, s32[32]{0:T(128)}, u32[]{:S(2)}) %copy-start.8) | copy-done | bytes 152
  6.9 0.0 copy-start.7
  6.9 14.2 %row_sums.1 = f32[4,64,256]{2,1,0:T(8,128)S(1)} custom-call(s32[16,128]{1,0:T(8,128)S(1)} %bitcast.8, s32[1,32]{1,0:T(1,128)S(1)} %bitcast.11, f32[1,1024]{1,0:T(1,128)S(1)} %bitcast.9, bf16[2048,1024]{1,0:T(8,128)(2,1)} %x_hbm.1, bf16[1024,256]{1,0:T(8,128)(2,1)S(1)} %copy-done.1, bf16[1024,256]{1,0:T(8,128)(2,1)S(1)} %copy-done.2, ...), custom_call_target="tpu_custom_call" | custom-call | tf_op jit(solution)/shard_map/row_sums/pallas_call | solution.py:285
  21.2 10.0 %all_to_all.21 = f32[4,64,256]{2,1,0:T(8,128)S(1)} all-to-all(f32[4,64,256]{2,1,0:T(8,128)S(1)} %row_sums.1), channel_id=1, replica_groups=mesh['dp'=8,'mp'=4] {'mp'}, dimensions={0} | all-to-all | bytes 524288 | tf_op jit(solution)/shard_map/all_to_all | solution.py:454
  31.2 13.4 %all_to_all.22 = f32[8,8,256]{2,1,0:T(8,128)S(1)} all-to-all(f32[8,8,256]{2,1,0:T(8,128)S(1)} %bitcast.6), channel_id=1, replica_groups=mesh['dp'=8,'mp'=4] {'dp'}, dimensions={0} | all-to-all | bytes 131072 | tf_op jit(solution)/shard_map/all_to_all | solution.py:456
  44.6 0.0 copy-done
  44.6 0.0 copy-done.7
  44.6 0.7 %products.1 = (f32[4,64,128]{2,1,0:T(8,128)S(1)}, f32[64,256]{1,0:T(8,128)S(1)}, f32[64,256]{1,0:T(8,128)S(1)}, f32[64,128]{1,0:T(8,128)S(1)}, f32[64,256]{1,0:T(8,128)S(1)}) custom-call(f32[64,256]{1,0:T(8,128)S(1)} %bitcast.7, f32[64,256]{1,0:T(8,128)S(1)} %reduce_sum.9.own_ref.meta_ref, f32[1024,256]{1,0:T(8,128)S(1)} %copy-done, f32[1,1024]{1,0:T(1,128)S(1)} %bitcast.10), custom_call_target="tpu_custom_call" | custom-call | tf_op jit(solution)/shard_map/products/pallas_call | solution.py:458
  45.4 7.0 %all_to_all.23.pay_ref = f32[4,64,128]{2,1,0:T(8,128)S(1)} all-to-all(f32[4,64,128]{2,1,0:T(8,128)S(1)} %get-tuple-element.7), channel_id=1, replica_groups=mesh['dp'=8,'mp'=4] {'mp'}, dimensions={0} | all-to-all | bytes 262144 | tf_op jit(solution)/shard_map/all_to_all | solution.py:470
  52.4 2.2 %update.1 = (f32[32,256]{1,0:T(8,128)}, f32[1024,256]{1,0:T(8,128)}) custom-call(f32[4,64,128]{2,1,0:T(8,128)S(1)} %all_to_all.23.pay_ref, f32[64,256]{1,0:T(8,128)S(1)} %get-tuple-element.8.docs_ref, f32[64,256]{1,0:T(8,128)S(1)} %get-tuple-element.9.near_ref, f32[64,128]{1,0:T(8,128)S(1)} %get-tuple-element.10.info_ref, ...), custom_call_target="tpu_custom_call" | custom-call | tf_op jit(solution)/shard_map/update/pallas_call | solution.py:471
  (1 shorter events, 0.0 us)
Async XLA Ops:
  0.6 44.0 %copy-start = (f32[1024,256]{1,0:T(8,128)S(1)}, f32[1024,256]{1,0:T(8,128)}, u32[]{:S(2)}) copy-start(f32[1024,256]{1,0:T(8,128)} %cent_ref.3) | copy-start | bytes 3145732
  0.6 1.1 %copy-start.1 = (bf16[1024,256]{1,0:T(8,128)(2,1)S(1)}, bf16[1024,256]{1,0:T(8,128)(2,1)}, u32[]{:S(2)}) copy-start(bf16[1024,256]{1,0:T(8,128)(2,1)} %wq_hbm.1) | copy-start | bytes 1572868
  1.8 1.0 %copy-start.2 = (bf16[1024,256]{1,0:T(8,128)(2,1)S(1)}, bf16[1024,256]{1,0:T(8,128)(2,1)}, u32[]{:S(2)}) copy-start(bf16[1024,256]{1,0:T(8,128)(2,1)} %wk_hbm.1) | copy-start | bytes 1572868
  2.8 1.0 %copy-start.3 = (bf16[1024,256]{1,0:T(8,128)(2,1)S(1)}, bf16[1024,256]{1,0:T(8,128)(2,1)}, u32[]{:S(2)}) copy-start(bf16[1024,256]{1,0:T(8,128)(2,1)} %wv_hbm.1) | copy-start | bytes 1572868
  3.9 1.0 %copy-start.4 = (bf16[256,1024]{1,0:T(8,128)(2,1)S(1)}, bf16[256,1024]{1,0:T(8,128)(2,1)}, u32[]{:S(2)}) copy-start(bf16[256,1024]{1,0:T(8,128)(2,1)} %wo_hbm.1) | copy-start | bytes 1572868
  4.9 0.7 %copy-start.5 = (s32[2048]{0:T(1024)S(1)}, s32[2048]{0:T(1024)}, u32[]{:S(2)}) copy-start(s32[2048]{0:T(1024)} %param.11) | copy-start | bytes 24580
  5.6 0.7 %copy-start.6 = (f32[1024]{0:T(1024)S(1)}, f32[1024]{0:T(1024)}, u32[]{:S(2)}) copy-start(f32[1024]{0:T(1024)} %param.12) | copy-start | bytes 12292
  6.3 0.7 %copy-start.8 = (s32[32]{0:T(128)S(1)}, s32[32]{0:T(128)}, u32[]{:S(2)}) copy-start(s32[32]{0:T(128)} %param.19) | copy-start | bytes 388
  6.9 37.7 %copy-start.7 = (f32[1024]{0:T(1024)S(1)}, f32[1024]{0:T(1024)}, u32[]{:S(2)}) copy-start(f32[1024]{0:T(1024)} %param.18) | copy-start | bytes 12292

commit v2 on v1

--- a/solution.py
+++ b/solution.py
@@ -309,7 +309,7 @@
             pltpu.SemaphoreType.DMA((length // tile,)),
             pltpu.SemaphoreType.DMA((4,)),
         ],
-        compiler_params=pltpu.CompilerParams(vmem_limit_bytes=48 * 1024 * 1024),
+        compiler_params=pltpu.CompilerParams(vmem_limit_bytes=62 * 1024 * 1024),
         name="row_sums",
     )(
         doc_ids.reshape(length // LANES, LANES), assigned.reshape(1, slots), ln_gain.reshape(1, D),

time: 55.6 us -> 52.3 us (0.941); the launches traced: 54.6 us -> 53 us
  local copies, waits for them, and re-layouts: 6.29 us -> 0.01 us
  Pallas kernels: 17.2 us -> 19.6 us
  blocking collectives: 30.5 us -> 32.7 us
    unnamed x18 -> x4, local copies, waits for them, and re-layouts: 6.29 us -> 0.01 us
    pallas_call x1, Pallas kernels: 14.2 us -> 16.6 us  [row_sums(): pl.pallas_call(functools.partial(row_kernel, sizes), in_specs=[pl.BlockSp...]
    all_to_all x1, blocking collectives: 13.4 us -> 15.5 us  [shards(): here = lax.all_to_all(own, 'dp', split_axis=0, concat_axis=0, tiled=True)]
where the time goes in v2:
time: 52.3 us; the launch traced here: 53 us
  blocking collectives  32.7 us (63%)
  Pallas kernels  19.6 us (37%)
  between operations  0.67 us (1%)
    pallas_call x1, Pallas kernels, row_sums(): pl.pallas_call(functools.partial(row_kernel, sizes), in_specs=[pl.BlockSp...  16.6 us
    all_to_all x1, blocking collectives, shards(): here = lax.all_to_all(own, 'dp', split_axis=0, concat_axis=0, tiled=True)  15.5 us
    all_to_all x1, blocking collectives, shards(): lax.all_to_all(partial, 'mp', split_axis=0, concat_axis=0, tiled=True)  10.2 us
    all_to_all x1, blocking collectives, shards(): pay = lax.all_to_all(pay, 'mp', split_axis=0, concat_axis=0, tiled=True)  7.02 us
    pallas_call x1, Pallas kernels, shards(): pl.pallas_call(functools.partial(update_kernel, sizes), out_shape=(jax.Sh...  2.22 us

profile of v2, /device:TPU:0, one launch (start us, length us, event | category | flops | bytes accessed | tf_op | source)
XLA Modules:
  0.0 53.0 jit_solution(12565737958772724289)
XLA Ops:
  0.6 0.0 copy-start
  0.6 0.0 copy-start.1
  0.7 16.6 %row_sums.1 = f32[4,64,256]{2,1,0:T(8,128)} custom-call(s32[16,128]{1,0:T(8,128)} %bitcast.9, s32[1,32]{1,0:T(1,128)} %bitcast.11, f32[1,1024]{1,0:T(1,128)} %bitcast.10, bf16[2048,1024]{1,0:T(8,128)(2,1)} %x_hbm.1, bf16[1024,256]{1,0:T(8,128)(2,1)} %wq_hbm.1, bf16[1024,256]{1,0:T(8,128)(2,1)} %wk_hbm.1, bf16[1024,256]{1,0:T(8,128)(2,1)} %wv_hbm.1, ...), custom_call_target="tpu_custom_call" | custom-call | tf_op jit(solution)/shard_map/row_sums/pallas_call | solution.py:285
  17.2 10.2 %all_to_all.21 = f32[4,64,256]{2,1,0:T(8,128)S(1)} all-to-all(f32[4,64,256]{2,1,0:T(8,128)} %row_sums.1), channel_id=1, replica_groups=mesh['dp'=8,'mp'=4] {'mp'}, dimensions={0} | all-to-all | bytes 524288 | tf_op jit(solution)/shard_map/all_to_all | solution.py:454
  27.5 15.5 %all_to_all.22 = f32[8,8,256]{2,1,0:T(8,128)S(1)} all-to-all(f32[8,8,256]{2,1,0:T(8,128)S(1)} %bitcast.6), channel_id=1, replica_groups=mesh['dp'=8,'mp'=4] {'dp'}, dimensions={0} | all-to-all | bytes 131072 | tf_op jit(solution)/shard_map/all_to_all | solution.py:456
  43.0 0.0 copy-done
  43.0 0.0 copy-done.1
  43.0 0.8 %products.1 = (f32[4,64,128]{2,1,0:T(8,128)S(1)}, f32[64,256]{1,0:T(8,128)S(1)}, f32[64,256]{1,0:T(8,128)S(1)}, f32[64,128]{1,0:T(8,128)S(1)}, f32[64,256]{1,0:T(8,128)S(1)}) custom-call(f32[64,256]{1,0:T(8,128)S(1)} %bitcast.7, f32[64,256]{1,0:T(8,128)S(1)} %reduce_sum.9.own_ref.meta_ref, f32[1024,256]{1,0:T(8,128)S(1)} %copy-done, f32[1,1024]{1,0:T(1,128)S(1)} %bitcast.8), custom_call_target="tpu_custom_call" | custom-call | tf_op jit(solution)/shard_map/products/pallas_call | solution.py:458
  43.7 7.0 %all_to_all.23.pay_ref = f32[4,64,128]{2,1,0:T(8,128)S(1)} all-to-all(f32[4,64,128]{2,1,0:T(8,128)S(1)} %get-tuple-element.7), channel_id=1, replica_groups=mesh['dp'=8,'mp'=4] {'mp'}, dimensions={0} | all-to-all | bytes 262144 | tf_op jit(solution)/shard_map/all_to_all | solution.py:470
  50.8 2.2 %update.1 = (f32[32,256]{1,0:T(8,128)}, f32[1024,256]{1,0:T(8,128)}) custom-call(f32[4,64,128]{2,1,0:T(8,128)S(1)} %all_to_all.23.pay_ref, f32[64,256]{1,0:T(8,128)S(1)} %get-tuple-element.8.docs_ref, f32[64,256]{1,0:T(8,128)S(1)} %get-tuple-element.9.near_ref, f32[64,128]{1,0:T(8,128)S(1)} %get-tuple-element.10.info_ref, ...), custom_call_target="tpu_custom_call" | custom-call | tf_op jit(solution)/shard_map/update/pallas_call | solution.py:471
  (1 shorter events, 0.0 us)
Async XLA Ops:
  0.6 42.3 %copy-start = (f32[1024,256]{1,0:T(8,128)S(1)}, f32[1024,256]{1,0:T(8,128)}, u32[]{:S(2)}) copy-start(f32[1024,256]{1,0:T(8,128)} %cent_ref.3) | copy-start | bytes 3145732
  0.6 42.3 %copy-start.1 = (f32[1024]{0:T(1024)S(1)}, f32[1024]{0:T(1024)}, u32[]{:S(2)}) copy-start(f32[1024]{0:T(1024)} %param.18) | copy-start | bytes 12292

commit v3 on v2

--- a/solution.py
+++ b/solution.py
@@ -10,9 +10,8 @@
 
 D = 1024
 HEAD_DIM = 64
-QB = 128
-GROUP = 4
-SLOTS = 48
+QB = 64
+GROUP = 8
 LANES = 128
 BF = jnp.bfloat16
 F32 = jnp.float32
@@ -50,15 +49,16 @@
 def row_kernel(
     sizes, ids_hbm, assigned_hbm, gain_hbm, x_hbm, wq_hbm, wk_hbm, wv_hbm, wo_hbm, out_ref,
     ids_ref, ids_sm, assigned_sm, gain_ref, x_ref, w_ref, wo_ref, normed_ref, q_ref, k_ref, v_ref,
-    slot_ref, slot_rows_ref, windows_sm, place_ref, meta_ref, acc_ref, part_ref, small_sems, x_sems, w_sems,
+    slot_ref, query_slots_ref, windows_ref, windows_sm, pool_ref, meta_ref, share_ref, small_sems, x_sems, w_sems,
 ):
     length, tile, slots, capacity, block_rows, dp, mp, width, cents = sizes
     tiles = length // tile
-    blocks_all = length // QB
+    lane_blocks = length // LANES
     rows = dp * block_rows
+    heads = width // HEAD_DIM
+    halves = width // LANES
     row = lax.axis_index("dp")
     column = lax.axis_index("mp")
-    pairs = width // LANES
 
     small_copies = [
         pltpu.make_async_copy(ids_hbm, ids_ref, small_sems.at[0]),
@@ -71,43 +71,32 @@
         for i in range(tiles)
     ]
     w_copies = [
-        pltpu.make_async_copy(w_hbm, w_ref.at[:, pl.ds(i * width, width)], w_sems.at[i])
+        pltpu.make_async_copy(w_hbm, w_ref.at[i], w_sems.at[i])
         for i, w_hbm in enumerate((wq_hbm, wk_hbm, wv_hbm))
     ] + [pltpu.make_async_copy(wo_hbm, wo_ref, w_sems.at[3])]
-    for copy in small_copies + x_copies[:1] + w_copies[:3] + x_copies[1:] + w_copies[3:]:
+    for copy in small_copies + x_copies[:1]:
         copy.start()
+    for copy in w_copies[:3]:
+        copy.start(priority=1)
+    for copy in x_copies[1:]:
+        copy.start()
+    w_copies[3].start(priority=1)
     for copy in small_copies:
         copy.wait()
 
     ids = ids_ref[...]
     local = ids - row * slots
     slot_rows = jnp.where(local < 0, slots, local).astype(F32)
-    slot_rows_ref[...] = slot_rows
-    on_diagonal = iota((LANES, LANES), 0) == iota((LANES, LANES), 1)
-    ones = jnp.ones((LANES, LANES), BF)
-    counts = jnp.zeros((8, LANES), F32)
-    for block in range(blocks_all):
-        slot = slot_rows[block:block + 1, :]
-        diagonal = jnp.where(on_diagonal, slot, 0.0).astype(BF)
-        slot_ref[block * LANES:(block + 1) * LANES, :] = dot(diagonal, ones)
-        member = (iota((LANES, LANES), 0).astype(F32) == slot).astype(F32).astype(BF)
-        counts += dot(ones[:8], member, NT)
-
-    for block in range(blocks_all):
-        first = ids_sm[block, 0]
-        last = ids_sm[block, QB - 1]
-        begin = jnp.sum((ids < first).astype(F32)).astype(jnp.int32)
-        end = jnp.sum((ids <= last).astype(F32)).astype(jnp.int32)
-        windows_sm[0, block] = (begin // 16) * 16
-        windows_sm[1, block] = end
+    turned = pltpu.roll(slot_rows, QB, 1)
+    front = iota(slot_rows.shape, 1) < QB
+    query_slots_ref[0] = jnp.where(front, slot_rows, turned)
+    query_slots_ref[1] = jnp.where(front, turned, slot_rows)
 
     lane = iota((1, LANES), 1)
     named = jnp.full((1, LANES), -1, jnp.int32)
-    owner = jnp.full((1, LANES), -1, jnp.int32)
     for j in range(slots):
-        name = assigned_sm[0, j]
-        named = jnp.where(lane == j, name, named)
-        owner = jnp.where(lane == j, name // cents, owner)
+        named = jnp.where(lane == j, assigned_sm[0, j], named)
+    owner = named // cents
     wide = jnp.broadcast_to(owner.astype(F32), (LANES, LANES))
     earlier = (wide.T == wide) & (iota((LANES, LANES), 0) < iota((LANES, LANES), 1))
     rank = jnp.sum(earlier.astype(F32), axis=0, keepdims=True)
@@ -116,132 +105,201 @@
     place = (row_of.astype(F32) == goes_to) | (
         (row_of % block_rows == capacity) & (iota((rows, LANES), 1) == slots)
     )
-    place_ref[...] = place.astype(F32).astype(BF)
-    last_slot = ids_sm[blocks_all - 1, QB - 1] - row * slots
+    place = place.astype(F32).astype(BF)
+
+    on_diagonal = iota((LANES, LANES), 0) == iota((LANES, LANES), 1)
+    ones = jnp.ones((LANES, LANES), BF)
+    counts = []
+    for block in range(lane_blocks):
+        here = slice(block * LANES, (block + 1) * LANES)
+        slot = slot_rows[block:block + 1, :]
+        diagonal = jnp.where(on_diagonal, slot, 0.0).astype(BF)
+        slot_ref[here, :] = dot(diagonal, ones)
+        member = (iota((LANES, LANES), 0).astype(F32) == slot).astype(F32).astype(BF)
+        counts.append(dot(ones[:8], member, NT))
+        pool_ref[:, here] = dot(place, member).astype(BF)
+    counts = functools.reduce(jnp.add, counts)
+
+    def order(shape, dim):
+        slot = iota(shape, dim)
+        return jnp.where(slot == slots, 0, slot + 1)
+
+    before = (order((LANES, LANES), 0) < order((LANES, LANES), 1)) & (iota((LANES, LANES), 0) <= slots)
+    before = before.astype(F32).astype(BF)
+    upper = counts.astype(BF)
+    starts = dot(upper, before) + dot((counts - upper.astype(F32)).astype(BF), before)
+
+    def at_position(values, position):
+        mine = iota(slot_rows.shape, 1).astype(F32) == slot_rows[:, position:position + 1]
+        return jnp.sum(jnp.where(mine, values[:1], 0.0), axis=1, keepdims=True)
+
+    spot = iota(slot_rows.shape, 1)
+    table = jnp.zeros(slot_rows.shape, F32)
+    for part in range(LANES // QB):
+        table = jnp.where(spot == 2 * part, at_position(starts, part * QB), table)
+        table = jnp.where(spot == 2 * part + 1, at_position(starts + counts, (part + 1) * QB - 1), table)
+    windows_ref[...] = table.astype(jnp.int32)
+    windows_copy = pltpu.make_async_copy(windows_ref, windows_sm, small_sems.at[4])
+    windows_copy.start()
+
+    last_slot = ids_sm[lane_blocks - 1, LANES - 1] - row * slots
     speaks = (column == 0).astype(F32)
     meta_ref[0:1, :LANES] = goes_to * speaks
     meta_ref[0:1, LANES:] = counts[:1] * speaks
     meta_ref[1:2, :LANES] = named.astype(F32) * speaks
     meta_ref[1:2, LANES:] = (lane == last_slot).astype(F32) * speaks
-    part_ref[...] = jnp.zeros_like(part_ref)
-    acc_ref[...] = jnp.zeros_like(acc_ref)
+    share_ref[...] = jnp.zeros_like(share_ref)
 
     own = pl.ds(pl.multiple_of(column * width, width), width)
     gain = gain_ref[...]
     piece_rows = 32
-
-    def normalise(i):
-        x_copies[i].wait()
-        for piece in range(tile // piece_rows):
-            at = i * tile + piece * piece_rows
-            widened = x_ref[at:at + piece_rows, :].astype(F32)
-            centered = widened - jnp.mean(widened, axis=1, keepdims=True)
-            variance = jnp.mean(centered * centered, axis=1, keepdims=True)
-            scaled = (centered * lax.rsqrt(variance + 1e-05) * gain).astype(BF)
-            normed_ref[i % 2, piece * piece_rows:(piece + 1) * piece_rows, :] = scaled
-
-    def project(i):
+    pieces = tile // piece_rows
+
+    def piece_of(i, piece):
+        at = i * tile + piece * piece_rows
+        return x_ref[at:at + piece_rows, :].astype(F32)
+
+    def averages(i):
+        return [jnp.sum(piece_of(i, p), axis=1, keepdims=True) * (1.0 / D) for p in range(pieces)]
+
+    def spreads(i, means):
+        out = []
+        for p in range(pieces):
+            centered = piece_of(i, p) - means[p]
+            variance = jnp.sum(centered * centered, axis=1, keepdims=True) * (1.0 / D)
+            out.append(lax.rsqrt(variance + 1e-05))
+        return out
+
+    def scale(i, means, inverses):
+        for p in range(pieces):
+            scaled = (piece_of(i, p) - means[p]) * inverses[p] * gain
+            normed_ref[i % 2, p * piece_rows:(p + 1) * piece_rows, :] = scaled.astype(BF)
+
+    def project(i, which):
         here = slice(i * tile, (i + 1) * tile)
-        both = dot(normed_ref[i % 2], w_ref[...])
-        q_ref[here, :] = (both[:, :width] * (1.0 / math.sqrt(HEAD_DIM))).astype(BF)
-        k_ref[here, :] = both[:, width:2 * width].astype(BF)
-        v_ref[here, :] = both[:, 2 * width:].astype(BF)
-        slot = jnp.concatenate(
-            [slot_rows_ref[b:b + 1, :] for b in range(i * tile // LANES, (i + 1) * tile // LANES)], axis=1
+        result = dot(normed_ref[i % 2], w_ref[which])
+        if which == 0:
+            q_ref[here, :] = (result * (1.0 / math.sqrt(HEAD_DIM))).astype(BF)
+        else:
+            (k_ref if which == 1 else v_ref)[here, :] = result.astype(BF)
+
+    tokens_sum = jnp.zeros((rows, width), F32)
+    means, inverses = {}, {}
+    for i in range(-2, tiles):
+        ahead = i + 2
+        if ahead < tiles:
+            x_copies[ahead].wait()
+            means[ahead] = averages(ahead)
+        if i == 0:
+            for copy in w_copies[:3]:
+                copy.wait()
+        if i >= 0:
+            project(i, 0)
+        if ahead < tiles:
+            inverses[ahead] = spreads(ahead, means[ahead])
+        if i >= 0:
+            project(i, 1)
+        if 0 <= i + 1 < tiles:
+            scale(i + 1, means[i + 1], inverses[i + 1])
+        if i >= 0:
+            project(i, 2)
+            here = slice(i * tile, (i + 1) * tile)
+            tokens_sum += dot(pool_ref[:, here], x_ref[here, own])
+
+    windows_copy.wait()
+
+    def window(block_pair, part):
+        return (windows_sm[block_pair, 2 * part] // 16) * 16, windows_sm[block_pair, 2 * part + 1]
+
+    def all_heads(block):
+        at = pl.multiple_of(block * QB, QB)
+        zero = jnp.zeros((QB, LANES), BF)
+        left = iota((QB, LANES), 1) < HEAD_DIM
+        stacked = []
+        for half in range(halves):
+            piece = q_ref[pl.ds(at, QB), half * LANES:(half + 1) * LANES]
+            for kept in (left, jnp.logical_not(left)):
+                mine = jnp.where(kept, piece, zero)
+                stacked.append(jnp.concatenate([mine if h == half else zero for h in range(halves)], axis=1))
+        return jnp.concatenate(stacked, axis=0)
+
+    def masked_scores(block, parity, at, extent):
+        scores = dot(k_ref[pl.ds(at, extent), :], all_heads(block), NT)
+        same = slot_ref[pl.ds(at, extent), :] == query_slots_ref[parity, pl.ds(block // 2, 1), :]
+        return jnp.concatenate(
+            [
+                jnp.where(same, scores[:, half * LANES:(half + 1) * LANES], -1e30)
+                for half in range(halves)
+            ],
+            axis=1,
         )
-        member = (iota((SLOTS, tile), 0).astype(F32) == slot).astype(F32).astype(BF)
-        return dot(member, x_ref[here, own])
-
-    tokens_sum = jnp.zeros((SLOTS, width), F32)
-    normalise(0)
-    for copy in w_copies[:3]:
-        copy.wait()
-    for i in range(1, tiles):
-        normalise(i)
-        tokens_sum += project(i - 1)
-    tokens_sum += project(tiles - 1)
-    part_ref[:SLOTS, own] = tokens_sum
-
-    low_head = iota((QB, LANES), 1) < HEAD_DIM
-
-    def two_heads(block, pair):
-        both = q_ref[pl.ds(pl.multiple_of(block * QB, QB), QB), pair * LANES:(pair + 1) * LANES]
-        zero = jnp.zeros_like(both)
-        return jnp.concatenate(
-            [jnp.where(low_head, both, zero), jnp.where(low_head, zero, both)], axis=0
-        )
-
-    def query_slots(block):
-        return slot_rows_ref[pl.ds(block, 1), :]
-
-    def masked_scores(block, pair, at, extent):
-        keys = k_ref[pl.ds(at, extent), pair * LANES:(pair + 1) * LANES]
-        scores = dot(keys, two_heads(block, pair), NT)
-        same = slot_ref[pl.ds(at, extent), :] == query_slots(block)
-        same = jnp.concatenate([same, same], axis=1)
-        return jnp.where(same, scores, -1e30)
-
-    def pooled_shares(block, raised, inverse):
-        member = iota((SLOTS, QB), 0).astype(F32) == query_slots(block)
-        zero = jnp.zeros((SLOTS, QB), F32)
-        left = jnp.concatenate([jnp.where(member, inverse[:, :QB], 0.0), zero], axis=1)
-        right = jnp.concatenate([zero, jnp.where(member, inverse[:, QB:], 0.0)], axis=1)
-        shares = jnp.concatenate([left, right], axis=0).astype(BF)
-        return dot(shares, raised.astype(BF), NT).astype(BF)
-
-    def values_at(pair, at, extent):
-        return v_ref[pl.ds(at, extent), pair * LANES:(pair + 1) * LANES]
+
+    head_of_lane = (iota((8, width), 1) // HEAD_DIM) == (iota((8, width), 0) % heads)
+    upper_rows = iota((8, width), 0) < heads
+
+    def key_shares(raised, inverse):
+        upper = inverse.astype(BF).astype(F32)
+        parts = jnp.where(upper_rows, upper, inverse - upper)
+        return dot(jnp.where(head_of_lane, parts, 0.0).astype(BF), raised.astype(BF), NT)
 
     def straight(blocks, begins, extent):
+        padded = round_up(extent, LANES)
         ats = [pl.multiple_of(jnp.minimum(begin, length - extent), 16) for begin in begins]
-        for pair in range(pairs):
-            chains = list(zip(blocks, ats))
-            scores = [masked_scores(block, pair, at, extent) for block, at in chains]
-            raised = [jnp.exp(s - jnp.max(s, axis=0, keepdims=True)) for s in scores]
-            inverse = [1.0 / jnp.sum(r, axis=0, keepdims=True) for r in raised]
-            shares = [pooled_shares(block, r, v) for block, r, v in zip(blocks, raised, inverse)]
-            total = [dot(share, values_at(pair, at, extent)) for share, at in zip(shares, ats)]
-            acc_ref[pair] += functools.reduce(jnp.add, total)
+        scores = [masked_scores(block, i % 2, at, extent) for i, (block, at) in enumerate(zip(blocks, ats))]
+        raised = [jnp.exp(s - jnp.max(s, axis=0, keepdims=True)) for s in scores]
+        inverse = [1.0 / jnp.sum(r, axis=0, keepdims=True) for r in raised]
+        for at, r, v in zip(ats, raised, inverse):
+            if padded > extent:
+                r = jnp.concatenate([r, jnp.zeros((padded - extent, width), F32)], axis=0)
+            shares = jnp.concatenate([key_shares(r, v), jnp.zeros((8, LANES), F32)], axis=1)
+            base = pl.multiple_of((at // LANES) * LANES, LANES)
+            share_ref[:, pl.ds(base, padded + LANES)] += pltpu.roll(shares, at % LANES, 1)
 
     def any_length(block):
         chunk = 256
-        first_chunk = windows_sm[0, block] // chunk
-        end_chunk = (windows_sm[1, block] + chunk - 1) // chunk
-        for pair in range(pairs):
-
-            def scores_at(index):
-                at = pl.multiple_of(index * chunk, chunk)
-                return at, masked_scores(block, pair, at, chunk)
-
-            def forward(index, carry):
-                top, total = carry
-                _, scores = scores_at(index)
-                higher = jnp.maximum(top, jnp.max(scores, axis=0, keepdims=True))
-                raised = jnp.sum(jnp.exp(scores - higher), axis=0, keepdims=True)
-                return higher, total * jnp.exp(top - higher) + raised
-
-            top, total = lax.fori_loop(
-                first_chunk, end_chunk, forward,
-                (jnp.full((1, 2 * QB), -1e30, F32), jnp.zeros((1, 2 * QB), F32)),
-            )
-            inverse = 1.0 / total
-
-            def again(index, nothing):
-                at, scores = scores_at(index)
-                raised = jnp.exp(scores - top)
-                acc_ref[pair] += dot(pooled_shares(block, raised, inverse), values_at(pair, at, chunk))
-                return nothing
-
-            lax.fori_loop(first_chunk, end_chunk, again, 0)
+        begin, end = window(block // 2, block % 2)
+        first_chunk = begin // chunk
+        end_chunk = (end + chunk - 1) // chunk
+
+        def scores_at(index):
+            at = pl.multiple_of(index * chunk, chunk)
+            scores = dot(k_ref[pl.ds(at, chunk), :], all_heads(block), NT)
+            even = query_slots_ref[0, pl.ds(block // 2, 1), :]
+            odd = query_slots_ref[1, pl.ds(block // 2, 1), :]
+            query_slots = jnp.where(block % 2 == 0, even, odd)
+            same = slot_ref[pl.ds(at, chunk), :] == query_slots
+            masked = [
+                jnp.where(same, scores[:, half * LANES:(half + 1) * LANES], -1e30) for half in range(halves)
+            ]
+            return at, jnp.concatenate(masked, axis=1)
+
+        def forward(index, carry):
+            top, total = carry
+            _, scores = scores_at(index)
+            higher = jnp.maximum(top, jnp.max(scores, axis=0, keepdims=True))
+            raised = jnp.sum(jnp.exp(scores - higher), axis=0, keepdims=True)
+            return higher, total * jnp.exp(top - higher) + raised
+
+        top, total = lax.fori_loop(
+            first_chunk, end_chunk, forward,
+            (jnp.full((1, width), -1e30, F32), jnp.zeros((1, width), F32)),
+        )
+        inverse = 1.0 / total
+
+        def again(index, nothing):
+            at, scores = scores_at(index)
+            share_ref[:, pl.ds(at, chunk)] += key_shares(jnp.exp(scores - top), inverse)
+            return nothing
+
+        lax.fori_loop(first_chunk, end_chunk, again, 0)
 
     def group_step(group, nothing):
         blocks = [group * GROUP + i for i in range(GROUP)]
-        begins = [windows_sm[0, block] for block in blocks]
-        widest = functools.reduce(
-            jnp.maximum, [windows_sm[1, block] - begin for block, begin in zip(blocks, begins)]
-        )
+        spans = [window(group * (GROUP // 2) + i // 2, i % 2) for i in range(GROUP)]
+        begins = [begin for begin, _ in spans]
+        widest = functools.reduce(jnp.maximum, [end - begin for begin, end in spans])
         done = jnp.int32(0)
-        for extent in (256, 384, 640):
+        for extent in (192, 256, 384, 640):
             if extent > length:
                 break
 
@@ -261,22 +319,29 @@
 
         return nothing
 
-    lax.fori_loop(0, blocks_all // GROUP, group_step, 0)
-
-    low = iota((SLOTS, LANES), 1) < HEAD_DIM
-    context = jnp.concatenate(
-        [jnp.where(low, acc_ref[pair, :SLOTS], acc_ref[pair, SLOTS:]) for pair in range(pairs)], axis=1
-    )
+    lax.fori_loop(0, length // QB // GROUP, group_step, 0)
+
+    shares = share_ref[:, :length]
+    pool = pool_ref[...]
+    weighted = jnp.concatenate(
+        [pool * (shares[h:h + 1] + shares[heads + h:heads + h + 1]).astype(BF) for h in range(heads)], axis=0
+    )
+    every = dot(weighted, v_ref[...])
+    lane_head = iota((rows, width), 1) // HEAD_DIM
+    context = jnp.zeros((rows, width), F32)
+    for h in range(heads):
+        context = jnp.where(lane_head == h, every[h * rows:(h + 1) * rows], context)
     upper = context.astype(BF)
     lower = (context - upper.astype(F32)).astype(BF)
     w_copies[3].wait()
-    part_ref[:SLOTS, :] += dot(upper, wo_ref[...]) + dot(lower, wo_ref[...])
-    sent = pick_rows(place_ref[...], part_ref[...])
-    row_wide = iota((rows, 2 * LANES), 0) % block_rows
+    sent = dot(upper, wo_ref[...]) + dot(lower, wo_ref[...])
     for target in range(mp):
-        piece = sent[:, target * width:(target + 1) * width]
-        piece = jnp.where(row_wide == capacity + 1, meta_ref[0:1, :], piece)
-        out_ref[target] = jnp.where(row_wide == capacity + 2, meta_ref[1:2, :], piece)
+        out_ref[target] = sent[:, target * width:(target + 1) * width]
+    out_ref[column] += tokens_sum
+    for target in range(mp):
+        for block in range(dp):
+            at = block * block_rows + capacity + 1
+            out_ref[target, at:at + 2, :] = meta_ref[:2, :]
 
 
 def row_sums(doc_ids, assigned, tokens, ln_gain, w_query, w_key, w_value, w_out, sizes):
@@ -292,20 +357,20 @@
             pltpu.SMEM((1, slots), jnp.int32),
             pltpu.VMEM((1, D), F32),
             pltpu.VMEM((length, D), BF),
-            pltpu.VMEM((D, 3 * width), BF),
+            pltpu.VMEM((3, D, width), BF),
             pltpu.VMEM((width, D), BF),
             pltpu.VMEM((2, tile, D), BF),
             pltpu.VMEM((length, width), BF),
             pltpu.VMEM((length, width), BF),
             pltpu.VMEM((length, width), BF),
             pltpu.VMEM((length, LANES), F32),
-            pltpu.VMEM((length // LANES, LANES), F32),
-            pltpu.SMEM((2, length // QB), jnp.int32),
-            pltpu.VMEM((rows, LANES), BF),
+            pltpu.VMEM((2, length // LANES, LANES), F32),
+            pltpu.VMEM((length // LANES, LANES), jnp.int32),
+            pltpu.SMEM((length // LANES, LANES), jnp.int32),
+            pltpu.VMEM((rows, length), BF),
             pltpu.VMEM((8, 2 * LANES), F32),
-            pltpu.VMEM((width // LANES, 2 * SLOTS, LANES), F32),
-            pltpu.VMEM((LANES, D), F32),
-            pltpu.SemaphoreType.DMA((4,)),
+            pltpu.VMEM((8, length + 2 * LANES), F32),
+            pltpu.SemaphoreType.DMA((5,)),
             pltpu.SemaphoreType.DMA((length // tile,)),
             pltpu.SemaphoreType.DMA((4,)),
         ],
@@ -381,11 +446,12 @@
     square = jnp.sum(near * near, axis=1, keepdims=True)
     own_square = jnp.sum(own * own, axis=1, keepdims=True)
     doc_square = jnp.sum(docs * docs, axis=1, keepdims=True)
-    for target in range(mp):
-        pay_ref[target] = jnp.zeros(pay_ref.shape[1:], F32)
-        pay_ref[target, :, :rows] = gram
-        for i, sums in enumerate((cross, square, own_square, doc_square)):
-            pay_ref[target, :, rows + i:rows + i + 1] = sums
+    pay_ref[0] = jnp.zeros(pay_ref.shape[1:], F32)
+    pay_ref[0, :, :rows] = gram
+    for i, sums in enumerate((cross, square, own_square, doc_square)):
+        pay_ref[0, :, rows + i:rows + i + 1] = sums
+    for target in range(1, mp):
+        pay_ref[target] = pay_ref[0]
     info_ref[...] = jnp.where(
         spot == 0, local, jnp.where(spot == 1, counts, jnp.where(spot == 2, valid, jnp.where(spot == 3, mass, own_counts)))
     )

time: 52.3 us -> 51.7 us (0.989); the launches traced: 53 us -> 50.9 us
  blocking collectives: 32.7 us -> 31 us
    all_to_all x1, blocking collectives: 15.5 us -> 13.7 us  [shards(): here = lax.all_to_all(own, 'dp', split_axis=0, concat_axis=0, tiled=True)]
where the time goes in v3:
time: 51.7 us; the launch traced here: 50.9 us
  blocking collectives  31 us (60%)
  Pallas kernels  19.3 us (37%)
  between operations  0.67 us (1%)
    pallas_call x1, Pallas kernels, row_sums(): pl.pallas_call(functools.partial(row_kernel, sizes), in_specs=[pl.BlockSp...  16.3 us
    all_to_all x1, blocking collectives, shards(): here = lax.all_to_all(own, 'dp', split_axis=0, concat_axis=0, tiled=True)  13.7 us
    all_to_all x1, blocking collectives, shards(): lax.all_to_all(partial, 'mp', split_axis=0, concat_axis=0, tiled=True)  10.3 us
    all_to_all x1, blocking collectives, shards(): pay = lax.all_to_all(pay, 'mp', split_axis=0, concat_axis=0, tiled=True)  7.02 us
    pallas_call x1, Pallas kernels, shards(): pl.pallas_call(functools.partial(update_kernel, sizes), out_shape=(jax.Sh...  2.22 us

profile of v3, /device:TPU:0, one launch (start us, length us, event | category | flops | bytes accessed | tf_op | source)
XLA Modules:
  0.0 50.9 jit_solution(10594283552393045522)
XLA Ops:
  0.6 0.0 copy-start
  0.6 0.0 copy-start.1
  0.7 16.3 %row_sums.1 = f32[4,64,256]{2,1,0:T(8,128)} custom-call(s32[16,128]{1,0:T(8,128)} %bitcast.9, s32[1,32]{1,0:T(1,128)} %bitcast.11, f32[1,1024]{1,0:T(1,128)} %bitcast.10, bf16[2048,1024]{1,0:T(8,128)(2,1)} %x_hbm.1, bf16[1024,256]{1,0:T(8,128)(2,1)} %wq_hbm.1, bf16[1024,256]{1,0:T(8,128)(2,1)} %wk_hbm.1, bf16[1024,256]{1,0:T(8,128)(2,1)} %wv_hbm.1, ...), custom_call_target="tpu_custom_call" | custom-call | tf_op jit(solution)/shard_map/row_sums/pallas_call | solution.py:350
  17.0 10.3 %all_to_all.21 = f32[4,64,256]{2,1,0:T(8,128)S(1)} all-to-all(f32[4,64,256]{2,1,0:T(8,128)} %row_sums.1), channel_id=1, replica_groups=mesh['dp'=8,'mp'=4] {'mp'}, dimensions={0} | all-to-all | bytes 524288 | tf_op jit(solution)/shard_map/all_to_all | solution.py:520
  27.3 13.7 %all_to_all.22 = f32[8,8,256]{2,1,0:T(8,128)S(1)} all-to-all(f32[8,8,256]{2,1,0:T(8,128)S(1)} %bitcast.6), channel_id=1, replica_groups=mesh['dp'=8,'mp'=4] {'dp'}, dimensions={0} | all-to-all | bytes 131072 | tf_op jit(solution)/shard_map/all_to_all | solution.py:522
  40.9 0.0 copy-done
  40.9 0.0 copy-done.1
  40.9 0.7 %products.1 = (f32[4,64,128]{2,1,0:T(8,128)S(1)}, f32[64,256]{1,0:T(8,128)S(1)}, f32[64,256]{1,0:T(8,128)S(1)}, f32[64,128]{1,0:T(8,128)S(1)}, f32[64,256]{1,0:T(8,128)S(1)}) custom-call(f32[64,256]{1,0:T(8,128)S(1)} %bitcast.7, f32[64,256]{1,0:T(8,128)S(1)} %reduce_sum.9.own_ref.meta_ref, f32[1024,256]{1,0:T(8,128)S(1)} %copy-done, f32[1,1024]{1,0:T(1,128)S(1)} %bitcast.8), custom_call_target="tpu_custom_call" | custom-call | tf_op jit(solution)/shard_map/products/pallas_call | solution.py:524
  41.7 7.0 %all_to_all.23.pay_ref = f32[4,64,128]{2,1,0:T(8,128)S(1)} all-to-all(f32[4,64,128]{2,1,0:T(8,128)S(1)} %get-tuple-element.7), channel_id=1, replica_groups=mesh['dp'=8,'mp'=4] {'mp'}, dimensions={0} | all-to-all | bytes 262144 | tf_op jit(solution)/shard_map/all_to_all | solution.py:536
  48.7 2.2 %update.1 = (f32[32,256]{1,0:T(8,128)}, f32[1024,256]{1,0:T(8,128)}) custom-call(f32[4,64,128]{2,1,0:T(8,128)S(1)} %all_to_all.23.pay_ref, f32[64,256]{1,0:T(8,128)S(1)} %get-tuple-element.8.docs_ref, f32[64,256]{1,0:T(8,128)S(1)} %get-tuple-element.9.near_ref, f32[64,128]{1,0:T(8,128)S(1)} %get-tuple-element.10.info_ref, ...), custom_call_target="tpu_custom_call" | custom-call | tf_op jit(solution)/shard_map/update/pallas_call | solution.py:537
  (1 shorter events, 0.0 us)
Async XLA Ops:
  0.6 40.3 %copy-start = (f32[1024,256]{1,0:T(8,128)S(1)}, f32[1024,256]{1,0:T(8,128)}, u32[]{:S(2)}) copy-start(f32[1024,256]{1,0:T(8,128)} %cent_ref.3) | copy-start | bytes 3145732
  0.6 40.3 %copy-start.1 = (f32[1024]{0:T(1024)S(1)}, f32[1024]{0:T(1024)}, u32[]{:S(2)}) copy-start(f32[1024]{0:T(1024)} %param.18) | copy-start | bytes 12292

commit v4 on v3

--- a/solution.py
+++ b/solution.py
@@ -12,6 +12,7 @@
 HEAD_DIM = 64
 QB = 64
 GROUP = 8
+EXTENTS = (192, 256, 384, 640)
 LANES = 128
 BF = jnp.bfloat16
 F32 = jnp.float32
@@ -49,7 +50,7 @@
 def row_kernel(
     sizes, ids_hbm, assigned_hbm, gain_hbm, x_hbm, wq_hbm, wk_hbm, wv_hbm, wo_hbm, out_ref,
     ids_ref, ids_sm, assigned_sm, gain_ref, x_ref, w_ref, wo_ref, normed_ref, q_ref, k_ref, v_ref,
-    slot_ref, query_slots_ref, windows_ref, windows_sm, pool_ref, meta_ref, share_ref, small_sems, x_sems, w_sems,
+    slot_ref, query_slots_ref, windows_ref, windows_sm, pool_ref, meta_ref, share_ref, scores_ref, raised_ref, small_sems, x_sems, w_sems,
 ):
     length, tile, slots, capacity, block_rows, dp, mp, width, cents = sizes
     tiles = length // tile
@@ -152,60 +153,61 @@
 
     own = pl.ds(pl.multiple_of(column * width, width), width)
     gain = gain_ref[...]
-    piece_rows = 32
+    piece_rows = 64
     pieces = tile // piece_rows
-
-    def piece_of(i, piece):
-        at = i * tile + piece * piece_rows
-        return x_ref[at:at + piece_rows, :].astype(F32)
+    lane_slices = [slice(j * LANES, (j + 1) * LANES) for j in range(D // LANES)]
+
+    def piece_of(i, p, lanes):
+        at = i * tile + p * piece_rows
+        return x_ref[at:at + piece_rows, lanes].astype(F32)
 
     def averages(i):
-        return [jnp.sum(piece_of(i, p), axis=1, keepdims=True) * (1.0 / D) for p in range(pieces)]
-
-    def spreads(i, means):
         out = []
         for p in range(pieces):
-            centered = piece_of(i, p) - means[p]
-            variance = jnp.sum(centered * centered, axis=1, keepdims=True) * (1.0 / D)
+            total = functools.reduce(jnp.add, [piece_of(i, p, lanes) for lanes in lane_slices])
+            mean = jnp.sum(total, axis=1, keepdims=True) * (1.0 / D)
+            out.append(jnp.broadcast_to(mean, (piece_rows, LANES)))
+        return out
+
+    def centre(i, means):
+        out = []
+        for p in range(pieces):
+            here = slice(p * piece_rows, (p + 1) * piece_rows)
+            squares = jnp.zeros((piece_rows, LANES), F32)
+            for lanes in lane_slices:
+                centered = piece_of(i, p, lanes) - means[p]
+                squares += centered * centered
+                normed_ref[i % 2, here, lanes] = (centered * gain[:, lanes]).astype(BF)
+            variance = jnp.sum(squares, axis=1, keepdims=True) * (1.0 / D)
             out.append(lax.rsqrt(variance + 1e-05))
-        return out
-
-    def scale(i, means, inverses):
-        for p in range(pieces):
-            scaled = (piece_of(i, p) - means[p]) * inverses[p] * gain
-            normed_ref[i % 2, p * piece_rows:(p + 1) * piece_rows, :] = scaled.astype(BF)
-
-    def project(i, which):
+        return jnp.concatenate(out, axis=0)
+
+    def project(i, which, inverse):
         here = slice(i * tile, (i + 1) * tile)
-        result = dot(normed_ref[i % 2], w_ref[which])
         if which == 0:
-            q_ref[here, :] = (result * (1.0 / math.sqrt(HEAD_DIM))).astype(BF)
-        else:
-            (k_ref if which == 1 else v_ref)[here, :] = result.astype(BF)
+            inverse = inverse * (math.log2(math.e) / math.sqrt(HEAD_DIM))
+        result = (dot(normed_ref[i % 2], w_ref[which]) * inverse).astype(BF)
+        (q_ref, k_ref, v_ref)[which][here, :] = result
 
     tokens_sum = jnp.zeros((rows, width), F32)
-    means, inverses = {}, {}
-    for i in range(-2, tiles):
-        ahead = i + 2
+    inverses = {}
+    for i in range(-1, tiles):
+        ahead = i + 1
         if ahead < tiles:
             x_copies[ahead].wait()
-            means[ahead] = averages(ahead)
+            means = averages(ahead)
         if i == 0:
             for copy in w_copies[:3]:
                 copy.wait()
         if i >= 0:
-            project(i, 0)
+            project(i, 0, inverses[i])
         if ahead < tiles:
-            inverses[ahead] = spreads(ahead, means[ahead])
+            inverses[ahead] = centre(ahead, means)
         if i >= 0:
-            project(i, 1)
-        if 0 <= i + 1 < tiles:
-            scale(i + 1, means[i + 1], inverses[i + 1])
-        if i >= 0:
-            project(i, 2)
+            project(i, 1, inverses[i])
+            project(i, 2, inverses[i])
             here = slice(i * tile, (i + 1) * tile)
             tokens_sum += dot(pool_ref[:, here], x_ref[here, own])
-
     windows_copy.wait()
 
     def window(block_pair, part):
@@ -223,35 +225,49 @@
                 stacked.append(jnp.concatenate([mine if h == half else zero for h in range(halves)], axis=1))
         return jnp.concatenate(stacked, axis=0)
 
-    def masked_scores(block, parity, at, extent):
-        scores = dot(k_ref[pl.ds(at, extent), :], all_heads(block), NT)
-        same = slot_ref[pl.ds(at, extent), :] == query_slots_ref[parity, pl.ds(block // 2, 1), :]
-        return jnp.concatenate(
-            [
-                jnp.where(same, scores[:, half * LANES:(half + 1) * LANES], -1e30)
-                for half in range(halves)
-            ],
-            axis=1,
-        )
-
     head_of_lane = (iota((8, width), 1) // HEAD_DIM) == (iota((8, width), 0) % heads)
     upper_rows = iota((8, width), 0) < heads
 
     def key_shares(raised, inverse):
         upper = inverse.astype(BF).astype(F32)
         parts = jnp.where(upper_rows, upper, inverse - upper)
-        return dot(jnp.where(head_of_lane, parts, 0.0).astype(BF), raised.astype(BF), NT)
+        return dot(jnp.where(head_of_lane, parts, 0.0).astype(BF), raised, NT)
 
     def straight(blocks, begins, extent):
         padded = round_up(extent, LANES)
+        step = 64
         ats = [pl.multiple_of(jnp.minimum(begin, length - extent), 16) for begin in begins]
-        scores = [masked_scores(block, i % 2, at, extent) for i, (block, at) in enumerate(zip(blocks, ats))]
-        raised = [jnp.exp(s - jnp.max(s, axis=0, keepdims=True)) for s in scores]
-        inverse = [1.0 / jnp.sum(r, axis=0, keepdims=True) for r in raised]
-        for at, r, v in zip(ats, raised, inverse):
+        halves_of = [slice(half * LANES, (half + 1) * LANES) for half in range(halves)]
+        for i, (block, at) in enumerate(zip(blocks, ats)):
+            scores_ref[i, :extent, :] = dot(k_ref[pl.ds(at, extent), :], all_heads(block), NT)
+        tops = []
+        for i, (block, at) in enumerate(zip(blocks, ats)):
+            mine = query_slots_ref[i % 2, pl.ds(block // 2, 1), :]
+            top = [jnp.full((8, LANES), -1e30, F32) for _ in range(halves)]
+            for key in range(0, extent, step):
+                same = slot_ref[pl.ds(at + key, step), :] == mine
+                for half, lanes in enumerate(halves_of):
+                    masked = jnp.where(same, scores_ref[i, key:key + step, lanes], -1e30)
+                    scores_ref[i, key:key + step, lanes] = masked
+                    highest = jnp.max(masked.reshape(step // 8, 8, LANES), axis=0)
+                    top[half] = jnp.maximum(top[half], highest)
+            tops.append([jnp.max(t, axis=0, keepdims=True) for t in top])
+        inverses = []
+        for i in range(len(blocks)):
+            total = [jnp.zeros((8, LANES), F32) for _ in range(halves)]
+            for key in range(0, extent, step):
+                for half, lanes in enumerate(halves_of):
+                    raised = jnp.exp2(scores_ref[i, key:key + step, lanes] - tops[i][half])
+                    total[half] += jnp.sum(raised.reshape(step // 8, 8, LANES), axis=0)
+                    raised_ref[i, key:key + step, lanes] = raised.astype(BF)
             if padded > extent:
-                r = jnp.concatenate([r, jnp.zeros((padded - extent, width), F32)], axis=0)
-            shares = jnp.concatenate([key_shares(r, v), jnp.zeros((8, LANES), F32)], axis=1)
+                raised_ref[i, extent:padded, :] = jnp.zeros((padded - extent, width), BF)
+            inverses.append(
+                jnp.concatenate([1.0 / jnp.sum(t, axis=0, keepdims=True) for t in total], axis=1)
+            )
+        for i, at in enumerate(ats):
+            shares = key_shares(raised_ref[i, :padded, :], inverses[i])
+            shares = jnp.concatenate([shares, jnp.zeros((8, LANES), F32)], axis=1)
             base = pl.multiple_of((at // LANES) * LANES, LANES)
             share_ref[:, pl.ds(base, padded + LANES)] += pltpu.roll(shares, at % LANES, 1)
 
@@ -277,8 +293,8 @@
             top, total = carry
             _, scores = scores_at(index)
             higher = jnp.maximum(top, jnp.max(scores, axis=0, keepdims=True))
-            raised = jnp.sum(jnp.exp(scores - higher), axis=0, keepdims=True)
-            return higher, total * jnp.exp(top - higher) + raised
+            raised = jnp.sum(jnp.exp2(scores - higher), axis=0, keepdims=True)
+            return higher, total * jnp.exp2(top - higher) + raised
 
         top, total = lax.fori_loop(
             first_chunk, end_chunk, forward,
@@ -288,7 +304,7 @@
 
         def again(index, nothing):
             at, scores = scores_at(index)
-            share_ref[:, pl.ds(at, chunk)] += key_shares(jnp.exp(scores - top), inverse)
+            share_ref[:, pl.ds(at, chunk)] += key_shares(jnp.exp2(scores - top).astype(BF), inverse)
             return nothing
 
         lax.fori_loop(first_chunk, end_chunk, again, 0)
@@ -299,7 +315,7 @@
         begins = [begin for begin, _ in spans]
         widest = functools.reduce(jnp.maximum, [end - begin for begin, end in spans])
         done = jnp.int32(0)
-        for extent in (192, 256, 384, 640):
+        for extent in EXTENTS:
             if extent > length:
                 break
 
@@ -334,7 +350,8 @@
     upper = context.astype(BF)
     lower = (context - upper.astype(F32)).astype(BF)
     w_copies[3].wait()
-    sent = dot(upper, wo_ref[...]) + dot(lower, wo_ref[...])
+    sent = dot(jnp.concatenate([upper, lower], axis=0), wo_ref[...])
+    sent = sent[:rows] + sent[rows:]
     for target in range(mp):
         out_ref[target] = sent[:, target * width:(target + 1) * width]
     out_ref[column] += tokens_sum
@@ -370,6 +387,8 @@
             pltpu.VMEM((rows, length), BF),
             pltpu.VMEM((8, 2 * LANES), F32),
             pltpu.VMEM((8, length + 2 * LANES), F32),
+            pltpu.VMEM((GROUP, EXTENTS[-1], width), F32),
+            pltpu.VMEM((GROUP, EXTENTS[-1], width), BF),
             pltpu.SemaphoreType.DMA((5,)),
             pltpu.SemaphoreType.DMA((length // tile,)),
             pltpu.SemaphoreType.DMA((4,)),

time: 51.7 us -> 51.1 us (0.988)
  Pallas kernels: 19.3 us -> 18.5 us
  blocking collectives: 31 us -> 31.6 us
    pallas_call x1, Pallas kernels: 16.3 us -> 15.5 us  [row_sums(): pl.pallas_call(functools.partial(row_kernel, sizes), in_specs=[pl.BlockSp...]
    all_to_all x1, blocking collectives: 13.7 us -> 14.3 us  [shards(): here = lax.all_to_all(own, 'dp', split_axis=0, concat_axis=0, tiled=True)]
where the time goes in v4:
time: 51.1 us; the launch traced here: 50.8 us
  blocking collectives  31.6 us (62%)
  Pallas kernels  18.5 us (36%)
  between operations  0.67 us (1%)
    pallas_call x1, Pallas kernels, row_sums(): pl.pallas_call(functools.partial(row_kernel, sizes), in_specs=[pl.BlockSp...  15.5 us
    all_to_all x1, blocking collectives, shards(): here = lax.all_to_all(own, 'dp', split_axis=0, concat_axis=0, tiled=True)  14.3 us
    all_to_all x1, blocking collectives, shards(): lax.all_to_all(partial, 'mp', split_axis=0, concat_axis=0, tiled=True)  10.3 us
    all_to_all x1, blocking collectives, shards(): pay = lax.all_to_all(pay, 'mp', split_axis=0, concat_axis=0, tiled=True)  7.02 us
    pallas_call x1, Pallas kernels, shards(): pl.pallas_call(functools.partial(update_kernel, sizes), out_shape=(jax.Sh...  2.22 us

profile of v4, /device:TPU:0, one launch (start us, length us, event | category | flops | bytes accessed | tf_op | source)
XLA Modules:
  0.0 50.8 jit_solution(10323627607636943063)
XLA Ops:
  0.6 0.0 copy-start
  0.6 0.0 copy-start.1
  0.7 15.5 %row_sums.1 = f32[4,64,256]{2,1,0:T(8,128)} custom-call(s32[16,128]{1,0:T(8,128)} %bitcast.9, s32[1,32]{1,0:T(1,128)} %bitcast.11, f32[1,1024]{1,0:T(1,128)} %bitcast.10, bf16[2048,1024]{1,0:T(8,128)(2,1)} %x_hbm.1, bf16[1024,256]{1,0:T(8,128)(2,1)} %wq_hbm.1, bf16[1024,256]{1,0:T(8,128)(2,1)} %wk_hbm.1, bf16[1024,256]{1,0:T(8,128)(2,1)} %wv_hbm.1, ...), custom_call_target="tpu_custom_call" | custom-call | tf_op jit(solution)/shard_map/row_sums/pallas_call | solution.py:367
  16.2 10.3 %all_to_all.21 = f32[4,64,256]{2,1,0:T(8,128)S(1)} all-to-all(f32[4,64,256]{2,1,0:T(8,128)} %row_sums.1), channel_id=1, replica_groups=mesh['dp'=8,'mp'=4] {'mp'}, dimensions={0} | all-to-all | bytes 524288 | tf_op jit(solution)/shard_map/all_to_all | solution.py:539
  26.5 14.3 %all_to_all.22 = f32[8,8,256]{2,1,0:T(8,128)S(1)} all-to-all(f32[8,8,256]{2,1,0:T(8,128)S(1)} %bitcast.6), channel_id=1, replica_groups=mesh['dp'=8,'mp'=4] {'dp'}, dimensions={0} | all-to-all | bytes 131072 | tf_op jit(solution)/shard_map/all_to_all | solution.py:541
  40.8 0.0 copy-done
  40.8 0.0 copy-done.1
  40.8 0.7 %products.1 = (f32[4,64,128]{2,1,0:T(8,128)S(1)}, f32[64,256]{1,0:T(8,128)S(1)}, f32[64,256]{1,0:T(8,128)S(1)}, f32[64,128]{1,0:T(8,128)S(1)}, f32[64,256]{1,0:T(8,128)S(1)}) custom-call(f32[64,256]{1,0:T(8,128)S(1)} %bitcast.7, f32[64,256]{1,0:T(8,128)S(1)} %reduce_sum.9.own_ref.meta_ref, f32[1024,256]{1,0:T(8,128)S(1)} %copy-done, f32[1,1024]{1,0:T(1,128)S(1)} %bitcast.8), custom_call_target="tpu_custom_call" | custom-call | tf_op jit(solution)/shard_map/products/pallas_call | solution.py:543
  41.6 7.0 %all_to_all.23.pay_ref = f32[4,64,128]{2,1,0:T(8,128)S(1)} all-to-all(f32[4,64,128]{2,1,0:T(8,128)S(1)} %get-tuple-element.7), channel_id=1, replica_groups=mesh['dp'=8,'mp'=4] {'mp'}, dimensions={0} | all-to-all | bytes 262144 | tf_op jit(solution)/shard_map/all_to_all | solution.py:555
  48.6 2.2 %update.1 = (f32[32,256]{1,0:T(8,128)}, f32[1024,256]{1,0:T(8,128)}) custom-call(f32[4,64,128]{2,1,0:T(8,128)S(1)} %all_to_all.23.pay_ref, f32[64,256]{1,0:T(8,128)S(1)} %get-tuple-element.8.docs_ref, f32[64,256]{1,0:T(8,128)S(1)} %get-tuple-element.9.near_ref, f32[64,128]{1,0:T(8,128)S(1)} %get-tuple-element.10.info_ref, ...), custom_call_target="tpu_custom_call" | custom-call | tf_op jit(solution)/shard_map/update/pallas_call | solution.py:556
  (1 shorter events, 0.0 us)
Async XLA Ops:
  0.6 40.2 %copy-start = (f32[1024,256]{1,0:T(8,128)S(1)}, f32[1024,256]{1,0:T(8,128)}, u32[]{:S(2)}) copy-start(f32[1024,256]{1,0:T(8,128)} %cent_ref.3) | copy-start | bytes 3145732
  0.6 40.2 %copy-start.1 = (f32[1024]{0:T(1024)S(1)}, f32[1024]{0:T(1024)}, u32[]{:S(2)}) copy-start(f32[1024]{0:T(1024)} %param.18) | copy-start | bytes 12292

commit v5 on v4

--- a/solution.py
+++ b/solution.py
@@ -10,9 +10,9 @@
 
 D = 1024
 HEAD_DIM = 64
-QB = 64
-GROUP = 8
-EXTENTS = (192, 256, 384, 640)
+QB = 128
+GROUP = 4
+EXTENTS = (256, 320, 384, 640)
 LANES = 128
 BF = jnp.bfloat16
 F32 = jnp.float32
@@ -50,14 +50,13 @@
 def row_kernel(
     sizes, ids_hbm, assigned_hbm, gain_hbm, x_hbm, wq_hbm, wk_hbm, wv_hbm, wo_hbm, out_ref,
     ids_ref, ids_sm, assigned_sm, gain_ref, x_ref, w_ref, wo_ref, normed_ref, q_ref, k_ref, v_ref,
-    slot_ref, query_slots_ref, windows_ref, windows_sm, pool_ref, meta_ref, share_ref, scores_ref, raised_ref, small_sems, x_sems, w_sems,
+    slot_ref, query_slots_ref, windows_ref, windows_sm, pool_ref, meta_ref, share_ref, scores_ref, small_sems, x_sems, w_sems,
 ):
     length, tile, slots, capacity, block_rows, dp, mp, width, cents = sizes
     tiles = length // tile
     lane_blocks = length // LANES
     rows = dp * block_rows
-    heads = width // HEAD_DIM
-    halves = width // LANES
+    pairs = width // LANES
     row = lax.axis_index("dp")
     column = lax.axis_index("mp")
 
@@ -72,7 +71,7 @@
         for i in range(tiles)
     ]
     w_copies = [
-        pltpu.make_async_copy(w_hbm, w_ref.at[i], w_sems.at[i])
+        pltpu.make_async_copy(w_hbm, w_ref.at[:, pl.ds(i * width, width)], w_sems.at[i])
         for i, w_hbm in enumerate((wq_hbm, wk_hbm, wv_hbm))
     ] + [pltpu.make_async_copy(wo_hbm, wo_ref, w_sems.at[3])]
     for copy in small_copies + x_copies[:1]:
@@ -87,11 +86,9 @@
 
     ids = ids_ref[...]
     local = ids - row * slots
-    slot_rows = jnp.where(local < 0, slots, local).astype(F32)
-    turned = pltpu.roll(slot_rows, QB, 1)
-    front = iota(slot_rows.shape, 1) < QB
-    query_slots_ref[0] = jnp.where(front, slot_rows, turned)
-    query_slots_ref[1] = jnp.where(front, turned, slot_rows)
+    slot_ids = jnp.where(local < 0, slots, local)
+    slot_rows = slot_ids.astype(F32)
+    query_slots_ref[...] = slot_rows
 
     lane = iota((1, LANES), 1)
     named = jnp.full((1, LANES), -1, jnp.int32)
@@ -102,24 +99,22 @@
     earlier = (wide.T == wide) & (iota((LANES, LANES), 0) < iota((LANES, LANES), 1))
     rank = jnp.sum(earlier.astype(F32), axis=0, keepdims=True)
     goes_to = jnp.where(lane < slots, owner.astype(F32) * block_rows + rank, -1.0)
+    goes = jnp.take_along_axis(jnp.broadcast_to(goes_to, slot_rows.shape), slot_ids, axis=1)
     row_of = iota((rows, LANES), 0)
-    place = (row_of.astype(F32) == goes_to) | (
-        (row_of % block_rows == capacity) & (iota((rows, LANES), 1) == slots)
-    )
-    place = place.astype(F32).astype(BF)
-
-    on_diagonal = iota((LANES, LANES), 0) == iota((LANES, LANES), 1)
-    ones = jnp.ones((LANES, LANES), BF)
-    counts = []
+    continued = (row_of % block_rows == capacity).astype(F32)
+    row_of = row_of.astype(F32)
+    lane_number = iota((8, LANES), 1).astype(F32)
+    counts = jnp.zeros((8, LANES), F32)
     for block in range(lane_blocks):
         here = slice(block * LANES, (block + 1) * LANES)
         slot = slot_rows[block:block + 1, :]
-        diagonal = jnp.where(on_diagonal, slot, 0.0).astype(BF)
-        slot_ref[here, :] = dot(diagonal, ones)
-        member = (iota((LANES, LANES), 0).astype(F32) == slot).astype(F32).astype(BF)
-        counts.append(dot(ones[:8], member, NT))
-        pool_ref[:, here] = dot(place, member).astype(BF)
-    counts = functools.reduce(jnp.add, counts)
+        upright = jnp.broadcast_to(slot, (LANES, LANES)).T
+        slot_ref[here, :] = upright
+        for part in range(0, LANES, 8):
+            counts += (upright[part:part + 8] == lane_number).astype(F32)
+        mine = jnp.where(row_of == goes[block:block + 1, :], 1.0, 0.0)
+        pool_ref[:, here] = jnp.where(slot == slots, continued, mine).astype(BF)
+    counts = jnp.broadcast_to(jnp.sum(counts, axis=0, keepdims=True), (8, LANES))
 
     def order(shape, dim):
         slot = iota(shape, dim)
@@ -135,10 +130,7 @@
         return jnp.sum(jnp.where(mine, values[:1], 0.0), axis=1, keepdims=True)
 
     spot = iota(slot_rows.shape, 1)
-    table = jnp.zeros(slot_rows.shape, F32)
-    for part in range(LANES // QB):
-        table = jnp.where(spot == 2 * part, at_position(starts, part * QB), table)
-        table = jnp.where(spot == 2 * part + 1, at_position(starts + counts, (part + 1) * QB - 1), table)
+    table = jnp.where(spot == 0, at_position(starts, 0), at_position(starts + counts, QB - 1))
     windows_ref[...] = table.astype(jnp.int32)
     windows_copy = pltpu.make_async_copy(windows_ref, windows_sm, small_sems.at[4])
     windows_copy.start()
@@ -169,149 +161,150 @@
             out.append(jnp.broadcast_to(mean, (piece_rows, LANES)))
         return out
 
-    def centre(i, means):
+    def spreads(i, means):
         out = []
         for p in range(pieces):
-            here = slice(p * piece_rows, (p + 1) * piece_rows)
             squares = jnp.zeros((piece_rows, LANES), F32)
             for lanes in lane_slices:
                 centered = piece_of(i, p, lanes) - means[p]
                 squares += centered * centered
-                normed_ref[i % 2, here, lanes] = (centered * gain[:, lanes]).astype(BF)
             variance = jnp.sum(squares, axis=1, keepdims=True) * (1.0 / D)
-            out.append(lax.rsqrt(variance + 1e-05))
-        return jnp.concatenate(out, axis=0)
-
-    def project(i, which, inverse):
+            out.append(jnp.broadcast_to(lax.rsqrt(variance + 1e-05), (piece_rows, LANES)))
+        return out
+
+    def scale(i, means, inverses):
+        for p in range(pieces):
+            here = slice(p * piece_rows, (p + 1) * piece_rows)
+            for lanes in lane_slices:
+                scaled = (piece_of(i, p, lanes) - means[p]) * inverses[p] * gain[:, lanes]
+                normed_ref[i % 2, here, lanes] = scaled.astype(BF)
+
+    def project(i):
         here = slice(i * tile, (i + 1) * tile)
-        if which == 0:
-            inverse = inverse * (math.log2(math.e) / math.sqrt(HEAD_DIM))
-        result = (dot(normed_ref[i % 2], w_ref[which]) * inverse).astype(BF)
-        (q_ref, k_ref, v_ref)[which][here, :] = result
+        result = dot(normed_ref[i % 2], w_ref[...])
+        q_ref[here, :] = (result[:, :width] * (1.0 / math.sqrt(HEAD_DIM))).astype(BF)
+        k_ref[here, :] = result[:, width:2 * width].astype(BF)
+        v_ref[here, :] = result[:, 2 * width:].astype(BF)
 
     tokens_sum = jnp.zeros((rows, width), F32)
-    inverses = {}
-    for i in range(-1, tiles):
-        ahead = i + 1
+    means, inverses = {}, {}
+    for i in range(-2, tiles):
+        ahead = i + 2
         if ahead < tiles:
             x_copies[ahead].wait()
-            means = averages(ahead)
+            means[ahead] = averages(ahead)
         if i == 0:
             for copy in w_copies[:3]:
                 copy.wait()
+        if 0 <= i + 1 < tiles:
+            scale(i + 1, means[i + 1], inverses[i + 1])
         if i >= 0:
-            project(i, 0, inverses[i])
-        if ahead < tiles:
-            inverses[ahead] = centre(ahead, means)
-        if i >= 0:
-            project(i, 1, inverses[i])
-            project(i, 2, inverses[i])
+            project(i)
             here = slice(i * tile, (i + 1) * tile)
             tokens_sum += dot(pool_ref[:, here], x_ref[here, own])
+        if ahead < tiles:
+            inverses[ahead] = spreads(ahead, means[ahead])
     windows_copy.wait()
 
-    def window(block_pair, part):
-        return (windows_sm[block_pair, 2 * part] // 16) * 16, windows_sm[block_pair, 2 * part + 1]
-
-    def all_heads(block):
-        at = pl.multiple_of(block * QB, QB)
-        zero = jnp.zeros((QB, LANES), BF)
-        left = iota((QB, LANES), 1) < HEAD_DIM
-        stacked = []
-        for half in range(halves):
-            piece = q_ref[pl.ds(at, QB), half * LANES:(half + 1) * LANES]
-            for kept in (left, jnp.logical_not(left)):
-                mine = jnp.where(kept, piece, zero)
-                stacked.append(jnp.concatenate([mine if h == half else zero for h in range(halves)], axis=1))
-        return jnp.concatenate(stacked, axis=0)
-
-    head_of_lane = (iota((8, width), 1) // HEAD_DIM) == (iota((8, width), 0) % heads)
-    upper_rows = iota((8, width), 0) < heads
-
-    def key_shares(raised, inverse):
-        upper = inverse.astype(BF).astype(F32)
-        parts = jnp.where(upper_rows, upper, inverse - upper)
-        return dot(jnp.where(head_of_lane, parts, 0.0).astype(BF), raised, NT)
+    def window(block):
+        return (windows_sm[block, 0] // 16) * 16, windows_sm[block, 1]
+
+    low_head = iota((QB, LANES), 1) < HEAD_DIM
+    low_lane = iota((8, LANES), 1) < HEAD_DIM
+
+    def scores_of(block, pair, at, extent):
+        lanes = slice(pair * LANES, (pair + 1) * LANES)
+        both = q_ref[pl.ds(pl.multiple_of(block * QB, QB), QB), lanes]
+        zero = jnp.zeros_like(both)
+        queries = jnp.concatenate(
+            [jnp.where(low_head, both, zero), jnp.where(low_head, zero, both)], axis=0
+        )
+        return dot(k_ref[pl.ds(at, extent), lanes], queries, NT)
+
+    def masked(scores, at, extent, mine):
+        return jnp.where(slot_ref[pl.ds(at, extent), :] == mine, scores, -1e30)
+
+    def by_eights(x):
+        return x.reshape(x.shape[0] // 8, 8, LANES)
+
+    def add_shares(pair, at, extent, first, second):
+        low = jnp.broadcast_to(low_lane[:1], (extent, LANES))
+        sums = [jnp.sum(x, axis=1, keepdims=True) for x in (first, second)]
+        share_ref[pair, pl.ds(at, extent), :] += jnp.where(low, sums[0], sums[1])
 
     def straight(blocks, begins, extent):
-        padded = round_up(extent, LANES)
         step = 64
         ats = [pl.multiple_of(jnp.minimum(begin, length - extent), 16) for begin in begins]
-        halves_of = [slice(half * LANES, (half + 1) * LANES) for half in range(halves)]
-        for i, (block, at) in enumerate(zip(blocks, ats)):
-            scores_ref[i, :extent, :] = dot(k_ref[pl.ds(at, extent), :], all_heads(block), NT)
+        chains = [(block, at, pair) for pair in range(pairs) for block, at in zip(blocks, ats)]
+        sides = (slice(0, LANES), slice(LANES, 2 * LANES))
+        for i, (block, at, pair) in enumerate(chains):
+            scores_ref[i, :extent, :] = scores_of(block, pair, at, extent)
         tops = []
-        for i, (block, at) in enumerate(zip(blocks, ats)):
-            mine = query_slots_ref[i % 2, pl.ds(block // 2, 1), :]
-            top = [jnp.full((8, LANES), -1e30, F32) for _ in range(halves)]
+        for i, (block, at, pair) in enumerate(chains):
+            mine = query_slots_ref[pl.ds(block, 1), :]
+            top = [jnp.full((8, LANES), -1e30, F32) for _ in sides]
             for key in range(0, extent, step):
-                same = slot_ref[pl.ds(at + key, step), :] == mine
-                for half, lanes in enumerate(halves_of):
-                    masked = jnp.where(same, scores_ref[i, key:key + step, lanes], -1e30)
-                    scores_ref[i, key:key + step, lanes] = masked
-                    highest = jnp.max(masked.reshape(step // 8, 8, LANES), axis=0)
-                    top[half] = jnp.maximum(top[half], highest)
+                for side, lanes in enumerate(sides):
+                    kept = masked(scores_ref[i, key:key + step, lanes], at + key, step, mine)
+                    scores_ref[i, key:key + step, lanes] = kept
+                    top[side] = jnp.maximum(top[side], jnp.max(by_eights(kept), axis=0))
             tops.append([jnp.max(t, axis=0, keepdims=True) for t in top])
         inverses = []
-        for i in range(len(blocks)):
-            total = [jnp.zeros((8, LANES), F32) for _ in range(halves)]
+        for i in range(len(chains)):
+            total = [jnp.zeros((8, LANES), F32) for _ in sides]
             for key in range(0, extent, step):
-                for half, lanes in enumerate(halves_of):
-                    raised = jnp.exp2(scores_ref[i, key:key + step, lanes] - tops[i][half])
-                    total[half] += jnp.sum(raised.reshape(step // 8, 8, LANES), axis=0)
-                    raised_ref[i, key:key + step, lanes] = raised.astype(BF)
-            if padded > extent:
-                raised_ref[i, extent:padded, :] = jnp.zeros((padded - extent, width), BF)
-            inverses.append(
-                jnp.concatenate([1.0 / jnp.sum(t, axis=0, keepdims=True) for t in total], axis=1)
-            )
-        for i, at in enumerate(ats):
-            shares = key_shares(raised_ref[i, :padded, :], inverses[i])
-            shares = jnp.concatenate([shares, jnp.zeros((8, LANES), F32)], axis=1)
-            base = pl.multiple_of((at // LANES) * LANES, LANES)
-            share_ref[:, pl.ds(base, padded + LANES)] += pltpu.roll(shares, at % LANES, 1)
+                for side, lanes in enumerate(sides):
+                    raised = jnp.exp(scores_ref[i, key:key + step, lanes] - tops[i][side])
+                    total[side] += jnp.sum(by_eights(raised), axis=0)
+                    scores_ref[i, key:key + step, lanes] = raised
+            inverses.append([1.0 / jnp.sum(t, axis=0, keepdims=True) for t in total])
+        for i, (block, at, pair) in enumerate(chains):
+            for key in range(0, extent, step):
+                weights = [
+                    scores_ref[i, key:key + step, lanes] * inverses[i][side]
+                    for side, lanes in enumerate(sides)
+                ]
+                add_shares(pair, pl.multiple_of(at + key, 16), step, *weights)
 
     def any_length(block):
         chunk = 256
-        begin, end = window(block // 2, block % 2)
+        begin, end = window(block)
         first_chunk = begin // chunk
         end_chunk = (end + chunk - 1) // chunk
-
-        def scores_at(index):
-            at = pl.multiple_of(index * chunk, chunk)
-            scores = dot(k_ref[pl.ds(at, chunk), :], all_heads(block), NT)
-            even = query_slots_ref[0, pl.ds(block // 2, 1), :]
-            odd = query_slots_ref[1, pl.ds(block // 2, 1), :]
-            query_slots = jnp.where(block % 2 == 0, even, odd)
-            same = slot_ref[pl.ds(at, chunk), :] == query_slots
-            masked = [
-                jnp.where(same, scores[:, half * LANES:(half + 1) * LANES], -1e30) for half in range(halves)
-            ]
-            return at, jnp.concatenate(masked, axis=1)
-
-        def forward(index, carry):
-            top, total = carry
-            _, scores = scores_at(index)
-            higher = jnp.maximum(top, jnp.max(scores, axis=0, keepdims=True))
-            raised = jnp.sum(jnp.exp2(scores - higher), axis=0, keepdims=True)
-            return higher, total * jnp.exp2(top - higher) + raised
-
-        top, total = lax.fori_loop(
-            first_chunk, end_chunk, forward,
-            (jnp.full((1, width), -1e30, F32), jnp.zeros((1, width), F32)),
-        )
-        inverse = 1.0 / total
-
-        def again(index, nothing):
-            at, scores = scores_at(index)
-            share_ref[:, pl.ds(at, chunk)] += key_shares(jnp.exp2(scores - top).astype(BF), inverse)
-            return nothing
-
-        lax.fori_loop(first_chunk, end_chunk, again, 0)
+        mine = query_slots_ref[pl.ds(block, 1), :]
+        mine = jnp.concatenate([mine, mine], axis=1)
+        for pair in range(pairs):
+
+            def scores_at(index):
+                at = pl.multiple_of(index * chunk, chunk)
+                keys = slot_ref[pl.ds(at, chunk), :]
+                same = jnp.concatenate([keys, keys], axis=1) == mine
+                return at, jnp.where(same, scores_of(block, pair, at, chunk), -1e30)
+
+            def forward(index, carry):
+                top, total = carry
+                _, scores = scores_at(index)
+                higher = jnp.maximum(top, jnp.max(scores, axis=0, keepdims=True))
+                raised = jnp.sum(jnp.exp(scores - higher), axis=0, keepdims=True)
+                return higher, total * jnp.exp(top - higher) + raised
+
+            top, total = lax.fori_loop(
+                first_chunk, end_chunk, forward,
+                (jnp.full((1, 2 * QB), -1e30, F32), jnp.zeros((1, 2 * QB), F32)),
+            )
+            inverse = 1.0 / total
+
+            def again(index, nothing):
+                at, scores = scores_at(index)
+                weights = jnp.exp(scores - top) * inverse
+                add_shares(pair, at, chunk, weights[:, :QB], weights[:, QB:])
+                return nothing
+
+            lax.fori_loop(first_chunk, end_chunk, again, 0)
 
     def group_step(group, nothing):
         blocks = [group * GROUP + i for i in range(GROUP)]
-        spans = [window(group * (GROUP // 2) + i // 2, i % 2) for i in range(GROUP)]
+        spans = [window(block) for block in blocks]
         begins = [begin for begin, _ in spans]
         widest = functools.reduce(jnp.maximum, [end - begin for begin, end in spans])
         done = jnp.int32(0)
@@ -337,16 +330,14 @@
 
     lax.fori_loop(0, length // QB // GROUP, group_step, 0)
 
-    shares = share_ref[:, :length]
-    pool = pool_ref[...]
-    weighted = jnp.concatenate(
-        [pool * (shares[h:h + 1] + shares[heads + h:heads + h + 1]).astype(BF) for h in range(heads)], axis=0
-    )
-    every = dot(weighted, v_ref[...])
-    lane_head = iota((rows, width), 1) // HEAD_DIM
     context = jnp.zeros((rows, width), F32)
-    for h in range(heads):
-        context = jnp.where(lane_head == h, every[h * rows:(h + 1) * rows], context)
+    for at in range(0, length, tile):
+        here = slice(at, at + tile)
+        weighted = [
+            v_ref[here, pair * LANES:(pair + 1) * LANES].astype(F32) * share_ref[pair, here, :]
+            for pair in range(pairs)
+        ]
+        context += dot(pool_ref[:, here], jnp.concatenate(weighted, axis=1).astype(BF))
     upper = context.astype(BF)
     lower = (context - upper.astype(F32)).astype(BF)
     w_copies[3].wait()
@@ -374,21 +365,20 @@
             pltpu.SMEM((1, slots), jnp.int32),
             pltpu.VMEM((1, D), F32),
             pltpu.VMEM((length, D), BF),
-            pltpu.VMEM((3, D, width), BF),
+            pltpu.VMEM((D, 3 * width), BF),
             pltpu.VMEM((width, D), BF),
             pltpu.VMEM((2, tile, D), BF),
             pltpu.VMEM((length, width), BF),
             pltpu.VMEM((length, width), BF),
             pltpu.VMEM((length, width), BF),
             pltpu.VMEM((length, LANES), F32),
-            pltpu.VMEM((2, length // LANES, LANES), F32),
+            pltpu.VMEM((length // LANES, LANES), F32),
             pltpu.VMEM((length // LANES, LANES), jnp.int32),
             pltpu.SMEM((length // LANES, LANES), jnp.int32),
             pltpu.VMEM((rows, length), BF),
             pltpu.VMEM((8, 2 * LANES), F32),
-            pltpu.VMEM((8, length + 2 * LANES), F32),
-            pltpu.VMEM((GROUP, EXTENTS[-1], width), F32),
-            pltpu.VMEM((GROUP, EXTENTS[-1], width), BF),
+            pltpu.VMEM((width // LANES, length, LANES), F32),
+            pltpu.VMEM((GROUP * width // LANES, EXTENTS[-1], 2 * QB), F32),
             pltpu.SemaphoreType.DMA((5,)),
             pltpu.SemaphoreType.DMA((length // tile,)),
             pltpu.SemaphoreType.DMA((4,)),

time: 51.1 us -> 51.7 us (1.012)
    pallas_call x1, Pallas kernels: 15.5 us -> 16.1 us  [row_sums(): pl.pallas_call(functools.partial(row_kernel, sizes), in_specs=[pl.BlockSp...]
where the time goes in v5:
time: 51.7 us; the launch traced here: 51.2 us
  blocking collectives  31.5 us (61%)
  Pallas kernels  19 us (37%)
  between operations  0.67 us (1%)
    pallas_call x1, Pallas kernels, row_sums(): pl.pallas_call(functools.partial(row_kernel, sizes), in_specs=[pl.BlockSp...  16.1 us
    all_to_all x1, blocking collectives, shards(): here = lax.all_to_all(own, 'dp', split_axis=0, concat_axis=0, tiled=True)  14.2 us
    all_to_all x1, blocking collectives, shards(): lax.all_to_all(partial, 'mp', split_axis=0, concat_axis=0, tiled=True)  10.2 us
    all_to_all x1, blocking collectives, shards(): pay = lax.all_to_all(pay, 'mp', split_axis=0, concat_axis=0, tiled=True)  7.02 us
    pallas_call x1, Pallas kernels, shards(): pl.pallas_call(functools.partial(update_kernel, sizes), out_shape=(jax.Sh...  2.22 us

profile of v5, /device:TPU:0, one launch (start us, length us, event | category | flops | bytes accessed | tf_op | source)
XLA Modules:
  0.0 51.2 jit_solution(5746697331469141181)
XLA Ops:
  0.6 0.0 copy-start
  0.6 0.0 copy-start.1
  0.7 16.1 %row_sums.1 = f32[4,64,256]{2,1,0:T(8,128)} custom-call(s32[16,128]{1,0:T(8,128)} %bitcast.9, s32[1,32]{1,0:T(1,128)} %bitcast.11, f32[1,1024]{1,0:T(1,128)} %bitcast.10, bf16[2048,1024]{1,0:T(8,128)(2,1)} %x_hbm.1, bf16[1024,256]{1,0:T(8,128)(2,1)} %wq_hbm.1, bf16[1024,256]{1,0:T(8,128)(2,1)} %wk_hbm.1, bf16[1024,256]{1,0:T(8,128)(2,1)} %wv_hbm.1, ...), custom_call_target="tpu_custom_call" | custom-call | tf_op jit(solution)/shard_map/row_sums/pallas_call | solution.py:358
  16.7 10.2 %all_to_all.21 = f32[4,64,256]{2,1,0:T(8,128)S(1)} all-to-all(f32[4,64,256]{2,1,0:T(8,128)} %row_sums.1), channel_id=1, replica_groups=mesh['dp'=8,'mp'=4] {'mp'}, dimensions={0} | all-to-all | bytes 524288 | tf_op jit(solution)/shard_map/all_to_all | solution.py:529
  27.0 14.2 %all_to_all.22 = f32[8,8,256]{2,1,0:T(8,128)S(1)} all-to-all(f32[8,8,256]{2,1,0:T(8,128)S(1)} %bitcast.6), channel_id=1, replica_groups=mesh['dp'=8,'mp'=4] {'dp'}, dimensions={0} | all-to-all | bytes 131072 | tf_op jit(solution)/shard_map/all_to_all | solution.py:531
  41.3 0.0 copy-done
  41.3 0.0 copy-done.1
  41.3 0.7 %products.1 = (f32[4,64,128]{2,1,0:T(8,128)S(1)}, f32[64,256]{1,0:T(8,128)S(1)}, f32[64,256]{1,0:T(8,128)S(1)}, f32[64,128]{1,0:T(8,128)S(1)}, f32[64,256]{1,0:T(8,128)S(1)}) custom-call(f32[64,256]{1,0:T(8,128)S(1)} %bitcast.7, f32[64,256]{1,0:T(8,128)S(1)} %reduce_sum.9.own_ref.meta_ref, f32[1024,256]{1,0:T(8,128)S(1)} %copy-done, f32[1,1024]{1,0:T(1,128)S(1)} %bitcast.8), custom_call_target="tpu_custom_call" | custom-call | tf_op jit(solution)/shard_map/products/pallas_call | solution.py:533
  42.0 7.0 %all_to_all.23.pay_ref = f32[4,64,128]{2,1,0:T(8,128)S(1)} all-to-all(f32[4,64,128]{2,1,0:T(8,128)S(1)} %get-tuple-element.7), channel_id=1, replica_groups=mesh['dp'=8,'mp'=4] {'mp'}, dimensions={0} | all-to-all | bytes 262144 | tf_op jit(solution)/shard_map/all_to_all | solution.py:545
  49.0 2.2 %update.1 = (f32[32,256]{1,0:T(8,128)}, f32[1024,256]{1,0:T(8,128)}) custom-call(f32[4,64,128]{2,1,0:T(8,128)S(1)} %all_to_all.23.pay_ref, f32[64,256]{1,0:T(8,128)S(1)} %get-tuple-element.8.docs_ref, f32[64,256]{1,0:T(8,128)S(1)} %get-tuple-element.9.near_ref, f32[64,128]{1,0:T(8,128)S(1)} %get-tuple-element.10.info_ref, ...), custom_call_target="tpu_custom_call" | custom-call | tf_op jit(solution)/shard_map/update/pallas_call | solution.py:546
  (1 shorter events, 0.0 us)
Async XLA Ops:
  0.6 40.6 %copy-start = (f32[1024,256]{1,0:T(8,128)S(1)}, f32[1024,256]{1,0:T(8,128)}, u32[]{:S(2)}) copy-start(f32[1024,256]{1,0:T(8,128)} %cent_ref.3) | copy-start | bytes 3145732
  0.6 40.6 %copy-start.1 = (f32[1024]{0:T(1024)S(1)}, f32[1024]{0:T(1024)}, u32[]{:S(2)}) copy-start(f32[1024]{0:T(1024)} %param.18) | copy-start | bytes 12292

commit v6 on v4

--- a/solution.py
+++ b/solution.py
@@ -87,7 +87,8 @@
 
     ids = ids_ref[...]
     local = ids - row * slots
-    slot_rows = jnp.where(local < 0, slots, local).astype(F32)
+    slot_ids = jnp.where(local < 0, slots, local)
+    slot_rows = slot_ids.astype(F32)
     turned = pltpu.roll(slot_rows, QB, 1)
     front = iota(slot_rows.shape, 1) < QB
     query_slots_ref[0] = jnp.where(front, slot_rows, turned)
@@ -102,24 +103,22 @@
     earlier = (wide.T == wide) & (iota((LANES, LANES), 0) < iota((LANES, LANES), 1))
     rank = jnp.sum(earlier.astype(F32), axis=0, keepdims=True)
     goes_to = jnp.where(lane < slots, owner.astype(F32) * block_rows + rank, -1.0)
+    goes = jnp.take_along_axis(jnp.broadcast_to(goes_to, slot_rows.shape), slot_ids, axis=1)
     row_of = iota((rows, LANES), 0)
-    place = (row_of.astype(F32) == goes_to) | (
-        (row_of % block_rows == capacity) & (iota((rows, LANES), 1) == slots)
-    )
-    place = place.astype(F32).astype(BF)
-
-    on_diagonal = iota((LANES, LANES), 0) == iota((LANES, LANES), 1)
-    ones = jnp.ones((LANES, LANES), BF)
-    counts = []
+    continued = (row_of % block_rows == capacity).astype(F32)
+    row_of = row_of.astype(F32)
+    lane_number = iota((8, LANES), 1).astype(F32)
+    counts = jnp.zeros((8, LANES), F32)
     for block in range(lane_blocks):
         here = slice(block * LANES, (block + 1) * LANES)
         slot = slot_rows[block:block + 1, :]
-        diagonal = jnp.where(on_diagonal, slot, 0.0).astype(BF)
-        slot_ref[here, :] = dot(diagonal, ones)
-        member = (iota((LANES, LANES), 0).astype(F32) == slot).astype(F32).astype(BF)
-        counts.append(dot(ones[:8], member, NT))
-        pool_ref[:, here] = dot(place, member).astype(BF)
-    counts = functools.reduce(jnp.add, counts)
+        upright = jnp.broadcast_to(slot, (LANES, LANES)).T
+        slot_ref[here, :] = upright
+        for part in range(0, LANES, 8):
+            counts += (upright[part:part + 8] == lane_number).astype(F32)
+        mine = jnp.where(row_of == goes[block:block + 1, :], 1.0, 0.0)
+        pool_ref[:, here] = jnp.where(slot == slots, continued, mine).astype(BF)
+    counts = jnp.broadcast_to(jnp.sum(counts, axis=0, keepdims=True), (8, LANES))
 
     def order(shape, dim):
         slot = iota(shape, dim)
@@ -161,53 +160,48 @@
         at = i * tile + p * piece_rows
         return x_ref[at:at + piece_rows, lanes].astype(F32)
 
-    def averages(i):
-        out = []
-        for p in range(pieces):
+    def normalise(i, group):
+        means, inverses = [], []
+        for p in group:
             total = functools.reduce(jnp.add, [piece_of(i, p, lanes) for lanes in lane_slices])
             mean = jnp.sum(total, axis=1, keepdims=True) * (1.0 / D)
-            out.append(jnp.broadcast_to(mean, (piece_rows, LANES)))
-        return out
-
-    def centre(i, means):
-        out = []
-        for p in range(pieces):
-            here = slice(p * piece_rows, (p + 1) * piece_rows)
+            means.append(jnp.broadcast_to(mean, (piece_rows, LANES)))
+        for p, mean in zip(group, means):
             squares = jnp.zeros((piece_rows, LANES), F32)
             for lanes in lane_slices:
-                centered = piece_of(i, p, lanes) - means[p]
+                centered = piece_of(i, p, lanes) - mean
                 squares += centered * centered
-                normed_ref[i % 2, here, lanes] = (centered * gain[:, lanes]).astype(BF)
             variance = jnp.sum(squares, axis=1, keepdims=True) * (1.0 / D)
-            out.append(lax.rsqrt(variance + 1e-05))
-        return jnp.concatenate(out, axis=0)
-
-    def project(i, which, inverse):
+            inverses.append(jnp.broadcast_to(lax.rsqrt(variance + 1e-05), (piece_rows, LANES)))
+        for p, mean, inverse in zip(group, means, inverses):
+            here = slice(p * piece_rows, (p + 1) * piece_rows)
+            for lanes in lane_slices:
+                scaled = (piece_of(i, p, lanes) - mean) * inverse * gain[:, lanes]
+                normed_ref[i % 2, here, lanes] = scaled.astype(BF)
+
+    def project(i, which):
         here = slice(i * tile, (i + 1) * tile)
+        result = dot(normed_ref[i % 2], w_ref[which])
         if which == 0:
-            inverse = inverse * (math.log2(math.e) / math.sqrt(HEAD_DIM))
-        result = (dot(normed_ref[i % 2], w_ref[which]) * inverse).astype(BF)
-        (q_ref, k_ref, v_ref)[which][here, :] = result
-
+            result = result * (1.0 / math.sqrt(HEAD_DIM))
+        (q_ref, k_ref, v_ref)[which][here, :] = result.astype(BF)
+
+    groups = [range(pieces * g // 3, pieces * (g + 1) // 3) for g in range(3)]
     tokens_sum = jnp.zeros((rows, width), F32)
-    inverses = {}
-    for i in range(-1, tiles):
-        ahead = i + 1
-        if ahead < tiles:
-            x_copies[ahead].wait()
-            means = averages(ahead)
-        if i == 0:
-            for copy in w_copies[:3]:
-                copy.wait()
-        if i >= 0:
-            project(i, 0, inverses[i])
-        if ahead < tiles:
-            inverses[ahead] = centre(ahead, means)
-        if i >= 0:
-            project(i, 1, inverses[i])
-            project(i, 2, inverses[i])
-            here = slice(i * tile, (i + 1) * tile)
-            tokens_sum += dot(pool_ref[:, here], x_ref[here, own])
+    x_copies[0].wait()
+    for group in groups:
+        normalise(0, group)
+    for copy in w_copies[:3]:
+        copy.wait()
+    for i in range(tiles):
+        if i + 1 < tiles:
+            x_copies[i + 1].wait()
+        for which, group in enumerate(groups):
+            if i + 1 < tiles:
+                normalise(i + 1, group)
+            project(i, which)
+        here = slice(i * tile, (i + 1) * tile)
+        tokens_sum += dot(pool_ref[:, here], x_ref[here, own])
     windows_copy.wait()
 
     def window(block_pair, part):
@@ -257,7 +251,7 @@
             total = [jnp.zeros((8, LANES), F32) for _ in range(halves)]
             for key in range(0, extent, step):
                 for half, lanes in enumerate(halves_of):
-                    raised = jnp.exp2(scores_ref[i, key:key + step, lanes] - tops[i][half])
+                    raised = jnp.exp(scores_ref[i, key:key + step, lanes] - tops[i][half])
                     total[half] += jnp.sum(raised.reshape(step // 8, 8, LANES), axis=0)
                     raised_ref[i, key:key + step, lanes] = raised.astype(BF)
             if padded > extent:
@@ -293,8 +287,8 @@
             top, total = carry
             _, scores = scores_at(index)
             higher = jnp.maximum(top, jnp.max(scores, axis=0, keepdims=True))
-            raised = jnp.sum(jnp.exp2(scores - higher), axis=0, keepdims=True)
-            return higher, total * jnp.exp2(top - higher) + raised
+            raised = jnp.sum(jnp.exp(scores - higher), axis=0, keepdims=True)
+            return higher, total * jnp.exp(top - higher) + raised
 
         top, total = lax.fori_loop(
             first_chunk, end_chunk, forward,
@@ -304,7 +298,7 @@
 
         def again(index, nothing):
             at, scores = scores_at(index)
-            share_ref[:, pl.ds(at, chunk)] += key_shares(jnp.exp2(scores - top).astype(BF), inverse)
+            share_ref[:, pl.ds(at, chunk)] += key_shares(jnp.exp(scores - top).astype(BF), inverse)
             return nothing
 
         lax.fori_loop(first_chunk, end_chunk, again, 0)
@@ -532,7 +526,7 @@
     capacity = max(2, (slots + dp - 2) // (dp - 1))
     block_rows = round_up(capacity + 3, 8)
     rows = dp * block_rows
-    sizes = (length, min(256, length), slots, capacity, block_rows, dp, mp, width, cents)
+    sizes = (length, min(512, length), slots, capacity, block_rows, dp, mp, width, cents)
     limit = pltpu.CompilerParams(vmem_limit_bytes=48 * 1024 * 1024)
 
     partial = row_sums(doc_ids, assigned, tokens, ln_gain, w_query, w_key, w_value, w_out, sizes)

time: 51.1 us -> 50.2 us (0.982); the launches traced: 50.8 us -> 50.9 us
  blocking collectives: 31.6 us -> 32.4 us
  Pallas kernels: 18.5 us -> 17.8 us
    all_to_all x1, blocking collectives: 14.3 us -> 15.1 us  [shards(): here = lax.all_to_all(own, 'dp', split_axis=0, concat_axis=0, tiled=True)]
    pallas_call x1, Pallas kernels: 15.5 us -> 14.8 us  [row_sums(): pl.pallas_call(functools.partial(row_kernel, sizes), in_specs=[pl.BlockSp...]
where the time goes in v6:
time: 50.2 us; the launch traced here: 50.9 us
  blocking collectives  32.4 us (65%)
  Pallas kernels  17.8 us (35%)
  between operations  0.67 us (1%)
    all_to_all x1, blocking collectives, shards(): here = lax.all_to_all(own, 'dp', split_axis=0, concat_axis=0, tiled=True)  15.1 us
    pallas_call x1, Pallas kernels, row_sums(): pl.pallas_call(functools.partial(row_kernel, sizes), in_specs=[pl.BlockSp...  14.8 us
    all_to_all x1, blocking collectives, shards(): lax.all_to_all(partial, 'mp', split_axis=0, concat_axis=0, tiled=True)  10.3 us
    all_to_all x1, blocking collectives, shards(): pay = lax.all_to_all(pay, 'mp', split_axis=0, concat_axis=0, tiled=True)  7.02 us
    pallas_call x1, Pallas kernels, shards(): pl.pallas_call(functools.partial(update_kernel, sizes), out_shape=(jax.Sh...  2.22 us

profile of v6, /device:TPU:0, one launch (start us, length us, event | category | flops | bytes accessed | tf_op | source)
XLA Modules:
  0.0 50.9 jit_solution(17534921735283827568)
XLA Ops:
  0.6 0.0 copy-start
  0.6 0.0 copy-start.1
  0.7 14.8 %row_sums.1 = f32[4,64,256]{2,1,0:T(8,128)} custom-call(s32[16,128]{1,0:T(8,128)} %bitcast.9, s32[1,32]{1,0:T(1,128)} %bitcast.11, f32[1,1024]{1,0:T(1,128)} %bitcast.10, bf16[2048,1024]{1,0:T(8,128)(2,1)} %x_hbm.1, bf16[1024,256]{1,0:T(8,128)(2,1)} %wq_hbm.1, bf16[1024,256]{1,0:T(8,128)(2,1)} %wk_hbm.1, bf16[1024,256]{1,0:T(8,128)(2,1)} %wv_hbm.1, ...), custom_call_target="tpu_custom_call" | custom-call | tf_op jit(solution)/shard_map/row_sums/pallas_call | solution.py:361
  15.5 10.3 %all_to_all.21 = f32[4,64,256]{2,1,0:T(8,128)S(1)} all-to-all(f32[4,64,256]{2,1,0:T(8,128)} %row_sums.1), channel_id=1, replica_groups=mesh['dp'=8,'mp'=4] {'mp'}, dimensions={0} | all-to-all | bytes 524288 | tf_op jit(solution)/shard_map/all_to_all | solution.py:533
  25.8 15.1 %all_to_all.22 = f32[8,8,256]{2,1,0:T(8,128)S(1)} all-to-all(f32[8,8,256]{2,1,0:T(8,128)S(1)} %bitcast.6), channel_id=1, replica_groups=mesh['dp'=8,'mp'=4] {'dp'}, dimensions={0} | all-to-all | bytes 131072 | tf_op jit(solution)/shard_map/all_to_all | solution.py:535
  40.9 0.0 copy-done
  40.9 0.0 copy-done.1
  40.9 0.7 %products.1 = (f32[4,64,128]{2,1,0:T(8,128)S(1)}, f32[64,256]{1,0:T(8,128)S(1)}, f32[64,256]{1,0:T(8,128)S(1)}, f32[64,128]{1,0:T(8,128)S(1)}, f32[64,256]{1,0:T(8,128)S(1)}) custom-call(f32[64,256]{1,0:T(8,128)S(1)} %bitcast.7, f32[64,256]{1,0:T(8,128)S(1)} %reduce_sum.9.own_ref.meta_ref, f32[1024,256]{1,0:T(8,128)S(1)} %copy-done, f32[1,1024]{1,0:T(1,128)S(1)} %bitcast.8), custom_call_target="tpu_custom_call" | custom-call | tf_op jit(solution)/shard_map/products/pallas_call | solution.py:537
  41.6 7.0 %all_to_all.23.pay_ref = f32[4,64,128]{2,1,0:T(8,128)S(1)} all-to-all(f32[4,64,128]{2,1,0:T(8,128)S(1)} %get-tuple-element.7), channel_id=1, replica_groups=mesh['dp'=8,'mp'=4] {'mp'}, dimensions={0} | all-to-all | bytes 262144 | tf_op jit(solution)/shard_map/all_to_all | solution.py:549
  48.6 2.2 %update.1 = (f32[32,256]{1,0:T(8,128)}, f32[1024,256]{1,0:T(8,128)}) custom-call(f32[4,64,128]{2,1,0:T(8,128)S(1)} %all_to_all.23.pay_ref, f32[64,256]{1,0:T(8,128)S(1)} %get-tuple-element.8.docs_ref, f32[64,256]{1,0:T(8,128)S(1)} %get-tuple-element.9.near_ref, f32[64,128]{1,0:T(8,128)S(1)} %get-tuple-element.10.info_ref, ...), custom_call_target="tpu_custom_call" | custom-call | tf_op jit(solution)/shard_map/update/pallas_call | solution.py:550
  (1 shorter events, 0.0 us)
Async XLA Ops:
  0.6 40.2 %copy-start = (f32[1024,256]{1,0:T(8,128)S(1)}, f32[1024,256]{1,0:T(8,128)}, u32[]{:S(2)}) copy-start(f32[1024,256]{1,0:T(8,128)} %cent_ref.3) | copy-start | bytes 3145732
  0.6 40.2 %copy-start.1 = (f32[1024]{0:T(1024)S(1)}, f32[1024]{0:T(1024)}, u32[]{:S(2)}) copy-start(f32[1024]{0:T(1024)} %param.18) | copy-start | bytes 12292

commit v7 on v6

--- a/solution.py
+++ b/solution.py
@@ -12,7 +12,7 @@
 HEAD_DIM = 64
 QB = 64
 GROUP = 8
-EXTENTS = (192, 256, 384, 640)
+EXTENTS = (192, 256, 320, 384, 512, 640)
 LANES = 128
 BF = jnp.bfloat16
 F32 = jnp.float32
@@ -53,7 +53,10 @@
     slot_ref, query_slots_ref, windows_ref, windows_sm, pool_ref, meta_ref, share_ref, scores_ref, raised_ref, small_sems, x_sems, w_sems,
 ):
     length, tile, slots, capacity, block_rows, dp, mp, width, cents = sizes
-    tiles = length // tile
+    small = tile // 2
+    sizes_of = [small] + [tile] * (length // tile - 1) + [small]
+    begins_of = [sum(sizes_of[:i]) for i in range(len(sizes_of))]
+    tiles = len(sizes_of)
     lane_blocks = length // LANES
     rows = dp * block_rows
     heads = width // HEAD_DIM
@@ -68,8 +71,8 @@
         pltpu.make_async_copy(gain_hbm, gain_ref, small_sems.at[3]),
     ]
     x_copies = [
-        pltpu.make_async_copy(x_hbm.at[pl.ds(i * tile, tile), :], x_ref.at[pl.ds(i * tile, tile), :], x_sems.at[i])
-        for i in range(tiles)
+        pltpu.make_async_copy(x_hbm.at[pl.ds(at, size), :], x_ref.at[pl.ds(at, size), :], x_sems.at[i])
+        for i, (at, size) in enumerate(zip(begins_of, sizes_of))
     ]
     w_copies = [
         pltpu.make_async_copy(w_hbm, w_ref.at[i], w_sems.at[i])
@@ -153,11 +156,10 @@
     own = pl.ds(pl.multiple_of(column * width, width), width)
     gain = gain_ref[...]
     piece_rows = 64
-    pieces = tile // piece_rows
     lane_slices = [slice(j * LANES, (j + 1) * LANES) for j in range(D // LANES)]
 
     def piece_of(i, p, lanes):
-        at = i * tile + p * piece_rows
+        at = begins_of[i] + p * piece_rows
         return x_ref[at:at + piece_rows, lanes].astype(F32)
 
     def normalise(i, group):
@@ -180,27 +182,29 @@
                 normed_ref[i % 2, here, lanes] = scaled.astype(BF)
 
     def project(i, which):
-        here = slice(i * tile, (i + 1) * tile)
-        result = dot(normed_ref[i % 2], w_ref[which])
+        here = slice(begins_of[i], begins_of[i] + sizes_of[i])
+        result = dot(normed_ref[i % 2, :sizes_of[i], :], w_ref[which])
         if which == 0:
             result = result * (1.0 / math.sqrt(HEAD_DIM))
         (q_ref, k_ref, v_ref)[which][here, :] = result.astype(BF)
 
-    groups = [range(pieces * g // 3, pieces * (g + 1) // 3) for g in range(3)]
+    def groups(i):
+        pieces = sizes_of[i] // piece_rows
+        return [range(pieces * g // 3, pieces * (g + 1) // 3) for g in range(3)]
+
     tokens_sum = jnp.zeros((rows, width), F32)
     x_copies[0].wait()
-    for group in groups:
-        normalise(0, group)
+    normalise(0, range(sizes_of[0] // piece_rows))
     for copy in w_copies[:3]:
         copy.wait()
     for i in range(tiles):
         if i + 1 < tiles:
             x_copies[i + 1].wait()
-        for which, group in enumerate(groups):
+        for which in range(3):
             if i + 1 < tiles:
-                normalise(i + 1, group)
+                normalise(i + 1, groups(i + 1)[which])
             project(i, which)
-        here = slice(i * tile, (i + 1) * tile)
+        here = slice(begins_of[i], begins_of[i] + sizes_of[i])
         tokens_sum += dot(pool_ref[:, here], x_ref[here, own])
     windows_copy.wait()
 
@@ -232,22 +236,24 @@
         step = 64
         ats = [pl.multiple_of(jnp.minimum(begin, length - extent), 16) for begin in begins]
         halves_of = [slice(half * LANES, (half + 1) * LANES) for half in range(halves)]
-        for i, (block, at) in enumerate(zip(blocks, ats)):
-            scores_ref[i, :extent, :] = dot(k_ref[pl.ds(at, extent), :], all_heads(block), NT)
-        tops = []
-        for i, (block, at) in enumerate(zip(blocks, ats)):
-            mine = query_slots_ref[i % 2, pl.ds(block // 2, 1), :]
+        tops, inverses = {}, {}
+
+        def score(i):
+            scores_ref[i, :extent, :] = dot(k_ref[pl.ds(ats[i], extent), :], all_heads(blocks[i]), NT)
+
+        def mask(i):
+            mine = query_slots_ref[i % 2, pl.ds(blocks[i] // 2, 1), :]
             top = [jnp.full((8, LANES), -1e30, F32) for _ in range(halves)]
             for key in range(0, extent, step):
-                same = slot_ref[pl.ds(at + key, step), :] == mine
+                same = slot_ref[pl.ds(ats[i] + key, step), :] == mine
                 for half, lanes in enumerate(halves_of):
                     masked = jnp.where(same, scores_ref[i, key:key + step, lanes], -1e30)
                     scores_ref[i, key:key + step, lanes] = masked
                     highest = jnp.max(masked.reshape(step // 8, 8, LANES), axis=0)
                     top[half] = jnp.maximum(top[half], highest)
-            tops.append([jnp.max(t, axis=0, keepdims=True) for t in top])
-        inverses = []
-        for i in range(len(blocks)):
+            tops[i] = [jnp.max(t, axis=0, keepdims=True) for t in top]
+
+        def raise_all(i):
             total = [jnp.zeros((8, LANES), F32) for _ in range(halves)]
             for key in range(0, extent, step):
                 for half, lanes in enumerate(halves_of):
@@ -256,14 +262,22 @@
                     raised_ref[i, key:key + step, lanes] = raised.astype(BF)
             if padded > extent:
                 raised_ref[i, extent:padded, :] = jnp.zeros((padded - extent, width), BF)
-            inverses.append(
-                jnp.concatenate([1.0 / jnp.sum(t, axis=0, keepdims=True) for t in total], axis=1)
+            inverses[i] = jnp.concatenate(
+                [1.0 / jnp.sum(t, axis=0, keepdims=True) for t in total], axis=1
             )
-        for i, at in enumerate(ats):
+
+        def share(i):
             shares = key_shares(raised_ref[i, :padded, :], inverses[i])
             shares = jnp.concatenate([shares, jnp.zeros((8, LANES), F32)], axis=1)
-            base = pl.multiple_of((at // LANES) * LANES, LANES)
-            share_ref[:, pl.ds(base, padded + LANES)] += pltpu.roll(shares, at % LANES, 1)
+            base = pl.multiple_of((ats[i] // LANES) * LANES, LANES)
+            share_ref[:, pl.ds(base, padded + LANES)] += pltpu.roll(shares, ats[i] % LANES, 1)
+
+        stages = (score, mask, raise_all, share)
+        behind = (0, 2, 3, 5)
+        for turn in range(len(blocks) + behind[-1]):
+            for stage, late in zip(stages, behind):
+                if 0 <= turn - late < len(blocks):
+                    stage(turn - late)
 
     def any_length(block):
         chunk = 256
@@ -384,7 +398,7 @@
             pltpu.VMEM((GROUP, EXTENTS[-1], width), F32),
             pltpu.VMEM((GROUP, EXTENTS[-1], width), BF),
             pltpu.SemaphoreType.DMA((5,)),
-            pltpu.SemaphoreType.DMA((length // tile,)),
+            pltpu.SemaphoreType.DMA((length // tile + 1,)),
             pltpu.SemaphoreType.DMA((4,)),
         ],
         compiler_params=pltpu.CompilerParams(vmem_limit_bytes=62 * 1024 * 1024),

time: 50.2 us -> 51.2 us (1.020); the launches traced: 50.9 us -> 51.3 us
  Pallas kernels: 17.8 us -> 18.5 us
    pallas_call x1, Pallas kernels: 14.8 us -> 15.5 us  [row_sums(): pl.pallas_call(functools.partial(row_kernel, sizes), in_specs=[pl.BlockSp...]
where the time goes in v7:
time: 51.2 us; the launch traced here: 51.3 us
  blocking collectives  32.2 us (63%)
  Pallas kernels  18.5 us (36%)
  between operations  0.67 us (1%)
    pallas_call x1, Pallas kernels, row_sums(): pl.pallas_call(functools.partial(row_kernel, sizes), in_specs=[pl.BlockSp...  15.5 us
    all_to_all x1, blocking collectives, shards(): here = lax.all_to_all(own, 'dp', split_axis=0, concat_axis=0, tiled=True)  14.9 us
    all_to_all x1, blocking collectives, shards(): lax.all_to_all(partial, 'mp', split_axis=0, concat_axis=0, tiled=True)  10.3 us
    all_to_all x1, blocking collectives, shards(): pay = lax.all_to_all(pay, 'mp', split_axis=0, concat_axis=0, tiled=True)  7.02 us
    pallas_call x1, Pallas kernels, shards(): pl.pallas_call(functools.partial(update_kernel, sizes), out_shape=(jax.Sh...  2.22 us

profile of v7, /device:TPU:0, one launch (start us, length us, event | category | flops | bytes accessed | tf_op | source)
XLA Modules:
  0.0 51.3 jit_solution(99593172526346497)
XLA Ops:
  0.6 0.0 copy-start
  0.6 0.0 copy-start.1
  0.7 15.5 %row_sums.1 = f32[4,64,256]{2,1,0:T(8,128)} custom-call(s32[16,128]{1,0:T(8,128)} %bitcast.9, s32[1,32]{1,0:T(1,128)} %bitcast.11, f32[1,1024]{1,0:T(1,128)} %bitcast.10, bf16[2048,1024]{1,0:T(8,128)(2,1)} %x_hbm.1, bf16[1024,256]{1,0:T(8,128)(2,1)} %wq_hbm.1, bf16[1024,256]{1,0:T(8,128)(2,1)} %wk_hbm.1, bf16[1024,256]{1,0:T(8,128)(2,1)} %wv_hbm.1, ...), custom_call_target="tpu_custom_call" | custom-call | tf_op jit(solution)/shard_map/row_sums/pallas_call | solution.py:375
  16.2 10.3 %all_to_all.21 = f32[4,64,256]{2,1,0:T(8,128)S(1)} all-to-all(f32[4,64,256]{2,1,0:T(8,128)} %row_sums.1), channel_id=1, replica_groups=mesh['dp'=8,'mp'=4] {'mp'}, dimensions={0} | all-to-all | bytes 524288 | tf_op jit(solution)/shard_map/all_to_all | solution.py:547
  26.4 14.9 %all_to_all.22 = f32[8,8,256]{2,1,0:T(8,128)S(1)} all-to-all(f32[8,8,256]{2,1,0:T(8,128)S(1)} %bitcast.6), channel_id=1, replica_groups=mesh['dp'=8,'mp'=4] {'dp'}, dimensions={0} | all-to-all | bytes 131072 | tf_op jit(solution)/shard_map/all_to_all | solution.py:549
  41.3 0.0 copy-done
  41.3 0.0 copy-done.1
  41.3 0.7 %products.1 = (f32[4,64,128]{2,1,0:T(8,128)S(1)}, f32[64,256]{1,0:T(8,128)S(1)}, f32[64,256]{1,0:T(8,128)S(1)}, f32[64,128]{1,0:T(8,128)S(1)}, f32[64,256]{1,0:T(8,128)S(1)}) custom-call(f32[64,256]{1,0:T(8,128)S(1)} %bitcast.7, f32[64,256]{1,0:T(8,128)S(1)} %reduce_sum.9.own_ref.meta_ref, f32[1024,256]{1,0:T(8,128)S(1)} %copy-done, f32[1,1024]{1,0:T(1,128)S(1)} %bitcast.8), custom_call_target="tpu_custom_call" | custom-call | tf_op jit(solution)/shard_map/products/pallas_call | solution.py:551
  42.1 7.0 %all_to_all.23.pay_ref = f32[4,64,128]{2,1,0:T(8,128)S(1)} all-to-all(f32[4,64,128]{2,1,0:T(8,128)S(1)} %get-tuple-element.7), channel_id=1, replica_groups=mesh['dp'=8,'mp'=4] {'mp'}, dimensions={0} | all-to-all | bytes 262144 | tf_op jit(solution)/shard_map/all_to_all | solution.py:563
  49.1 2.2 %update.1 = (f32[32,256]{1,0:T(8,128)}, f32[1024,256]{1,0:T(8,128)}) custom-call(f32[4,64,128]{2,1,0:T(8,128)S(1)} %all_to_all.23.pay_ref, f32[64,256]{1,0:T(8,128)S(1)} %get-tuple-element.8.docs_ref, f32[64,256]{1,0:T(8,128)S(1)} %get-tuple-element.9.near_ref, f32[64,128]{1,0:T(8,128)S(1)} %get-tuple-element.10.info_ref, ...), custom_call_target="tpu_custom_call" | custom-call | tf_op jit(solution)/shard_map/update/pallas_call | solution.py:564
  (1 shorter events, 0.0 us)
Async XLA Ops:
  0.6 40.7 %copy-start = (f32[1024,256]{1,0:T(8,128)S(1)}, f32[1024,256]{1,0:T(8,128)}, u32[]{:S(2)}) copy-start(f32[1024,256]{1,0:T(8,128)} %cent_ref.3) | copy-start | bytes 3145732
  0.6 40.7 %copy-start.1 = (f32[1024]{0:T(1024)S(1)}, f32[1024]{0:T(1024)}, u32[]{:S(2)}) copy-start(f32[1024]{0:T(1024)} %param.18) | copy-start | bytes 12292

commit v8 on v6

--- a/solution.py
+++ b/solution.py
@@ -12,7 +12,7 @@
 HEAD_DIM = 64
 QB = 64
 GROUP = 8
-EXTENTS = (192, 256, 384, 640)
+EXTENTS = (192, 256, 320, 384, 512, 640)
 LANES = 128
 BF = jnp.bfloat16
 F32 = jnp.float32
@@ -67,19 +67,20 @@
         pltpu.make_async_copy(assigned_hbm, assigned_sm, small_sems.at[2]),
         pltpu.make_async_copy(gain_hbm, gain_ref, small_sems.at[3]),
     ]
+    part_rows = tile // 4
     x_copies = [
-        pltpu.make_async_copy(x_hbm.at[pl.ds(i * tile, tile), :], x_ref.at[pl.ds(i * tile, tile), :], x_sems.at[i])
-        for i in range(tiles)
+        pltpu.make_async_copy(x_hbm.at[pl.ds(at, part_rows), :], x_ref.at[pl.ds(at, part_rows), :], x_sems.at[i])
+        for i, at in enumerate(range(0, length, part_rows))
     ]
     w_copies = [
         pltpu.make_async_copy(w_hbm, w_ref.at[i], w_sems.at[i])
         for i, w_hbm in enumerate((wq_hbm, wk_hbm, wv_hbm))
     ] + [pltpu.make_async_copy(wo_hbm, wo_ref, w_sems.at[3])]
-    for copy in small_copies + x_copies[:1]:
+    for copy in small_copies + x_copies[:4]:
         copy.start()
     for copy in w_copies[:3]:
         copy.start(priority=1)
-    for copy in x_copies[1:]:
+    for copy in x_copies[4:]:
         copy.start()
     w_copies[3].start(priority=1)
     for copy in small_copies:
@@ -188,14 +189,15 @@
 
     groups = [range(pieces * g // 3, pieces * (g + 1) // 3) for g in range(3)]
     tokens_sum = jnp.zeros((rows, width), F32)
-    x_copies[0].wait()
-    for group in groups:
-        normalise(0, group)
+    for quarter in range(4):
+        x_copies[quarter].wait()
+        normalise(0, range(pieces * quarter // 4, pieces * (quarter + 1) // 4))
     for copy in w_copies[:3]:
         copy.wait()
     for i in range(tiles):
         if i + 1 < tiles:
-            x_copies[i + 1].wait()
+            for quarter in range(4):
+                x_copies[4 * (i + 1) + quarter].wait()
         for which, group in enumerate(groups):
             if i + 1 < tiles:
                 normalise(i + 1, group)
@@ -384,7 +386,7 @@
             pltpu.VMEM((GROUP, EXTENTS[-1], width), F32),
             pltpu.VMEM((GROUP, EXTENTS[-1], width), BF),
             pltpu.SemaphoreType.DMA((5,)),
-            pltpu.SemaphoreType.DMA((length // tile,)),
+            pltpu.SemaphoreType.DMA((4 * length // tile,)),
             pltpu.SemaphoreType.DMA((4,)),
         ],
         compiler_params=pltpu.CompilerParams(vmem_limit_bytes=62 * 1024 * 1024),
@@ -526,7 +528,7 @@
     capacity = max(2, (slots + dp - 2) // (dp - 1))
     block_rows = round_up(capacity + 3, 8)
     rows = dp * block_rows
-    sizes = (length, min(512, length), slots, capacity, block_rows, dp, mp, width, cents)
+    sizes = (length, min(1024, length), slots, capacity, block_rows, dp, mp, width, cents)
     limit = pltpu.CompilerParams(vmem_limit_bytes=48 * 1024 * 1024)
 
     partial = row_sums(doc_ids, assigned, tokens, ln_gain, w_query, w_key, w_value, w_out, sizes)

time: 50.2 us -> 50.6 us (level)
  no operation moved by 1% of the time
where the time goes in v8:
time: 50.6 us; the launch traced here: 51.2 us
  blocking collectives  32.9 us (65%)
  Pallas kernels  17.6 us (35%)
  between operations  0.67 us (1%)
    all_to_all x1, blocking collectives, shards(): here = lax.all_to_all(own, 'dp', split_axis=0, concat_axis=0, tiled=True)  15.6 us
    pallas_call x1, Pallas kernels, row_sums(): pl.pallas_call(functools.partial(row_kernel, sizes), in_specs=[pl.BlockSp...  14.7 us
    all_to_all x1, blocking collectives, shards(): lax.all_to_all(partial, 'mp', split_axis=0, concat_axis=0, tiled=True)  10.3 us
    all_to_all x1, blocking collectives, shards(): pay = lax.all_to_all(pay, 'mp', split_axis=0, concat_axis=0, tiled=True)  7.02 us
    pallas_call x1, Pallas kernels, shards(): pl.pallas_call(functools.partial(update_kernel, sizes), out_shape=(jax.Sh...  2.22 us

profile of v8, /device:TPU:0, one launch (start us, length us, event | category | flops | bytes accessed | tf_op | source)
XLA Modules:
  0.0 51.2 jit_solution(15021520369376387245)
XLA Ops:
  0.6 0.0 copy-start
  0.6 0.0 copy-start.1
  0.7 14.7 %row_sums.1 = f32[4,64,256]{2,1,0:T(8,128)} custom-call(s32[16,128]{1,0:T(8,128)} %bitcast.9, s32[1,32]{1,0:T(1,128)} %bitcast.11, f32[1,1024]{1,0:T(1,128)} %bitcast.10, bf16[2048,1024]{1,0:T(8,128)(2,1)} %x_hbm.1, bf16[1024,256]{1,0:T(8,128)(2,1)} %wq_hbm.1, bf16[1024,256]{1,0:T(8,128)(2,1)} %wk_hbm.1, bf16[1024,256]{1,0:T(8,128)(2,1)} %wv_hbm.1, ...), custom_call_target="tpu_custom_call" | custom-call | tf_op jit(solution)/shard_map/row_sums/pallas_call | solution.py:363
  15.4 10.3 %all_to_all.21 = f32[4,64,256]{2,1,0:T(8,128)S(1)} all-to-all(f32[4,64,256]{2,1,0:T(8,128)} %row_sums.1), channel_id=1, replica_groups=mesh['dp'=8,'mp'=4] {'mp'}, dimensions={0} | all-to-all | bytes 524288 | tf_op jit(solution)/shard_map/all_to_all | solution.py:535
  25.6 15.6 %all_to_all.22 = f32[8,8,256]{2,1,0:T(8,128)S(1)} all-to-all(f32[8,8,256]{2,1,0:T(8,128)S(1)} %bitcast.6), channel_id=1, replica_groups=mesh['dp'=8,'mp'=4] {'dp'}, dimensions={0} | all-to-all | bytes 131072 | tf_op jit(solution)/shard_map/all_to_all | solution.py:537
  41.2 0.0 copy-done
  41.2 0.0 copy-done.1
  41.2 0.7 %products.1 = (f32[4,64,128]{2,1,0:T(8,128)S(1)}, f32[64,256]{1,0:T(8,128)S(1)}, f32[64,256]{1,0:T(8,128)S(1)}, f32[64,128]{1,0:T(8,128)S(1)}, f32[64,256]{1,0:T(8,128)S(1)}) custom-call(f32[64,256]{1,0:T(8,128)S(1)} %bitcast.7, f32[64,256]{1,0:T(8,128)S(1)} %reduce_sum.9.own_ref.meta_ref, f32[1024,256]{1,0:T(8,128)S(1)} %copy-done, f32[1,1024]{1,0:T(1,128)S(1)} %bitcast.8), custom_call_target="tpu_custom_call" | custom-call | tf_op jit(solution)/shard_map/products/pallas_call | solution.py:539
  42.0 7.0 %all_to_all.23.pay_ref = f32[4,64,128]{2,1,0:T(8,128)S(1)} all-to-all(f32[4,64,128]{2,1,0:T(8,128)S(1)} %get-tuple-element.7), channel_id=1, replica_groups=mesh['dp'=8,'mp'=4] {'mp'}, dimensions={0} | all-to-all | bytes 262144 | tf_op jit(solution)/shard_map/all_to_all | solution.py:551
  49.0 2.2 %update.1 = (f32[32,256]{1,0:T(8,128)}, f32[1024,256]{1,0:T(8,128)}) custom-call(f32[4,64,128]{2,1,0:T(8,128)S(1)} %all_to_all.23.pay_ref, f32[64,256]{1,0:T(8,128)S(1)} %get-tuple-element.8.docs_ref, f32[64,256]{1,0:T(8,128)S(1)} %get-tuple-element.9.near_ref, f32[64,128]{1,0:T(8,128)S(1)} %get-tuple-element.10.info_ref, ...), custom_call_target="tpu_custom_call" | custom-call | tf_op jit(solution)/shard_map/update/pallas_call | solution.py:552
  (1 shorter events, 0.0 us)
Async XLA Ops:
  0.6 40.6 %copy-start = (f32[1024,256]{1,0:T(8,128)S(1)}, f32[1024,256]{1,0:T(8,128)}, u32[]{:S(2)}) copy-start(f32[1024,256]{1,0:T(8,128)} %cent_ref.3) | copy-start | bytes 3145732
  0.6 40.6 %copy-start.1 = (f32[1024]{0:T(1024)S(1)}, f32[1024]{0:T(1024)}, u32[]{:S(2)}) copy-start(f32[1024]{0:T(1024)} %param.18) | copy-start | bytes 12292

commit v9 on v8

--- a/solution.py
+++ b/solution.py
@@ -461,25 +461,22 @@
     square = jnp.sum(near * near, axis=1, keepdims=True)
     own_square = jnp.sum(own * own, axis=1, keepdims=True)
     doc_square = jnp.sum(docs * docs, axis=1, keepdims=True)
-    pay_ref[0] = jnp.zeros(pay_ref.shape[1:], F32)
-    pay_ref[0, :, :rows] = gram
+    pay_ref[...] = jnp.zeros_like(pay_ref)
+    pay_ref[:, :rows] = gram
     for i, sums in enumerate((cross, square, own_square, doc_square)):
-        pay_ref[0, :, rows + i:rows + i + 1] = sums
-    for target in range(1, mp):
-        pay_ref[target] = pay_ref[0]
+        pay_ref[:, rows + i:rows + i + 1] = sums
     info_ref[...] = jnp.where(
         spot == 0, local, jnp.where(spot == 1, counts, jnp.where(spot == 2, valid, jnp.where(spot == 3, mass, own_counts)))
     )
 
 
-def update_kernel(
-    sizes, pay_ref, docs_ref, near_ref, info_ref, own_ref, meta_ref, cent_ref, vec_ref, new_ref
-):
+def update_kernel(sizes, *refs):
+    *pay_refs, docs_ref, near_ref, info_ref, own_ref, meta_ref, cent_ref, vec_ref, new_ref = refs
     length, tile, slots, capacity, block_rows, dp, mp, width, cents = sizes
     rows = dp * block_rows
     info = info_ref[...]
     local, counts, valid, mass, own_counts = (info[:, i:i + 1] for i in range(5))
-    pay = functools.reduce(jnp.add, [pay_ref[i] for i in range(mp)])
+    pay = functools.reduce(jnp.add, [pay_ref[...] for pay_ref in pay_refs])
     cross, square, own_square, doc_square = (pay[:, rows + i:rows + i + 1] for i in range(4))
 
     def scale(sums, count):
@@ -539,7 +536,7 @@
     pay, docs, near, info, own_sums = pl.pallas_call(
         functools.partial(products_kernel, sizes),
         out_shape=(
-            jax.ShapeDtypeStruct((mp, rows, round_up(rows + 4, LANES)), F32),
+            jax.ShapeDtypeStruct((rows, round_up(rows + 4, LANES)), F32),
             jax.ShapeDtypeStruct((rows, width), F32),
             jax.ShapeDtypeStruct((rows, width), F32),
             jax.ShapeDtypeStruct((rows, LANES), F32),
@@ -548,7 +545,9 @@
         compiler_params=limit,
         name="products",
     )(here, own, centroids, cluster_mass.reshape(1, cents))
-    pay = lax.all_to_all(pay, "mp", split_axis=0, concat_axis=0, tiled=True)
+    pays = [pay] + [
+        lax.ppermute(pay, "mp", [(i, (i + by) % mp) for i in range(mp)]) for by in range(1, mp)
+    ]
     return pl.pallas_call(
         functools.partial(update_kernel, sizes),
         out_shape=(
@@ -557,7 +556,7 @@
         ),
         compiler_params=limit,
         name="update",
-    )(pay, docs, near, info, own_sums, own, centroids)
+    )(*pays, docs, near, info, own_sums, own, centroids)
 
 
 def solution(mesh):

time: 50.6 us -> 47.9 us (0.947); the launches traced: 51.2 us -> 47.7 us
  blocking collectives: 32.9 us -> 25.1 us
  waiting for transfers between devices: 0 us -> 3.57 us
  starting transfers between devices: 0 us -> 0.65 us
    all_to_all x1 -> x0, blocking collectives: 7.02 us -> none  [shards(): pay = lax.all_to_all(pay, 'mp', split_axis=0, concat_axis=0, tiled=True)]
    ppermute x0 -> x3, waiting for transfers between devices: none -> 3.57 us  [shards(): lax.ppermute(pay, 'mp', [(i, (i + by) % mp) for i in range(mp)])]
    all_to_all x1, blocking collectives: 15.6 us -> 14.9 us  [shards(): here = lax.all_to_all(own, 'dp', split_axis=0, concat_axis=0, tiled=True)]
    ppermute x0 -> x3, starting transfers between devices: none -> 0.65 us  [shards(): lax.ppermute(pay, 'mp', [(i, (i + by) % mp) for i in range(mp)])]
  transfers between devices with their start and end apart: 0 -> 3, of which waited for: 0 -> 2; matrix products, arithmetic and copies ran while one was open for 0% -> 0% of each run, Pallas kernels for 0% -> 0%
where the time goes in v9:
time: 47.9 us; the launch traced here: 47.7 us
  blocking collectives  25.1 us (52%)
  Pallas kernels  17.6 us (37%)
  waiting for transfers between devices  3.57 us (7%)
  between operations  0.68 us (1%)
  starting transfers between devices  0.65 us (1%)
    all_to_all x1, blocking collectives, shards(): here = lax.all_to_all(own, 'dp', split_axis=0, concat_axis=0, tiled=True)  14.9 us
    pallas_call x1, Pallas kernels, row_sums(): pl.pallas_call(functools.partial(row_kernel, sizes), in_specs=[pl.BlockSp...  14.7 us
    all_to_all x1, blocking collectives, shards(): lax.all_to_all(partial, 'mp', split_axis=0, concat_axis=0, tiled=True)  10.3 us
    ppermute x3, waiting for transfers between devices, shards(): lax.ppermute(pay, 'mp', [(i, (i + by) % mp) for i in range(mp)])  3.57 us
    pallas_call x1, Pallas kernels, shards(): pl.pallas_call(functools.partial(update_kernel, sizes), out_shape=(jax.Sh...  2.22 us
  transfers between devices with their start and end apart: 3, of which 2 were waited for; matrix products, arithmetic and copies ran while one was open for 0% of the time, Pallas kernels for 0%

profile of v9, /device:TPU:0, one launch (start us, length us, event | category | flops | bytes accessed | tf_op | source)
XLA Modules:
  0.0 47.7 jit_solution(13352725672174712783)
XLA Ops:
  0.6 0.0 copy-start
  0.6 0.0 copy-start.1
  0.7 14.7 %row_sums.1 = f32[4,64,256]{2,1,0:T(8,128)} custom-call(s32[16,128]{1,0:T(8,128)} %bitcast.9, s32[1,32]{1,0:T(1,128)} %bitcast.11, f32[1,1024]{1,0:T(1,128)} %bitcast.10, bf16[2048,1024]{1,0:T(8,128)(2,1)} %x_hbm.1, bf16[1024,256]{1,0:T(8,128)(2,1)} %wq_hbm.1, bf16[1024,256]{1,0:T(8,128)(2,1)} %wk_hbm.1, bf16[1024,256]{1,0:T(8,128)(2,1)} %wv_hbm.1, ...), custom_call_target="tpu_custom_call" | custom-call | tf_op jit(solution)/shard_map/row_sums/pallas_call | solution.py:363
  15.4 10.3 %all_to_all.16 = f32[4,64,256]{2,1,0:T(8,128)S(1)} all-to-all(f32[4,64,256]{2,1,0:T(8,128)} %row_sums.1), channel_id=1, replica_groups=mesh['dp'=8,'mp'=4] {'mp'}, dimensions={0} | all-to-all | bytes 524288 | tf_op jit(solution)/shard_map/all_to_all | solution.py:532
  25.6 14.9 %all_to_all.17 = f32[8,8,256]{2,1,0:T(8,128)S(1)} all-to-all(f32[8,8,256]{2,1,0:T(8,128)S(1)} %bitcast.6), channel_id=1, replica_groups=mesh['dp'=8,'mp'=4] {'dp'}, dimensions={0} | all-to-all | bytes 131072 | tf_op jit(solution)/shard_map/all_to_all | solution.py:534
  40.5 0.0 copy-done
  40.5 0.0 copy-done.1
  40.5 0.7 %products.1 = (f32[64,128]{1,0:T(8,128)S(1)}, f32[64,256]{1,0:T(8,128)S(1)}, f32[64,256]{1,0:T(8,128)S(1)}, f32[64,128]{1,0:T(8,128)S(1)}, f32[64,256]{1,0:T(8,128)S(1)}) custom-call(f32[64,256]{1,0:T(8,128)S(1)} %bitcast.7, f32[64,256]{1,0:T(8,128)S(1)} %reduce_sum.9.own_ref.refs_8_, f32[1024,256]{1,0:T(8,128)S(1)} %copy-done, f32[1,1024]{1,0:T(1,128)S(1)} %bitcast.8), custom_call_target="tpu_custom_call" | custom-call | tf_op jit(solution)/shard_map/products/pallas_call | solution.py:536
  41.3 0.1 collective-permute-start.2
  41.3 0.4 collective-permute-start.1
  41.7 0.2 collective-permute-start
  41.9 1.1 %collective-permute-done.2.refs_3_ = f32[64,128]{1,0:T(8,128)S(1)} collective-permute-done((f32[64,128]{1,0:T(8,128)S(1)}, f32[64,128]{1,0:T(8,128)S(1)}, u32[]{:S(2)}, u32[]{:S(2)}) %collective-permute-start.2) | collective-permute-done | bytes 32800 | tf_op jit(solution)/shard_map/ppermute | solution.py:549
  43.0 2.5 %collective-permute-done.1.refs_2_ = f32[64,128]{1,0:T(8,128)S(1)} collective-permute-done((f32[64,128]{1,0:T(8,128)S(1)}, f32[64,128]{1,0:T(8,128)S(1)}, u32[]{:S(2)}, u32[]{:S(2)}) %collective-permute-start.1) | collective-permute-done | bytes 32800 | tf_op jit(solution)/shard_map/ppermute | solution.py:549
  45.5 0.0 collective-permute-done.refs_1_
  45.5 2.2 %update.1 = (f32[32,256]{1,0:T(8,128)}, f32[1024,256]{1,0:T(8,128)}) custom-call(f32[64,128]{1,0:T(8,128)S(1)} %get-tuple-element.7.refs_0_, f32[64,128]{1,0:T(8,128)S(1)} %collective-permute-done.refs_1_, f32[64,128]{1,0:T(8,128)S(1)} %collective-permute-done.1.refs_2_, f32[64,128]{1,0:T(8,128)S(1)} %collective-permute-done.2.refs_3_, ...), custom_call_target="tpu_custom_call" | custom-call | tf_op jit(solution)/shard_map/update/pallas_call | solution.py:551
  (1 shorter events, 0.0 us)
Async XLA Ops:
  0.6 39.9 %copy-start = (f32[1024,256]{1,0:T(8,128)S(1)}, f32[1024,256]{1,0:T(8,128)}, u32[]{:S(2)}) copy-start(f32[1024,256]{1,0:T(8,128)} %refs_9_.1) | copy-start | bytes 3145732
  0.6 39.9 %copy-start.1 = (f32[1024]{0:T(1024)S(1)}, f32[1024]{0:T(1024)}, u32[]{:S(2)}) copy-start(f32[1024]{0:T(1024)} %param.18) | copy-start | bytes 12292
  41.3 1.8 %collective-permute-start.2 = (f32[64,128]{1,0:T(8,128)S(1)}, f32[64,128]{1,0:T(8,128)S(1)}, u32[]{:S(2)}, u32[]{:S(2)}) collective-permute-start(f32[64,128]{1,0:T(8,128)S(1)} %get-tuple-element.7.refs_0_), channel_id=1, source_target_pairs={{0,3},{1,0},{2,1},{3,2},{4,7},{5,4},{6,5},{7,6},{8,11},{9,8},{10,9... | collective-permute-start | bytes 98312 | tf_op jit(solution)/shard_map/ppermute | solution.py:549
  41.3 4.2 %collective-permute-start.1 = (f32[64,128]{1,0:T(8,128)S(1)}, f32[64,128]{1,0:T(8,128)S(1)}, u32[]{:S(2)}, u32[]{:S(2)}) collective-permute-start(f32[64,128]{1,0:T(8,128)S(1)} %get-tuple-element.7.refs_0_), channel_id=1, source_target_pairs={{0,2},{1,3},{2,0},{3,1},{4,6},{5,7},{6,4},{7,5},{8,10},{9,11},{10,... | collective-permute-start | bytes 98312 | tf_op jit(solution)/shard_map/ppermute | solution.py:549
  41.7 3.7 %collective-permute-start = (f32[64,128]{1,0:T(8,128)S(1)}, f32[64,128]{1,0:T(8,128)S(1)}, u32[]{:S(2)}, u32[]{:S(2)}) collective-permute-start(f32[64,128]{1,0:T(8,128)S(1)} %get-tuple-element.7.refs_0_), channel_id=1, source_target_pairs={{0,1},{1,2},{2,3},{3,0},{4,5},{5,6},{6,7},{7,4},{8,9},{9,10},{10,1... | collective-permute-start | bytes 98312 | tf_op jit(solution)/shard_map/ppermute | solution.py:549

commit v10 on v9

--- a/solution.py
+++ b/solution.py
@@ -48,10 +48,14 @@
 
 
 def row_kernel(
-    sizes, ids_hbm, assigned_hbm, gain_hbm, x_hbm, wq_hbm, wk_hbm, wv_hbm, wo_hbm, out_ref,
-    ids_ref, ids_sm, assigned_sm, gain_ref, x_ref, w_ref, wo_ref, normed_ref, q_ref, k_ref, v_ref,
-    slot_ref, query_slots_ref, windows_ref, windows_sm, pool_ref, meta_ref, share_ref, scores_ref, raised_ref, small_sems, x_sems, w_sems,
+    sizes, ids_hbm, assigned_hbm, gain_hbm, x_hbm, wq_hbm, wk_hbm, wv_hbm, wo_hbm, *refs
 ):
+    mp = sizes[6]
+    out_refs = refs[:mp]
+    (
+        ids_ref, ids_sm, assigned_sm, gain_ref, x_ref, w_ref, wo_ref, normed_ref, q_ref, k_ref, v_ref,
+        slot_ref, query_slots_ref, windows_ref, windows_sm, pool_ref, meta_ref, share_ref, scores_ref, raised_ref, small_sems, x_sems, w_sems, sent_ref,
+    ) = refs[mp:]
     length, tile, slots, capacity, block_rows, dp, mp, width, cents = sizes
     tiles = length // tile
     lane_blocks = length // LANES
@@ -349,12 +353,13 @@
     sent = dot(jnp.concatenate([upper, lower], axis=0), wo_ref[...])
     sent = sent[:rows] + sent[rows:]
     for target in range(mp):
-        out_ref[target] = sent[:, target * width:(target + 1) * width]
-    out_ref[column] += tokens_sum
-    for target in range(mp):
+        sent_ref[(target - column + mp) % mp] = sent[:, target * width:(target + 1) * width]
+    sent_ref[0] += tokens_sum
+    for by, out_ref in enumerate(out_refs):
+        out_ref[...] = sent_ref[by]
         for block in range(dp):
             at = block * block_rows + capacity + 1
-            out_ref[target, at:at + 2, :] = meta_ref[:2, :]
+            out_ref[at:at + 2, :] = meta_ref[:2, :]
 
 
 def row_sums(doc_ids, assigned, tokens, ln_gain, w_query, w_key, w_value, w_out, sizes):
@@ -363,7 +368,7 @@
     return pl.pallas_call(
         functools.partial(row_kernel, sizes),
         in_specs=[pl.BlockSpec(memory_space=pltpu.HBM)] * 8,
-        out_shape=jax.ShapeDtypeStruct((mp, rows, width), F32),
+        out_shape=[jax.ShapeDtypeStruct((rows, width), F32)] * mp,
         scratch_shapes=[
             pltpu.VMEM((length // LANES, LANES), jnp.int32),
             pltpu.SMEM((length // LANES, LANES), jnp.int32),
@@ -388,6 +393,7 @@
             pltpu.SemaphoreType.DMA((5,)),
             pltpu.SemaphoreType.DMA((4 * length // tile,)),
             pltpu.SemaphoreType.DMA((4,)),
+            pltpu.VMEM((mp, rows, width), F32),
         ],
         compiler_params=pltpu.CompilerParams(vmem_limit_bytes=62 * 1024 * 1024),
         name="row_sums",
@@ -529,8 +535,9 @@
     limit = pltpu.CompilerParams(vmem_limit_bytes=48 * 1024 * 1024)
 
     partial = row_sums(doc_ids, assigned, tokens, ln_gain, w_query, w_key, w_value, w_out, sizes)
-    shared = lax.all_to_all(partial, "mp", split_axis=0, concat_axis=0, tiled=True)
-    own = jnp.sum(shared, axis=0)
+    own = partial[0]
+    for by in range(1, mp):
+        own = own + lax.ppermute(partial[by], "mp", [(i, (i + by) % mp) for i in range(mp)])
     here = lax.all_to_all(own, "dp", split_axis=0, concat_axis=0, tiled=True)
 
     pay, docs, near, info, own_sums = pl.pallas_call(

time: 47.9 us -> 44.7 us (0.933)
  blocking collectives: 25.1 us -> 13.3 us
  starting transfers between devices: 0.65 us -> 6.26 us
  waiting for transfers between devices: 3.57 us -> 5.39 us
  other arithmetic: 0.02 us -> 0.86 us
    all_to_all x1 -> x0, blocking collectives: 10.3 us -> none  [shards(): lax.all_to_all(partial, 'mp', split_axis=0, concat_axis=0, tiled=True)]
    ppermute x0 -> x3, starting transfers between devices: none -> 4.46 us  [shards(): lax.ppermute(partial[by], 'mp', [(i, (i + by) % mp) for i in range(mp)])]
    ppermute x0 -> x3, waiting for transfers between devices: none -> 2.22 us  [shards(): lax.ppermute(partial[by], 'mp', [(i, (i + by) % mp) for i in range(mp)])]
    all_to_all x1, blocking collectives: 14.9 us -> 13.3 us  [shards(): here = lax.all_to_all(own, 'dp', split_axis=0, concat_axis=0, tiled=True)]
    ppermute x3, starting transfers between devices: 0.65 us -> 1.81 us  [shards(): lax.ppermute(pay, 'mp', [(i, (i + by) % mp) for i in range(mp)])]
    add x0 -> x1, other arithmetic: none -> 0.86 us  [shards(): own + lax.ppermute(partial[by], 'mp', [(i, (i + by) % mp) for i in range(...]
  transfers between devices with their start and end apart: 3 -> 6, of which waited for: 2 -> 6; matrix products, arithmetic and copies ran while one was open for 0% -> 0% of each run, Pallas kernels for 0% -> 0%
where the time goes in v10:
time: 44.7 us; the launch traced here: 44.2 us
  Pallas kernels  17.6 us (39%)
  blocking collectives  13.3 us (30%)
  starting transfers between devices  6.26 us (14%)
  waiting for transfers between devices  5.39 us (12%)
  other arithmetic  0.86 us (2%)
  between operations  0.68 us (2%)
    pallas_call x1, Pallas kernels, row_sums(): pl.pallas_call(functools.partial(row_kernel, sizes), in_specs=[pl.BlockSp...  14.7 us
    all_to_all x1, blocking collectives, shards(): here = lax.all_to_all(own, 'dp', split_axis=0, concat_axis=0, tiled=True)  13.3 us
    ppermute x3, starting transfers between devices, shards(): lax.ppermute(partial[by], 'mp', [(i, (i + by) % mp) for i in range(mp)])  4.46 us
    ppermute x3, waiting for transfers between devices, shards(): lax.ppermute(pay, 'mp', [(i, (i + by) % mp) for i in range(mp)])  3.17 us
    pallas_call x1, Pallas kernels, shards(): pl.pallas_call(functools.partial(update_kernel, sizes), out_shape=(jax.Sh...  2.23 us
    ppermute x3, waiting for transfers between devices, shards(): lax.ppermute(partial[by], 'mp', [(i, (i + by) % mp) for i in range(mp)])  2.22 us
    ppermute x3, starting transfers between devices, shards(): lax.ppermute(pay, 'mp', [(i, (i + by) % mp) for i in range(mp)])  1.81 us
  transfers between devices with their start and end apart: 6, of which 6 were waited for; matrix products, arithmetic and copies ran while one was open for 0% of the time, Pallas kernels for 0%

profile of v10, /device:TPU:0, one launch (start us, length us, event | category | flops | bytes accessed | tf_op | source)
XLA Modules:
  0.0 44.2 jit_solution(3479814492602502145)
XLA Ops:
  0.6 0.0 copy-start
  0.6 0.0 copy-start.1
  0.7 14.7 %row_sums.1 = (f32[64,256]{1,0:T(8,128)}, f32[64,256]{1,0:T(8,128)}, f32[64,256]{1,0:T(8,128)}, f32[64,256]{1,0:T(8,128)}) custom-call(s32[16,128]{1,0:T(8,128)} %bitcast.9, s32[1,32]{1,0:T(1,128)} %bitcast.11, f32[1,1024]{1,0:T(1,128)} %bitcast.10, bf16[2048,1024]{1,0:T(8,128)(2,1)} %x_hbm.1, bf16[1024,256]{1,0:T(8,128)(2,1)} %wq_hbm.1, ...), custom_call_target="tpu_custom_call" | custom-call | tf_op jit(solution)/shard_map/row_sums/pallas_call | solution.py:368
  15.3 0.5 %collective-permute-start = (f32[64,256]{1,0:T(8,128)}, f32[64,256]{1,0:T(8,128)S(1)}, u32[]{:S(2)}, u32[]{:S(2)}) collective-permute-start(f32[64,256]{1,0:T(8,128)} %get-tuple-element.12), channel_id=1, source_target_pairs={{0,1},{1,2},{2,3},{3,0},{4,5},{5,6},{6,7},{7,4},{8,9},{9,10},{10,1... | collective-permute-start | bytes 196616 | tf_op jit(solution)/shard_map/ppermute | solution.py:540
  15.8 2.6 %collective-permute-start.1 = (f32[64,256]{1,0:T(8,128)}, f32[64,256]{1,0:T(8,128)S(1)}, u32[]{:S(2)}, u32[]{:S(2)}) collective-permute-start(f32[64,256]{1,0:T(8,128)} %get-tuple-element.13), channel_id=1, source_target_pairs={{0,2},{1,3},{2,0},{3,1},{4,6},{5,7},{6,4},{7,5},{8,10},{9,11},{10,... | collective-permute-start | bytes 196616 | tf_op jit(solution)/shard_map/ppermute | solution.py:540
  18.4 1.4 %collective-permute-start.2 = (f32[64,256]{1,0:T(8,128)}, f32[64,256]{1,0:T(8,128)S(1)}, u32[]{:S(2)}, u32[]{:S(2)}) collective-permute-start(f32[64,256]{1,0:T(8,128)} %get-tuple-element.14), channel_id=1, source_target_pairs={{0,3},{1,0},{2,1},{3,2},{4,7},{5,4},{6,5},{7,6},{8,11},{9,8},{10,9... | collective-permute-start | bytes 196616 | tf_op jit(solution)/shard_map/ppermute | solution.py:540
  19.8 0.1 collective-permute-done
  19.9 1.2 %collective-permute-done.1 = f32[64,256]{1,0:T(8,128)S(1)} collective-permute-done((f32[64,256]{1,0:T(8,128)}, f32[64,256]{1,0:T(8,128)S(1)}, u32[]{:S(2)}, u32[]{:S(2)}) %collective-permute-start.1) | collective-permute-done | bytes 65568 | tf_op jit(solution)/shard_map/ppermute | solution.py:540
  21.1 0.9 %collective-permute-done.2 = f32[64,256]{1,0:T(8,128)S(1)} collective-permute-done((f32[64,256]{1,0:T(8,128)}, f32[64,256]{1,0:T(8,128)S(1)}, u32[]{:S(2)}, u32[]{:S(2)}) %collective-permute-start.2) | collective-permute-done | bytes 65568 | tf_op jit(solution)/shard_map/ppermute | solution.py:540
  22.0 0.9 %add_add_fusion.own_ref.refs_8_ = f32[64,256]{1,0:T(8,128)S(1)} fusion(f32[64,256]{1,0:T(8,128)S(1)} %collective-permute-done.2, f32[64,256]{1,0:T(8,128)S(1)} %collective-permute-done.1, f32[64,256]{1,0:T(8,128)} %get-tuple-element.11, f32[64,256]{1,0:T(8,128)S(1)} %collective-permute-done), kind=kLoop, calls=%fused_computation | loop fusion | flops 49152 | bytes 327680 | tf_op jit(solution)/shard_map/add | solution.py:540
  22.9 13.3 %all_to_all.11 = f32[8,8,256]{2,1,0:T(8,128)S(1)} all-to-all(f32[8,8,256]{2,1,0:T(8,128)S(1)} %bitcast.6), channel_id=1, replica_groups=mesh['dp'=8,'mp'=4] {'dp'}, dimensions={0} | all-to-all | bytes 131072 | tf_op jit(solution)/shard_map/all_to_all | solution.py:541
  36.2 0.0 copy-done
  36.2 0.0 copy-done.1
  36.2 0.7 %products.1 = (f32[64,128]{1,0:T(8,128)S(1)}, f32[64,256]{1,0:T(8,128)S(1)}, f32[64,256]{1,0:T(8,128)S(1)}, f32[64,128]{1,0:T(8,128)S(1)}, f32[64,256]{1,0:T(8,128)S(1)}) custom-call(f32[64,256]{1,0:T(8,128)S(1)} %bitcast.7, f32[64,256]{1,0:T(8,128)S(1)} %add_add_fusion.own_ref.refs_8_, f32[1024,256]{1,0:T(8,128)S(1)} %copy-done, f32[1,1024]{1,0:T(1,128)S(1)} %bitcast.8), custom_call_target="tpu_custom_call" | custom-call | tf_op jit(solution)/shard_map/products/pallas_call | solution.py:543
  36.9 0.4 collective-permute-start.5
  37.3 1.3 %collective-permute-start.4 = (f32[64,128]{1,0:T(8,128)S(1)}, f32[64,128]{1,0:T(8,128)S(1)}, u32[]{:S(2)}, u32[]{:S(2)}) collective-permute-start(f32[64,128]{1,0:T(8,128)S(1)} %get-tuple-element.15.refs_0_), channel_id=1, source_target_pairs={{0,2},{1,3},{2,0},{3,1},{4,6},{5,7},{6,4},{7,5},{8,10},{9,11},{10,... | collective-permute-start | bytes 98312 | tf_op jit(solution)/shard_map/ppermute | solution.py:556
  38.6 0.2 collective-permute-start.3
  38.8 0.1 collective-permute-done.5.refs_3_
  38.9 2.3 %collective-permute-done.4.refs_2_ = f32[64,128]{1,0:T(8,128)S(1)} collective-permute-done((f32[64,128]{1,0:T(8,128)S(1)}, f32[64,128]{1,0:T(8,128)S(1)}, u32[]{:S(2)}, u32[]{:S(2)}) %collective-permute-start.4) | collective-permute-done | bytes 32800 | tf_op jit(solution)/shard_map/ppermute | solution.py:556
  41.2 0.7 %collective-permute-done.3.refs_1_ = f32[64,128]{1,0:T(8,128)S(1)} collective-permute-done((f32[64,128]{1,0:T(8,128)S(1)}, f32[64,128]{1,0:T(8,128)S(1)}, u32[]{:S(2)}, u32[]{:S(2)}) %collective-permute-start.3) | collective-permute-done | bytes 32800 | tf_op jit(solution)/shard_map/ppermute | solution.py:556
  41.9 2.2 %update.1 = (f32[32,256]{1,0:T(8,128)}, f32[1024,256]{1,0:T(8,128)}) custom-call(f32[64,128]{1,0:T(8,128)S(1)} %get-tuple-element.15.refs_0_, f32[64,128]{1,0:T(8,128)S(1)} %collective-permute-done.3.refs_1_, f32[64,128]{1,0:T(8,128)S(1)} %collective-permute-done.4.refs_2_, f32[64,128]{1,0:T(8,128)S(1)} %collective-permute-done.5.refs_3_, ...), custom_call_target="tpu_custom_call" | custom-call | tf_op jit(solution)/shard_map/update/pallas_call | solution.py:558
Async XLA Ops:
  0.6 35.6 %copy-start = (f32[1024,256]{1,0:T(8,128)S(1)}, f32[1024,256]{1,0:T(8,128)}, u32[]{:S(2)}) copy-start(f32[1024,256]{1,0:T(8,128)} %refs_9_.1) | copy-start | bytes 3145732
  0.6 35.6 %copy-start.1 = (f32[1024]{0:T(1024)S(1)}, f32[1024]{0:T(1024)}, u32[]{:S(2)}) copy-start(f32[1024]{0:T(1024)} %param.18) | copy-start | bytes 12292
  15.3 4.6 %collective-permute-start = (f32[64,256]{1,0:T(8,128)}, f32[64,256]{1,0:T(8,128)S(1)}, u32[]{:S(2)}, u32[]{:S(2)}) collective-permute-start(f32[64,256]{1,0:T(8,128)} %get-tuple-element.12), channel_id=1, source_target_pairs={{0,1},{1,2},{2,3},{3,0},{4,5},{5,6},{6,7},{7,4},{8,9},{9,10},{10,1... | collective-permute-start | bytes 196616 | tf_op jit(solution)/shard_map/ppermute | solution.py:540
  15.8 5.3 %collective-permute-start.1 = (f32[64,256]{1,0:T(8,128)}, f32[64,256]{1,0:T(8,128)S(1)}, u32[]{:S(2)}, u32[]{:S(2)}) collective-permute-start(f32[64,256]{1,0:T(8,128)} %get-tuple-element.13), channel_id=1, source_target_pairs={{0,2},{1,3},{2,0},{3,1},{4,6},{5,7},{6,4},{7,5},{8,10},{9,11},{10,... | collective-permute-start | bytes 196616 | tf_op jit(solution)/shard_map/ppermute | solution.py:540
  18.4 3.6 %collective-permute-start.2 = (f32[64,256]{1,0:T(8,128)}, f32[64,256]{1,0:T(8,128)S(1)}, u32[]{:S(2)}, u32[]{:S(2)}) collective-permute-start(f32[64,256]{1,0:T(8,128)} %get-tuple-element.14), channel_id=1, source_target_pairs={{0,3},{1,0},{2,1},{3,2},{4,7},{5,4},{6,5},{7,6},{8,11},{9,8},{10,9... | collective-permute-start | bytes 196616 | tf_op jit(solution)/shard_map/ppermute | solution.py:540
  36.9 2.0 %collective-permute-start.5 = (f32[64,128]{1,0:T(8,128)S(1)}, f32[64,128]{1,0:T(8,128)S(1)}, u32[]{:S(2)}, u32[]{:S(2)}) collective-permute-start(f32[64,128]{1,0:T(8,128)S(1)} %get-tuple-element.15.refs_0_), channel_id=1, source_target_pairs={{0,3},{1,0},{2,1},{3,2},{4,7},{5,4},{6,5},{7,6},{8,11},{9,8},{10,9... | collective-permute-start | bytes 98312 | tf_op jit(solution)/shard_map/ppermute | solution.py:556
  37.3 3.9 %collective-permute-start.4 = (f32[64,128]{1,0:T(8,128)S(1)}, f32[64,128]{1,0:T(8,128)S(1)}, u32[]{:S(2)}, u32[]{:S(2)}) collective-permute-start(f32[64,128]{1,0:T(8,128)S(1)} %get-tuple-element.15.refs_0_), channel_id=1, source_target_pairs={{0,2},{1,3},{2,0},{3,1},{4,6},{5,7},{6,4},{7,5},{8,10},{9,11},{10,... | collective-permute-start | bytes 98312 | tf_op jit(solution)/shard_map/ppermute | solution.py:556
  38.6 3.3 %collective-permute-start.3 = (f32[64,128]{1,0:T(8,128)S(1)}, f32[64,128]{1,0:T(8,128)S(1)}, u32[]{:S(2)}, u32[]{:S(2)}) collective-permute-start(f32[64,128]{1,0:T(8,128)S(1)} %get-tuple-element.15.refs_0_), channel_id=1, source_target_pairs={{0,1},{1,2},{2,3},{3,0},{4,5},{5,6},{6,7},{7,4},{8,9},{9,10},{10,1... | collective-permute-start | bytes 98312 | tf_op jit(solution)/shard_map/ppermute | solution.py:556
